TPU v7x, 512 devices: a whole 4x4x16 slice. The times are simulated.
512 devices in a mesh: row: 16 (over z_lo, x), col: 32 (over y, z_hi, core).
Axes of the slice: x: 4, y: 4, z: 16 (z_hi: 4, z_lo: 4; z = z_hi * 4 + z_lo), core: 2. Of those that a mesh axis runs over, the one named last changes fastest.
Arguments:
- pair_rep: bfloat16 [256, 256, 128], P('row', 'col'), may hold values from -6 to 6
- cotangent: bfloat16 [256, 256, 128], P('row', 'col'), may hold values from -6 to 6
- contact: int32 [16, 16, 16], replicated, may hold values 0 or 1
- norm_gain: float32 [128], replicated, may hold values from 0.5 to 1.5
- w_out_proj: bfloat16 [128, 512], replicated, may hold values from -0.5 to 0.5
- w_in_proj: bfloat16 [128, 512], replicated, may hold values from -0.5 to 0.5
- update_gain: float32 [2, 128], replicated, may hold values from 0.5 to 1.5
- w_gate: bfloat16 [128, 256], replicated, may hold values from -0.5 to 0.5
- w_final: bfloat16 [2, 128, 128], replicated, may hold values from -0.5 to 0.5
Outputs:
- updated: bfloat16 [256, 256, 128], P('row', 'col')
- grad_pair: bfloat16 [256, 256, 128], P('row', 'col')
All inputs are finite; a program needn't handle non-finite values.
Results may differ from a plain program's by a relative error of at most 0.018.
Values may be sent and summed in bfloat16 or wider, within the bound.
No kernel may reach another device: no remote copies, remote signals or barrier semaphores. Data moves between devices by JAX's collectives and lax.ppermute only.
A program may use at most 128 MiB of HBM per device.

v0:
```python
import jax
import jax.numpy as jnp
from jax import lax
from jax.sharding import PartitionSpec as P

EPSILON = 1e-05


def normalize(values, gain):
    center = jnp.mean(values, axis=-1, keepdims=True)
    shifted = values - center
    inverse = lax.rsqrt(jnp.mean(shifted * shifted, axis=-1, keepdims=True) + EPSILON)
    scaled = shifted * inverse
    return (scaled * gain, scaled, inverse)


def normalize_back(upstream, gain, scaled, inverse):
    weighted = upstream * gain
    first_mean = jnp.mean(weighted, axis=-1, keepdims=True)
    second_mean = jnp.mean(weighted * scaled, axis=-1, keepdims=True)
    return inverse * (weighted - first_mean - scaled * second_mean)


def gated_pairs(projected, channels):
    first = jax.nn.sigmoid(projected[..., 0:channels]) * projected[..., channels : 2 * channels]
    second = (
        jax.nn.sigmoid(projected[..., 2 * channels : 3 * channels]) * projected[..., 3 * channels :]
    )
    return (first.astype(jnp.bfloat16), second.astype(jnp.bfloat16))


def gated_back(grad_first, grad_second, projected, channels):
    sig_first = jax.nn.sigmoid(projected[..., 0:channels])
    sig_second = jax.nn.sigmoid(projected[..., 2 * channels : 3 * channels])
    return jnp.concatenate(
        [
            grad_first * projected[..., channels : 2 * channels] * sig_first * (1.0 - sig_first),
            grad_first * sig_first,
            grad_second * projected[..., 3 * channels :] * sig_second * (1.0 - sig_second),
            grad_second * sig_second,
        ],
        axis=-1,
    )


def spread_mask(mask_layer, p_first, p_len, q_first, q_len, block_width):
    labels = jnp.arange(mask_layer.shape[0], dtype=jnp.int32)
    p_ids = (p_first + jnp.arange(p_len, dtype=jnp.int32)) // block_width
    q_ids = (q_first + jnp.arange(q_len, dtype=jnp.int32)) // block_width
    p_table = (p_ids[:, None] == labels[None, :]).astype(jnp.float32)
    q_table = (q_ids[:, None] == labels[None, :]).astype(jnp.float32)
    inner = jnp.dot(p_table, mask_layer, precision=lax.Precision.HIGHEST)
    return jnp.dot(inner, q_table.T, precision=lax.Precision.HIGHEST)


def pair_product(
    formula,
    left_side,
    right_side,
    left_axis,
    right_axis,
    mask_perm,
    p_first,
    q_first,
    r_first,
    r_len,
    block_width,
):
    piece_len = min(r_len, block_width)
    summed = None
    for piece_no in range(r_len // piece_len):
        left_piece = lax.slice_in_dim(
            left_side, piece_no * piece_len, (piece_no + 1) * piece_len, axis=left_axis
        )
        right_piece = lax.slice_in_dim(
            right_side, piece_no * piece_len, (piece_no + 1) * piece_len, axis=right_axis
        )
        product = jnp.einsum(formula, left_piece, right_piece, preferred_element_type=jnp.float32)
        block_id = (r_first + piece_no * piece_len) // block_width
        mask_layer = lax.dynamic_index_in_dim(mask_perm, block_id, 2, keepdims=False).astype(
            jnp.float32
        )
        weights = spread_mask(
            mask_layer, p_first, product.shape[0], q_first, product.shape[1], block_width
        )
        partial_value = weights[:, :, None] * product
        summed = partial_value if summed is None else summed + partial_value
    return summed


def gather_rows(values):
    return lax.all_gather(values, "row", axis=0, tiled=True)


def gather_cols(stacked):
    return lax.all_gather(stacked, "col", axis=2, tiled=True)


def sum_rows(maker, amount):
    return lax.psum_scatter(
        maker(jnp.int32(0), amount * lax.axis_size("row")).astype(jnp.bfloat16),
        "row",
        scatter_dimension=0,
        tiled=True,
    ).astype(jnp.float32)


def sum_cols(maker, amount):
    return lax.psum_scatter(
        maker(jnp.int32(0), amount * lax.axis_size("col")).astype(jnp.bfloat16),
        "col",
        scatter_dimension=0,
        tiled=True,
    ).astype(jnp.float32)


def on_device(
    pair_rep, cotangent, contact, norm_gain, w_out_proj, w_in_proj, update_gain, w_gate, w_final
):
    rows_here, cols_here, channels = pair_rep.shape
    residues = rows_here * lax.axis_size("row")
    block_width = residues // contact.shape[0]
    row_first = lax.axis_index("row") * rows_here
    col_first = lax.axis_index("col") * cols_here
    pair_f32 = pair_rep.astype(jnp.float32)
    normed, scaled_pair, inverse_pair = normalize(pair_f32, norm_gain)
    normed_half = normed.astype(jnp.bfloat16)
    out_proj = jnp.dot(normed_half, w_out_proj, preferred_element_type=jnp.float32)
    in_proj = jnp.dot(normed_half, w_in_proj, preferred_element_type=jnp.float32)
    left_out, right_out = gated_pairs(out_proj, channels)
    left_in, right_in = gated_pairs(in_proj, channels)
    right_all = gather_rows(right_out)
    left_all = gather_cols(left_in[None])[0]
    triangle_out = jnp.transpose(
        lax.psum_scatter(
            pair_product(
                "jkc,ikc->jic",
                right_all,
                left_out,
                1,
                1,
                jnp.transpose(contact, (1, 0, 2)),
                jnp.int32(0),
                row_first,
                col_first,
                cols_here,
                block_width,
            ).astype(jnp.bfloat16),
            "col",
            scatter_dimension=0,
            tiled=True,
        ).astype(jnp.float32),
        (1, 0, 2),
    )

    def in_terms(first, amount):
        return pair_product(
            "kic,kjc->ijc",
            left_all,
            right_in,
            0,
            0,
            contact,
            first,
            col_first,
            row_first,
            rows_here,
            block_width,
        )

    triangle_in = sum_rows(in_terms, rows_here)
    normed_out, scaled_out, inverse_out = normalize(triangle_out, update_gain[0])
    normed_in, scaled_in, inverse_in = normalize(triangle_in, update_gain[1])
    norm_out = normed_out.astype(jnp.bfloat16)
    norm_in = normed_in.astype(jnp.bfloat16)
    gate = jax.nn.sigmoid(jnp.dot(normed_half, w_gate, preferred_element_type=jnp.float32))
    final_out = jnp.dot(norm_out, w_final[0], preferred_element_type=jnp.float32)
    final_in = jnp.dot(norm_in, w_final[1], preferred_element_type=jnp.float32)
    updated = (
        pair_f32 + gate[..., :channels] * final_out + gate[..., channels:] * final_in
    ).astype(jnp.bfloat16)
    upstream = cotangent.astype(jnp.float32)
    grad_final_out = (upstream * gate[..., :channels]).astype(jnp.bfloat16)
    grad_final_in = (upstream * gate[..., channels:]).astype(jnp.bfloat16)
    grad_gate = (
        jnp.concatenate([upstream * final_out, upstream * final_in], axis=-1) * gate * (1.0 - gate)
    ).astype(jnp.bfloat16)
    grad_norm_out = jnp.dot(grad_final_out, w_final[0].T, preferred_element_type=jnp.float32)
    grad_norm_in = jnp.dot(grad_final_in, w_final[1].T, preferred_element_type=jnp.float32)
    grad_tri_out = normalize_back(grad_norm_out, update_gain[0], scaled_out, inverse_out).astype(
        jnp.bfloat16
    )
    grad_tri_in = normalize_back(grad_norm_in, update_gain[1], scaled_in, inverse_in).astype(
        jnp.bfloat16
    )
    grad_out_all = gather_cols(grad_tri_out[None])[0]
    grad_in_all = gather_rows(grad_tri_in)
    grad_left_out = pair_product(
        "ijc,jkc->ikc",
        grad_out_all,
        right_all,
        1,
        0,
        jnp.transpose(contact, (0, 2, 1)),
        row_first,
        col_first,
        0,
        residues,
        block_width,
    )

    def right_out_terms(first, amount):
        return pair_product(
            "ijc,ikc->jkc",
            grad_out_all,
            left_out,
            0,
            0,
            jnp.transpose(contact, (1, 2, 0)),
            first,
            col_first,
            row_first,
            rows_here,
            block_width,
        )

    grad_right_out = sum_rows(right_out_terms, rows_here)
    grad_right_in = pair_product(
        "kic,ijc->kjc",
        left_all,
        grad_in_all,
        1,
        0,
        jnp.transpose(contact, (2, 1, 0)),
        row_first,
        col_first,
        0,
        residues,
        block_width,
    )

    def left_in_terms(first, amount):
        return pair_product(
            "ijc,kjc->ikc",
            grad_in_all,
            right_in,
            1,
            1,
            jnp.transpose(contact, (0, 2, 1)),
            first,
            row_first,
            col_first,
            cols_here,
            block_width,
        )

    grad_left_in = jnp.transpose(sum_cols(left_in_terms, cols_here), (1, 0, 2))
    grad_proj_out = gated_back(grad_left_out, grad_right_out, out_proj, channels).astype(
        jnp.bfloat16
    )
    grad_proj_in = gated_back(grad_left_in, grad_right_in, in_proj, channels).astype(jnp.bfloat16)
    grad_normed = jnp.dot(grad_proj_out, w_out_proj.T, preferred_element_type=jnp.float32)
    grad_normed = grad_normed + jnp.dot(
        grad_proj_in, w_in_proj.T, preferred_element_type=jnp.float32
    )
    grad_normed = grad_normed + jnp.dot(grad_gate, w_gate.T, preferred_element_type=jnp.float32)
    grad_pair = (
        upstream + normalize_back(grad_normed, norm_gain, scaled_pair, inverse_pair)
    ).astype(jnp.bfloat16)
    return (updated, grad_pair)


def solution(mesh):
    in_specs = (P("row", "col", None), P("row", "col", None), P(), P(), P(), P(), P(), P(), P())
    out_specs = (P("row", "col", None), P("row", "col", None))
    return jax.shard_map(
        on_device, mesh=mesh, in_specs=in_specs, out_specs=out_specs, check_vma=False
    )
```

profile of v0, /device:TPU:1, one launch (start us, length us, event | category | flops | bytes accessed | tf_op | source)
XLA Modules:
  0.0 657.2 jit_solution(15644870184305476811)
XLA Ops:
  11.6 39.9 %all_gather.12 = bf16[256,8,128]{2,1,0:T(8,128)(2,1)S(1)} all-gather(bf16[16,8,128]{2,1,0:T(8,128)(2,1)S(1)} %get-tuple-element.82), channel_id=1, replica_groups=mesh['row'=16,'col'=32] {'row'}, dimensions={0}, use_global_device_ids=true | all-gather | bytes 557056 | tf_op jit(solution)/shard_map/all_gather | solution.py:92
  53.2 2.4 copy.405
  106.6 1.5 fusion.222
  109.3 65.1 %reduce-scatter.7.cloned.1.call-done = bf16[8,16,128]{2,1,0:T(8,128)(2,1)} async-done(((bf16[256,16,128]{2,1,0:T(8,128)(2,1)}), bf16[8,16,128]{2,1,0:T(8,128)(2,1)}) %reduce-scatter.7.cloned.1.call-update) | async-done | bytes 32784 | tf_op jit(solution)/shard_map/reduce_scatter | solution.py:135
  175.3 72.3 %all-gather.5.cloned.1.call-done = bf16[16,256,128]{2,1,0:T(8,128)(2,1)} async-done(((bf16[16,8,128]{2,1,0:T(8,128)(2,1)}), bf16[16,256,128]{2,1,0:T(8,128)(2,1)}) %all-gather.5.cloned.1.call-update) | async-done | bytes 1048592 | tf_op jit(solution)/shard_map/all_gather | solution.py:96
  247.6 8.8 %copy.409 = bf16[16,256,128]{0,1,2:T(8,128)(2,1)} copy(bf16[16,256,128]{2,1,0:T(8,128)(2,1)} %all-gather.5.cloned.1.call-done) | data formatting | bytes 2097152 | tf_op jit(solution)/shard_map/all_gather | solution.py:96
  256.4 5.6 fusion.3
  262.0 1.4 copy.410
  282.2 55.3 %reduce-scatter.9.cloned.1.call-done = bf16[16,8,128]{2,1,0:T(8,128)(2,1)} async-done(((bf16[256,8,128]{2,1,0:T(8,128)(2,1)}), bf16[16,8,128]{2,1,0:T(8,128)(2,1)}) %reduce-scatter.9.cloned.1.call-update) | async-done | bytes 32784 | tf_op jit(solution)/shard_map/reduce_scatter | solution.py:100
  341.3 34.1 %all_gather.15 = bf16[256,8,128]{2,1,0:T(8,128)(2,1)S(1)} all-gather(bf16[16,8,128]{2,1,0:T(8,128)(2,1)S(1)} %fusion.55), channel_id=1, replica_groups=mesh['row'=16,'col'=32] {'row'}, dimensions={0}, use_global_device_ids=true | all-gather | bytes 557056 | tf_op jit(solution)/shard_map/all_gather | solution.py:92
  387.1 2.4 fusion.377
  389.5 2.3 fusion.378
  391.8 2.4 fusion.379
  394.2 2.3 fusion.380
  396.5 2.3 fusion.381
  398.8 2.3 fusion.382
  401.2 2.3 fusion.383
  403.5 2.2 fusion.384
  405.7 2.2 fusion.385
  411.6 9.4 %all-gather.7.cloned.1.call-done = bf16[16,256,128]{2,0,1:T(8,128)(2,1)} async-done(((bf16[16,8,128]{2,0,1:T(8,128)(2,1)}), bf16[16,256,128]{2,0,1:T(8,128)(2,1)}) %all-gather.7.cloned.1.call-update) | async-done | bytes 1048592 | tf_op jit(solution)/shard_map/all_gather | solution.py:96
  421.0 7.6 %copy.482 = bf16[16,256,128]{0,1,2:T(8,128)(2,1)} copy(bf16[16,256,128]{2,0,1:T(8,128)(2,1)} %all-gather.7.cloned.1.call-done) | data formatting | bytes 2097152 | tf_op jit(solution)/shard_map/all_gather | solution.py:96
  428.5 5.6 fusion.376
  434.8 2.1 fusion.8
  437.4 2.2 fusion.389
  440.2 1.8 copy.494
  442.1 1.8 copy.498
  443.9 1.8 copy.502
  445.8 1.8 copy.506
  447.6 1.8 copy.510
  449.4 1.8 copy.514
  452.1 1.8 copy.522
  454.0 1.8 copy.526
  455.8 1.8 copy.530
  457.7 1.8 copy.534
  459.5 1.9 copy.538
  461.4 1.9 copy.542
  464.3 2.2 fusion.390
  466.5 1.8 copy.546
  470.6 1.8 copy.550
  475.9 1.8 copy.588
  479.0 2.5 multiply_convert_fusion.1
  482.5 1.9 convert_multiply_fusion.1
  496.4 1.3 copy.462
  497.7 1.3 copy.466
  499.1 1.4 fusion.360
  500.5 1.3 fusion.361
  501.8 1.5 fusion.362
  503.3 2.3 fusion.363
  505.7 2.3 fusion.364
  508.0 2.3 fusion.365
  510.3 2.3 fusion.366
  512.6 2.1 fusion.367
  514.8 2.1 fusion.368
  516.9 2.1 fusion.369
  519.1 2.2 fusion.370
  521.2 2.2 fusion.371
  523.4 1.3 fusion.372
  536.9 1.3 copy.470
  538.3 1.5 fusion.373
  540.0 1.3 copy.474
  541.3 1.3 fusion.374
  542.9 1.3 copy.478
  544.2 1.3 fusion.375
  548.1 98.0 %reduce-scatter.13.cloned.1.call-done = bf16[8,2048]{1,0:T(8,128)(2,1)} async-done(((bf16[256,2048]{1,0:T(8,128)(2,1)}), bf16[8,2048]{1,0:T(8,128)(2,1)}) %reduce-scatter.13.cloned.1.call-update) | async-done | bytes 32784
  (298 shorter events, 139.0 us)
Async XLA Ops:
  7.2 3.3 copy-start
  7.2 48.5 %copy-start.12 = (bf16[16,8,128]{2,1,0:T(8,128)(2,1)S(1)}, bf16[16,8,128]{2,1,0:T(8,128)(2,1)}, u32[]{:S(2)}) copy-start(bf16[16,8,128]{2,1,0:T(8,128)(2,1)} %param.9) | copy-start | bytes 98308
  7.2 49.5 %copy-start.14 = (s32[16,16,16]{2,1,0:T(8,128)S(1)}, s32[16,16,16]{2,1,0:T(8,128)}, u32[]{:S(2)}) copy-start(s32[16,16,16]{2,1,0:T(8,128)} %param.11) | copy-start | bytes 49156
  7.2 48.5 %copy-start.33 = (f32[128]{0:T(128)S(1)}, f32[128]{0:T(128)}, u32[]{:S(2)}) copy-start(f32[128]{0:T(128)} %param.12) | copy-start | bytes 1540
  7.2 48.5 %copy-start.28 = (bf16[128,512]{1,0:T(8,128)(2,1)S(1)}, bf16[128,512]{1,0:T(8,128)(2,1)}, u32[]{:S(2)}) copy-start(bf16[128,512]{1,0:T(8,128)(2,1)} %param.14) | copy-start | bytes 393220
  7.2 80.3 %copy-start.36 = (f32[2,128]{1,0:T(2,128)S(1)}, f32[2,128]{1,0:T(2,128)}, u32[]{:S(2)}) copy-start(f32[2,128]{1,0:T(2,128)} %param.15) | copy-start | bytes 3076
  7.2 167.2 %reduce-scatter.7.cloned.1.call-start = ((), (), s32[]{:S(2)}) async-start(), calls=%async_computation.4 | async-start | bytes 1081344 | tf_op jit(solution)/shard_map/reduce_scatter | solution.py:135
  7.3 80.9 %copy-start.37 = (s32[256]{0:T(256)}, s32[256]{0:T(256)S(1)}, u32[]{:S(2)}) copy-start(s32[256]{0:T(256)S(1)} %and_select_fusion.2) | copy-start | bytes 3076
  7.4 80.9 %copy-start.38 = (s32[16]{0:T(128)}, s32[16]{0:T(128)S(1)}, u32[]{:S(2)}) copy-start(s32[16]{0:T(128)S(1)} %and_select_fusion.1) | copy-start | bytes 196
  53.2 55.8 %copy-start.31 = (bf16[128,256]{1,0:T(8,128)(2,1)S(1)}, bf16[128,256]{1,0:T(8,128)(2,1)}, u32[]{:S(2)}) copy-start(bf16[128,256]{1,0:T(8,128)(2,1)} %param.16) | copy-start | bytes 196612
  53.2 55.8 %copy-start.34 = (f32[128]{0:T(128)S(1)}, f32[128]{0:T(128)}, u32[]{:S(2)}) copy-start(f32[128]{0:T(128)} %param.12) | copy-start | bytes 1540
  55.6 192.0 %all-gather.5.cloned.1.call-start = ((), (), s32[]{:S(2)}) async-start(), calls=%async_computation.7 | async-start | bytes 1081344 | tf_op jit(solution)/shard_map/all_gather | solution.py:96
  55.9 119.3 %copy-start.3 = (f32[16,8,512]{2,1,0:T(8,128)}, f32[16,8,512]{2,1,0:T(8,128)S(1)}, u32[]{:S(2)}) copy-start(f32[16,8,512]{2,1,0:T(8,128)S(1)} %fusion.27) | copy-start | bytes 786436
  56.7 280.8 %reduce-scatter.9.cloned.1.call-start = ((), (), s32[]{:S(2)}) async-start(), calls=%async_computation.5 | async-start | bytes 557056 | tf_op jit(solution)/shard_map/reduce_scatter | solution.py:100
  88.1 175.6 %copy-start.35 = (f32[128]{0:T(128)}, f32[128]{0:T(128)S(1)}, u32[]{:S(2)}) copy-start(f32[128]{0:T(128)S(1)} %get-tuple-element.108) | copy-start | bytes 1540
  109.3 230.1 %copy-start.19 = (f32[16,8,256]{2,1,0:T(8,128)}, f32[16,8,256]{2,1,0:T(8,128)S(1)}, u32[]{:S(2)}) copy-start(f32[16,8,256]{2,1,0:T(8,128)S(1)} %fusion.6) | copy-start | bytes 393220
  175.3 88.2 %copy-start.21 = (bf16[8,16,128]{2,1,0:T(8,128)(2,1)S(1)}, bf16[8,16,128]{2,1,0:T(8,128)(2,1)}, u32[]{:S(2)}) copy-start(bf16[8,16,128]{2,1,0:T(8,128)(2,1)} %reduce-scatter.7.cloned.1.call-done) | copy-start | bytes 98308
  175.3 88.4 %copy-start.22 = (bf16[16,8,128]{2,1,0:T(8,128)(2,1)S(1)}, bf16[16,8,128]{2,1,0:T(8,128)(2,1)}, u32[]{:S(2)}) copy-start(bf16[16,8,128]{2,1,0:T(8,128)(2,1)} %param.10) | copy-start | bytes 98308
  175.3 88.4 %copy-start.32 = (bf16[2,128,128]{2,1,0:T(8,128)(2,1)S(1)}, bf16[2,128,128]{2,1,0:T(8,128)(2,1)}, u32[]{:S(2)}) copy-start(bf16[2,128,128]{2,1,0:T(8,128)(2,1)} %param.17) | copy-start | bytes 196612
  247.6 17.4 %copy-start.2 = (bf16[16,256,128]{2,1,0:T(8,128)(2,1)S(1)}, bf16[16,256,128]{2,1,0:T(8,128)(2,1)}, u32[]{:S(2)}) copy-start(bf16[16,256,128]{2,1,0:T(8,128)(2,1)} %all-gather.5.cloned.1.call-done) | copy-start | bytes 3145732
  263.4 157.6 %all-gather.7.cloned.1.call-start = ((), (), s32[]{:S(2)}) async-start(), calls=%async_computation.8 | async-start | bytes 1081344 | tf_op jit(solution)/shard_map/all_gather | solution.py:96
  263.5 76.9 %copy-start.26 = (f32[16,8]{1,0:T(8,128)}, f32[16,8]{1,0:T(8,128)S(1)}, u32[]{:S(2)}) copy-start(f32[16,8]{1,0:T(8,128)S(1)} %broadcast_multiply_fusion.7) | copy-start | bytes 1540
  263.7 76.7 %copy-start.29 = (f32[16,8]{1,0:T(8,128)}, f32[16,8]{1,0:T(8,128)S(1)}, u32[]{:S(2)}) copy-start(f32[16,8]{1,0:T(8,128)S(1)} %add_rsqrt_fusion.1) | copy-start | bytes 1540
  264.8 282.3 %reduce-scatter.11.cloned.1.call-start = ((), (), s32[]{:S(2)}) async-start(), calls=%async_computation.6 | async-start | bytes 557056 | tf_op jit(solution)/shard_map/reduce_scatter | solution.py:100
  338.4 2.9 copy-start.27
  339.3 2.0 copy-start.30
  387.1 16.4 %copy-start.18 = (bf16[16,8,128]{0,1,2:T(8,128)(2,1)S(1)}, bf16[16,8,128]{0,1,2:T(8,128)(2,1)}, u32[]{:S(2)}) copy-start(bf16[16,8,128]{0,1,2:T(8,128)(2,1)} %copy.520) | copy-start | bytes 98308
  387.1 18.6 %copy-start.17 = (bf16[16,8,128]{0,1,2:T(8,128)(2,1)S(1)}, bf16[16,8,128]{0,1,2:T(8,128)(2,1)}, u32[]{:S(2)}) copy-start(bf16[16,8,128]{0,1,2:T(8,128)(2,1)} %copy.524) | copy-start | bytes 98308
  387.1 20.8 %copy-start.16 = (bf16[16,8,128]{0,1,2:T(8,128)(2,1)S(1)}, bf16[16,8,128]{0,1,2:T(8,128)(2,1)}, u32[]{:S(2)}) copy-start(bf16[16,8,128]{0,1,2:T(8,128)(2,1)} %copy.528) | copy-start | bytes 98308
  387.1 22.0 %copy-start.15 = (bf16[16,8,128]{0,1,2:T(8,128)(2,1)S(1)}, bf16[16,8,128]{0,1,2:T(8,128)(2,1)}, u32[]{:S(2)}) copy-start(bf16[16,8,128]{0,1,2:T(8,128)(2,1)} %copy.532) | copy-start | bytes 98308
  434.7 16.5 %copy-start.7 = (f32[128,8,16]{2,1,0:T(8,128)S(1)}, f32[128,8,16]{2,1,0:T(8,128)}, u32[]{:S(2)}) copy-start(f32[128,8,16]{2,1,0:T(8,128)} %fusion.383) | copy-start | bytes 196612
  434.8 38.7 %copy-start.5 = (bf16[16,16,128]{1,0,2:T(8,128)(2,1)S(1)}, bf16[16,16,128]{1,0,2:T(8,128)(2,1)}, u32[]{:S(2)}) copy-start(bf16[16,16,128]{1,0,2:T(8,128)(2,1)} %copy.553) | copy-start | bytes 196612
  436.9 32.5 %copy-start.6 = (bf16[16,16,128]{1,0,2:T(8,128)(2,1)S(1)}, bf16[16,16,128]{1,0,2:T(8,128)(2,1)}, u32[]{:S(2)}) copy-start(bf16[16,16,128]{1,0,2:T(8,128)(2,1)} %copy.549) | copy-start | bytes 196612
  436.9 209.2 %reduce-scatter.13.cloned.1.call-start = ((), (), s32[]{:S(2)}) async-start(), calls=%async_computation.9 | async-start | bytes 1081344
  459.5 24.9 %copy-start.1 = (bf16[16,256,128]{2,0,1:T(8,128)(2,1)S(1)}, bf16[16,256,128]{2,0,1:T(8,128)(2,1)}, u32[]{:S(2)}) copy-start(bf16[16,256,128]{2,0,1:T(8,128)(2,1)} %all-gather.7.cloned.1.call-done) | copy-start | bytes 3145732
  499.0 13.6 %copy-start.10 = (bf16[16,16,128]{1,0,2:T(8,128)(2,1)S(1)}, bf16[16,16,128]{1,0,2:T(8,128)(2,1)}, u32[]{:S(2)}) copy-start(bf16[16,16,128]{1,0,2:T(8,128)(2,1)} %copy.446) | copy-start | bytes 196612
  499.0 15.7 %copy-start.9 = (bf16[16,16,128]{1,0,2:T(8,128)(2,1)S(1)}, bf16[16,16,128]{1,0,2:T(8,128)(2,1)}, u32[]{:S(2)}) copy-start(bf16[16,16,128]{1,0,2:T(8,128)(2,1)} %copy.450) | copy-start | bytes 196612
  499.1 17.9 %copy-start.8 = (bf16[16,16,128]{1,0,2:T(8,128)(2,1)S(1)}, bf16[16,16,128]{1,0,2:T(8,128)(2,1)}, u32[]{:S(2)}) copy-start(bf16[16,16,128]{1,0,2:T(8,128)(2,1)} %copy.454) | copy-start | bytes 196612
  521.2 14.1 %copy-start.11 = (f32[128,8,16]{2,1,0:T(8,128)S(1)}, f32[128,8,16]{2,1,0:T(8,128)}, u32[]{:S(2)}) copy-start(f32[128,8,16]{2,1,0:T(8,128)} %fusion.370) | copy-start | bytes 196612
  525.6 120.5 %copy-start.4 = (f32[16,8,512]{2,1,0:T(8,128)S(1)}, f32[16,8,512]{2,1,0:T(8,128)}, u32[]{:S(2)}) copy-start(f32[16,8,512]{2,1,0:T(8,128)} %copy-done.3) | copy-start | bytes 786436
  526.4 19.3 %copy-start.24 = (f32[128,8,16]{0,1,2:T(8,128)S(1)}, f32[128,8,16]{0,1,2:T(8,128)}, u32[]{:S(2)}) copy-start(f32[128,8,16]{0,1,2:T(8,128)} %copy.419) | copy-start | bytes 196612
  526.4 19.4 %copy-start.25 = (f32[128,8,16]{0,1,2:T(8,128)S(1)}, f32[128,8,16]{0,1,2:T(8,128)}, u32[]{:S(2)}) copy-start(f32[128,8,16]{0,1,2:T(8,128)} %copy.423) | copy-start | bytes 196612
  526.6 121.5 %copy-start.13 = (bf16[16,8,128]{2,1,0:T(8,128)(2,1)S(1)}, bf16[16,8,128]{2,1,0:T(8,128)(2,1)}, u32[]{:S(2)}) copy-start(bf16[16,8,128]{2,1,0:T(8,128)(2,1)} %param.9) | copy-start | bytes 98308
  526.7 121.5 %copy-start.20 = (f32[16,8,256]{2,1,0:T(8,128)S(1)}, f32[16,8,256]{2,1,0:T(8,128)}, u32[]{:S(2)}) copy-start(f32[16,8,256]{2,1,0:T(8,128)} %copy-done.19) | copy-start | bytes 393220
  527.9 121.4 %copy-start.23 = (bf16[16,8,128]{2,1,0:T(8,128)(2,1)S(1)}, bf16[16,8,128]{2,1,0:T(8,128)(2,1)}, u32[]{:S(2)}) copy-start(bf16[16,8,128]{2,1,0:T(8,128)(2,1)} %param.10) | copy-start | bytes 98308
Sparse Core Ops, SparseCore 0:
  55.7 118.5 reduce-scatter.6
  178.5 69.0 all-gather.4
  263.5 73.9 reduce-scatter.8
  341.1 79.8 all-gather.6
  437.0 84.8 reduce-scatter.10
  526.8 119.2 reduce-scatter.12
where the time goes:
time: 670 us; the launch traced here: 657 us
  waiting for transfers between devices  300 us (45%)
  local copies, waits for them, and re-layouts  133 us (20%)
  matrix products  119 us (18%)
  blocking collectives  74 us (11%)
  between operations  15.4 us (2%)
  other arithmetic  14.8 us (2%)
    unnamed x7, waiting for transfers between devices  98.1 us
    all_gather x2, waiting for transfers between devices, gather_cols(): return lax.all_gather(stacked, 'col', axis=2, tiled=True)  81.7 us
    all_gather x2, blocking collectives, gather_rows(): return lax.all_gather(values, 'row', axis=0, tiled=True)  74 us
    dot_general x36, matrix products, pair_product(): jnp.einsum(formula, left_piece, right_piece, preferred_element_type=jnp.f...  73.2 us
    reduce_scatter x1, waiting for transfers between devices, on_device(): lax.psum_scatter(pair_product('jkc,ikc->jic', right_all, left_out, 1, 1,...  65.1 us
    reduce_scatter x2, waiting for transfers between devices, sum_rows(): lax.psum_scatter(maker(jnp.int32(0), amount * lax.axis_size('row')).astyp...  55.3 us
    dot_general x33, local copies, waits for them, and re-layouts, pair_product(): jnp.einsum(formula, left_piece, right_piece, preferred_element_type=jnp.f...  40.9 us
    slice x34, local copies, waits for them, and re-layouts, pair_product(): lax.slice_in_dim(left_side, piece_no * piece_len, (piece_no + 1) * piece_...  35.8 us
  transfers between devices with their start and end apart: 6, of which 5 were waited for; matrix products, arithmetic and copies ran while one was open for 34% of the time, Pallas kernels for 0%

commit v1 on v0

v1 whole, which is shorter than its diff:
```python
import jax
import jax.numpy as jnp
from jax import lax
from jax.experimental import pallas as pl
from jax.experimental.pallas import tpu as pltpu
from jax.sharding import PartitionSpec as P


EPSILON = 1e-05
BF = jnp.bfloat16
F32 = jnp.float32


def dot(a, b, dims=((1,), (0,))):
    return lax.dot_general(a, b, (dims, ((), ())), preferred_element_type=F32)


def norm(values):
    center = jnp.mean(values, axis=0, keepdims=True)
    shifted = values - center
    inverse = lax.rsqrt(jnp.mean(shifted * shifted, axis=0, keepdims=True) + EPSILON)
    return shifted * inverse, inverse


def norm_back(weighted, scaled, inverse):
    first = jnp.mean(weighted, axis=0, keepdims=True)
    second = jnp.mean(weighted * scaled, axis=0, keepdims=True)
    return inverse * (weighted - first - scaled * second)


def pair_order():
    here = lax.broadcasted_iota(jnp.int32, (128, 128), 0)
    there = lax.broadcasted_iota(jnp.int32, (128, 128), 1)
    same = (here >> 3 == (there & 15)) & ((here & 7) == there >> 4)
    return same.astype(F32).astype(BF)


def groups(values):
    return values.reshape(16, 8, 128)


def first_kernel(pair, gain, w_out, w_in, w_gate, send, proj, gates, scaled_t, inv):
    pair_t = dot(pair[...], pair_order(), ((0,), (0,)))
    scaled, inverse = norm(pair_t)
    normed = (scaled * gain[...]).astype(BF)
    scaled_t[...] = scaled
    inv[...] = inverse
    for half, weights in enumerate((w_out, w_in)):
        p = dot(weights[...], normed, ((0,), (0,)))
        proj[half] = p
        send[:, 2 * half] = groups(jax.nn.sigmoid(p[0:128]) * p[128:256]).astype(BF)
        send[:, 2 * half + 1] = groups(jax.nn.sigmoid(p[256:384]) * p[384:512]).astype(BF)
    gates[...] = jax.nn.sigmoid(dot(w_gate[...], normed, ((0,), (0,))))


def swap_groups(rows):
    rows = list(rows)
    group = lax.broadcasted_iota(jnp.int32, rows[0].shape, rows[0].ndim - 1) >> 4
    last = rows[0].ndim - 1
    for step in (4, 2, 1):
        low = (group & step) == 0
        for a in range(8):
            if a & step:
                continue
            x, y = rows[a], rows[a + step]
            rows[a] = jnp.where(low, x, pltpu.roll(y, 16 * step, last))
            rows[a + step] = jnp.where(low, pltpu.roll(x, 128 - 16 * step, last), y)
    return rows


def spread_kernel(got, send, held):
    amount = got.shape[1]
    for half in range(2):
        rows = swap_groups(
            [got[8 * half + r].astype(F32).reshape(amount * 8, 128) for r in range(8)]
        )
        for q in range(8):
            for a in range(amount):
                held[:, a, q, 128 * half : 128 * half + 128] = rows[q][8 * a : 8 * a + 8]
    values = held[...].astype(BF)
    for mate in range(4):
        send[:, mate] = values


def collect_kernel(got, send, held, out):
    held[...] = got[...].astype(F32)
    for mate in range(4):
        for tile in range(got.shape[3] // 128):
            rows = swap_groups(
                [held[:, mate, q, 128 * tile : 128 * tile + 128] for q in range(8)]
            )
            for g in range(8):
                out[mate, g & 3, 2 * tile + (g >> 2)] = rows[g]
    send[...] = out[...].astype(BF)


def whole(got, a):
    return got[:, a].astype(F32).reshape(256, 256).astype(BF)


def block_table():
    place = lax.broadcasted_iota(jnp.int32, (256, 16), 0) >> 4
    label = lax.broadcasted_iota(jnp.int32, (256, 16), 1)
    return (place == label).astype(F32).astype(BF)


def masked(values, table, layer, flip):
    side = dot(table, layer, ((1,), (1 if flip else 0,))).astype(BF)
    return values * dot(side, table, ((1,), (1,))).astype(BF)


def quarter(values, mate):
    place = lax.broadcasted_iota(jnp.int32, (64, 256), 0) + 64 * mate
    label = lax.broadcasted_iota(jnp.int32, (64, 256), 1)
    return dot((place == label).astype(F32).astype(BF), values, ((1,), (1,))).astype(BF)


def own_rows(got, a, mate):
    return got[pl.ds(8 * mate, 8), a].astype(F32).reshape(64, 256).astype(BF)


NN = ((1,), (0,))
NT = ((1,), (1,))


def forward_kernel(spot, got, by_i, send):
    mate = spot[0]
    table = block_table()
    right_out, right_in = whole(got, 1), whole(got, 3)
    left_out = quarter(whole(got, 0), mate)
    left_in = own_rows(got, 2, mate)
    outs, ins = [], []
    for t in range(4):
        layer = by_i[4 * mate + t]
        part = slice(16 * t, 16 * t + 16)
        outs.append(dot(left_out[part], masked(right_out, table, layer, True), NN))
        ins.append(dot(left_in[part], masked(right_in, table, layer, False), NT))
    send[...] = jnp.concatenate(outs + ins, axis=0).T.reshape(32, 8, 128).astype(BF)


def backward_kernel(spot, got, grads, by_i, by_j, by_k, send):
    mate = spot[0]
    table = block_table()
    left_out, right_out = whole(got, 0), whole(got, 1)
    left_in = quarter(whole(got, 2), mate)
    right_in = quarter(whole(got, 3), mate)
    grad_out_i = quarter(whole(grads, 0), mate)
    grad_out_j = own_rows(grads, 0, mate)
    grad_in = whole(grads, 1)
    results = [[], [], [], []]
    for t in range(4):
        part = slice(16 * t, 16 * t + 16)
        over_j = masked(right_out, table, by_i[4 * mate + t], True)
        results[0].append(dot(grad_out_i[part], over_j, NT))
        over_i = masked(left_out, table, by_j[4 * mate + t], True)
        results[1].append(dot(grad_out_j[part], over_i, NT))
        both = masked(grad_in, table, by_k[4 * mate + t], True)
        results[2].append(dot(right_in[part], both, NN))
        results[3].append(dot(left_in[part], both, NT))
    stacked = jnp.concatenate(results[0] + results[1] + results[2] + results[3], axis=0)
    send[...] = stacked.T.reshape(32, 8, 256).astype(BF)


def middle_kernel(pair, cotangent, got, gates, gain, w_final, updated, send, grad_gate):
    order = pair_order()
    upstream = dot(cotangent[...], order, ((0,), (0,)))
    total = dot(pair[...], order, ((0,), (0,)))
    for t in range(2):
        triangle = got[:, t].astype(F32).reshape(128, 128)
        scaled, inverse = norm(triangle)
        normed = (scaled * gain[t]).astype(BF)
        gate = gates[128 * t : 128 * t + 128]
        final = dot(w_final[t], normed, ((0,), (0,)))
        total = total + gate * final
        grad_final = (upstream * gate).astype(BF)
        grad_gate[128 * t : 128 * t + 128] = (upstream * final * gate * (1.0 - gate)).astype(BF)
        weighted = dot(w_final[t], grad_final) * gain[t]
        send[:, t] = groups(norm_back(weighted, scaled, inverse)).astype(BF)
    updated[...] = dot(order, total.astype(BF), NT).astype(BF)


def last_kernel(
    cotangent, got, proj, grad_gate, scaled_t, inv, gain, w_out, w_in, w_gate, grad_pair
):
    order = pair_order()
    upstream = dot(cotangent[...], order, ((0,), (0,)))
    grad_normed = dot(w_gate[...], grad_gate[...])
    for half, weights in enumerate((w_out, w_in)):
        p = proj[half]
        parts = []
        for side in range(2):
            grad = got[:, 2 * half + side].astype(F32).reshape(128, 128)
            sig = jax.nn.sigmoid(p[256 * side : 256 * side + 128])
            parts.append(grad * p[256 * side + 128 : 256 * side + 256] * sig * (1.0 - sig))
            parts.append(grad * sig)
        grad_normed = grad_normed + dot(
            weights[...], jnp.concatenate(parts, axis=0).astype(BF)
        )
    back = norm_back(grad_normed * gain[...], scaled_t[...], inv[...])
    grad_pair[...] = dot(order, (upstream + back).astype(BF), NT).astype(BF)


def call(kernel, out, *args, scratch=(), spot=False):
    specs = [pl.BlockSpec(memory_space=pltpu.VMEM)] * len(args)
    if spot:
        specs[0] = pl.BlockSpec(memory_space=pltpu.SMEM)
    multi = isinstance(out, list)
    shapes = [jax.ShapeDtypeStruct(s, d) for s, d in (out if multi else [out])]
    outs = [pl.BlockSpec(memory_space=pltpu.VMEM)] * len(shapes)
    result = pl.pallas_call(
        kernel,
        out_shape=shapes,
        in_specs=specs,
        out_specs=outs,
        scratch_shapes=[pltpu.VMEM(s, F32) for s in scratch],
        compiler_params=pltpu.CompilerParams(vmem_limit_bytes=32 * 1024 * 1024),
    )(*args)
    return result if multi else result[0]


def exchange(values, axis):
    return lax.all_to_all(values, axis, 0, 0, tiled=True)


def to_channels(send):
    amount = send.shape[1]
    got = exchange(send, "row")
    spread = call(
        spread_kernel,
        ((8, 4, amount, 8, 256), BF),
        got,
        scratch=[(8, amount, 8, 256)],
    )
    return exchange(spread.reshape(32, amount, 8, 256), "col")


def to_pairs(send):
    width = send.shape[2]
    amount = width // 64
    got = exchange(send, "col").reshape(8, 4, 8, width)
    back = call(
        collect_kernel,
        ((4, 4, amount, 8, 128), BF),
        got,
        scratch=[(8, 4, 8, width), (4, 4, amount, 8, 128)],
    )
    return exchange(back.reshape(16, amount, 8, 128), "row")


def on_device(
    pair_rep, cotangent, contact, norm_gain, w_out_proj, w_in_proj, update_gain, w_gate, w_final
):
    pair = pair_rep.reshape(128, 128)
    upstream = cotangent.reshape(128, 128)
    gain = norm_gain.reshape(128, 1)
    update = update_gain.reshape(2, 128, 1)
    mate = (lax.axis_index("col") & 3).reshape(1)
    by_i = contact.astype(BF)
    by_j = jnp.transpose(by_i, (1, 0, 2))
    by_k = jnp.transpose(by_i, (2, 0, 1))

    send, proj, gates, scaled_t, inv = call(
        first_kernel,
        [
            ((16, 4, 8, 128), BF),
            ((2, 512, 128), F32),
            ((256, 128), F32),
            ((128, 128), F32),
            ((1, 128), F32),
        ],
        pair,
        gain,
        w_out_proj,
        w_in_proj,
        w_gate,
    )
    sides = to_channels(send)
    triangles = call(forward_kernel, ((32, 8, 128), BF), mate, sides, by_i, spot=True)
    updated, send, grad_gate = call(
        middle_kernel,
        [((128, 128), BF), ((16, 2, 8, 128), BF), ((256, 128), BF)],
        pair,
        upstream,
        to_pairs(triangles),
        gates,
        update,
        w_final,
    )
    grads = call(
        backward_kernel,
        ((32, 8, 256), BF),
        mate,
        sides,
        to_channels(send),
        by_i,
        by_j,
        by_k,
        spot=True,
    )
    grad_pair = call(
        last_kernel,
        ((128, 128), BF),
        upstream,
        to_pairs(grads),
        proj,
        grad_gate,
        scaled_t,
        inv,
        gain,
        w_out_proj,
        w_in_proj,
        w_gate,
    )
    return (updated.reshape(pair_rep.shape), grad_pair.reshape(pair_rep.shape))


def solution(mesh):
    in_specs = (P("row", "col", None), P("row", "col", None), P(), P(), P(), P(), P(), P(), P())
    out_specs = (P("row", "col", None), P("row", "col", None))
    return jax.shard_map(
        on_device, mesh=mesh, in_specs=in_specs, out_specs=out_specs, check_vma=False
    )
```

time: 670 us -> 187 us (0.28); the launches traced: 657 us -> 186 us
  waiting for transfers between devices: 300 us -> 55.9 us
  local copies, waits for them, and re-layouts: 133 us -> 4.63 us
  matrix products: 119 us -> 0 us
  starting transfers between devices: 0.92 us -> 27.2 us
  other arithmetic: 14.8 us -> 0.04 us
  between operations: 15.4 us -> 0.78 us
  Pallas kernels: 0 us -> 12.2 us
  blocking collectives: 74 us -> 85.1 us
    reduce_scatter x3 -> x0, waiting for transfers between devices: 120 us -> none  [the longest x1 65.1 us: on_device(): lax.psum_scatter(pair_product('jkc,ikc->jic', right_all, left_out, 1, 1,...]
    dot_general x118 -> x0, matrix products: 119 us -> none  [the longest x36 73.2 us: pair_product(): jnp.einsum(formula, left_piece, right_piece, preferred_element_type=jnp.f...]
    unnamed x7 -> x0, waiting for transfers between devices: 98.1 us -> none
    all_to_all x0 -> x5, blocking collectives: none -> 85.1 us  [exchange(): return lax.all_to_all(values, axis, 0, 0, tiled=True)]
    all_gather x2 -> x0, waiting for transfers between devices: 81.7 us -> none  [gather_cols(): return lax.all_gather(stacked, 'col', axis=2, tiled=True)]
    all_gather x2 -> x0, blocking collectives: 74 us -> none  [gather_rows(): return lax.all_gather(values, 'row', axis=0, tiled=True)]
    slice x68 -> x0, local copies, waits for them, and re-layouts: 64.8 us -> none  [the longest x34 35.8 us: pair_product(): lax.slice_in_dim(left_side, piece_no * piece_len, (piece_no + 1) * piece_...]
    all_to_all x0 -> x3, waiting for transfers between devices: none -> 55.9 us  [exchange(): return lax.all_to_all(values, axis, 0, 0, tiled=True)]
  transfers between devices with their start and end apart: 6 -> 3, of which waited for: 5 -> 3; matrix products, arithmetic and copies ran while one was open for 34% -> 0% of each run, Pallas kernels for 0% -> 0%
where the time goes in v1:
time: 187 us; the launch traced here: 186 us
  blocking collectives  85.1 us (46%)
  waiting for transfers between devices  55.9 us (30%)
  starting transfers between devices  27.2 us (15%)
  Pallas kernels  12.2 us (7%)
  local copies, waits for them, and re-layouts  4.63 us (2%)
    all_to_all x5, blocking collectives, exchange(): return lax.all_to_all(values, axis, 0, 0, tiled=True)  85.1 us
    all_to_all x3, waiting for transfers between devices, exchange(): return lax.all_to_all(values, axis, 0, 0, tiled=True)  55.9 us
    all_to_all x3, starting transfers between devices, exchange(): return lax.all_to_all(values, axis, 0, 0, tiled=True)  27.2 us
    pallas_call x9, Pallas kernels, call(): pl.pallas_call(kernel, out_shape=shapes, in_specs=specs, out_specs=outs,...  12.2 us
    unnamed x25, local copies, waits for them, and re-layouts  4.11 us
  transfers between devices with their start and end apart: 3, of which 3 were waited for; matrix products, arithmetic and copies ran while one was open for 0% of the time, Pallas kernels for 0%

profile of v1, /device:TPU:1, one launch (start us, length us, event | category | flops | bytes accessed | tf_op | source)
XLA Modules:
  0.0 185.8 jit_solution(16577449330987928667)
XLA Ops:
  0.6 0.0 copy-start.11
  0.6 0.0 copy-start.4
  0.6 0.6 copy-done.11
  1.3 0.1 copy.17.gain
  1.4 0.1 copy-done.4
  1.5 0.0 copy-start
  1.5 0.9 copy-done
  2.4 0.0 copy-start.2
  2.4 0.9 copy-done.2
  3.3 0.0 copy-start.6
  3.3 0.8 copy-done.6
  4.1 0.5 shard_map.104
  4.5 16.7 %all_to_all.40.got = bf16[16,4,8,128]{3,2,1,0:T(8,128)(2,1)S(1)} all-to-all(bf16[16,4,8,128]{3,2,1,0:T(8,128)(2,1)S(1)} %get-tuple-element.10), channel_id=1, replica_groups=mesh['row'=16,'col'=32] {'row'}, dimensions={0} | all-to-all | bytes 262144 | tf_op jit(solution)/shard_map/all_to_all | solution.py:222
  21.2 1.3 shard_map.105
  22.4 0.0 copy-start.9
  22.4 17.4 %all-to-all-start.1 = ((bf16[32,4,8,256]{3,2,1,0:T(8,128)(2,1)}), bf16[32,4,8,256]{3,2,1,0:T(8,128)(2,1)S(1)}, u32[]{:S(2)}, u32[]{:S(2)}) async-start(bf16[32,4,8,256]{3,2,1,0:T(8,128)(2,1)} %bitcast.4), calls=%async_computation.1 | async-start | bytes 1048576 | tf_op jit(solution)/shard_map/all_to_all | solution.py:222
  39.8 0.0 copy-done.9
  39.8 0.1 copy.18
  40.0 0.1 copy.19.by_i
  40.1 29.4 %all-to-all-done.1.got = bf16[32,4,8,256]{3,2,1,0:T(8,128)(2,1)S(1)} async-done(((bf16[32,4,8,256]{3,2,1,0:T(8,128)(2,1)}), bf16[32,4,8,256]{3,2,1,0:T(8,128)(2,1)S(1)}, u32[]{:S(2)}, u32[]{:S(2)}) %all-to-all-start.1) | async-done | bytes 524320 | tf_op jit(solution)/shard_map/all_to_all | solution.py:222
  69.5 2.6 %shard_map.106 = bf16[32,8,128]{2,1,0:T(8,128)(2,1)S(1)} custom-call(s32[1]{0:T(128)} %bitcast.2.spot, bf16[32,4,8,256]{3,2,1,0:T(8,128)(2,1)S(1)} %all-to-all-done.1.got, bf16[16,16,16]{2,1,0:T(8,128)(2,1)S(1)} %copy.19.by_i), custom_call_target="tpu_custom_call" | custom-call | tf_op jit(solution)/shard_map/pallas_call | solution.py:210
  72.2 23.3 %all_to_all.41 = bf16[32,8,128]{2,1,0:T(8,128)(2,1)S(1)} all-to-all(bf16[32,8,128]{2,1,0:T(8,128)(2,1)S(1)} %shard_map.106), channel_id=1, replica_groups=mesh['row'=16,'col'=32] {'col'}, dimensions={0} | all-to-all | bytes 131072 | tf_op jit(solution)/shard_map/all_to_all | solution.py:222
  95.5 0.9 shard_map.107
  96.4 3.5 %all-to-all-start.3 = ((bf16[16,2,8,128]{3,2,1,0:T(8,128)(2,1)}), bf16[16,2,8,128]{3,2,1,0:T(8,128)(2,1)S(1)}, u32[]{:S(2)}, u32[]{:S(2)}) async-start(bf16[16,2,8,128]{3,2,1,0:T(8,128)(2,1)} %bitcast.6), calls=%async_computation.3 | async-start | bytes 131072 | tf_op jit(solution)/shard_map/all_to_all | solution.py:222
  99.9 0.0 copy-start.10
  99.9 0.7 copy-done.10
  100.6 0.0 copy-start.5
  100.6 0.0 copy-start.7
  100.6 0.0 copy-start.8
  100.6 0.1 copy.20.gain
  100.7 6.4 %all-to-all-done.3.got = bf16[16,2,8,128]{3,2,1,0:T(8,128)(2,1)S(1)} async-done(((bf16[16,2,8,128]{3,2,1,0:T(8,128)(2,1)}), bf16[16,2,8,128]{3,2,1,0:T(8,128)(2,1)S(1)}, u32[]{:S(2)}, u32[]{:S(2)}) %all-to-all-start.3) | async-done | bytes 65568 | tf_op jit(solution)/shard_map/all_to_all | solution.py:222
  107.1 0.0 copy-done.5
  107.1 0.0 copy-done.7
  107.1 0.0 copy-done.8
  107.1 1.1 shard_map.108
  108.2 9.8 %all_to_all.42.got = bf16[16,2,8,128]{3,2,1,0:T(8,128)(2,1)S(1)} all-to-all(bf16[16,2,8,128]{3,2,1,0:T(8,128)(2,1)S(1)} %get-tuple-element.13), channel_id=1, replica_groups=mesh['row'=16,'col'=32] {'row'}, dimensions={0} | all-to-all | bytes 131072 | tf_op jit(solution)/shard_map/all_to_all | solution.py:222
  118.0 1.0 shard_map.109
  119.0 6.4 %all-to-all-start.5 = ((bf16[32,2,8,256]{3,2,1,0:T(8,128)(2,1)}), bf16[32,2,8,256]{3,2,1,0:T(8,128)(2,1)S(1)}, u32[]{:S(2)}, u32[]{:S(2)}) async-start(bf16[32,2,8,256]{3,2,1,0:T(8,128)(2,1)} %bitcast.9), calls=%async_computation.5 | async-start | bytes 524288 | tf_op jit(solution)/shard_map/all_to_all | solution.py:222
  125.4 0.1 copy.22.by_j
  125.6 20.1 %all-to-all-done.5.grads = bf16[32,2,8,256]{3,2,1,0:T(8,128)(2,1)S(1)} async-done(((bf16[32,2,8,256]{3,2,1,0:T(8,128)(2,1)}), bf16[32,2,8,256]{3,2,1,0:T(8,128)(2,1)S(1)}, u32[]{:S(2)}, u32[]{:S(2)}) %all-to-all-start.5) | async-done | bytes 262176 | tf_op jit(solution)/shard_map/all_to_all | solution.py:222
  145.7 3.4 %shard_map.110 = bf16[32,8,256]{2,1,0:T(8,128)(2,1)S(1)} custom-call(s32[1]{0:T(128)} %bitcast.2.spot, bf16[32,4,8,256]{3,2,1,0:T(8,128)(2,1)S(1)} %all-to-all-done.1.got, bf16[32,2,8,256]{3,2,1,0:T(8,128)(2,1)S(1)} %all-to-all-done.5.grads, bf16[16,16,16]{2,1,0:T(8,128)(2,1)S(1)} %copy.19.by_i, bf16[16,16,16]{2,1,0:T(8,128)(2,1)S(1)} %copy.22.by_j, ...), custom_call_target="tpu_custom_call" | custom-call | tf_op jit(solution)/shard_map/pallas_call | solution.py:210
  149.1 22.3 %all_to_all.43 = bf16[32,8,256]{2,1,0:T(8,128)(2,1)S(1)} all-to-all(bf16[32,8,256]{2,1,0:T(8,128)(2,1)S(1)} %shard_map.110), channel_id=1, replica_groups=mesh['row'=16,'col'=32] {'col'}, dimensions={0} | all-to-all | bytes 262144 | tf_op jit(solution)/shard_map/all_to_all | solution.py:222
  171.4 0.3 shard_map.111
  171.8 0.0 copy-start.1
  171.8 0.0 copy-start.3
  171.8 13.0 %all_to_all.44.got = bf16[16,4,8,128]{3,2,1,0:T(8,128)(2,1)S(1)} all-to-all(bf16[16,4,8,128]{3,2,1,0:T(8,128)(2,1)S(1)} %bitcast.18), channel_id=1, replica_groups=mesh['row'=16,'col'=32] {'row'}, dimensions={0} | all-to-all | bytes 262144 | tf_op jit(solution)/shard_map/all_to_all | solution.py:222
  184.8 0.0 copy-done.1
  184.8 0.0 copy-done.3
  184.8 1.1 shard_map.112
  (3 shorter events, 0.0 us)
Async XLA Ops:
  0.6 0.7 copy-start.11
  0.6 0.8 copy-start.4
  1.5 0.9 copy-start
  2.4 0.9 copy-start.2
  3.3 0.8 copy-start.6
  22.4 17.4 %copy-start.9 = (s32[16,16,16]{2,1,0:T(8,128)S(1)}, s32[16,16,16]{2,1,0:T(8,128)}, u32[]{:S(2)}) copy-start(s32[16,16,16]{2,1,0:T(8,128)} %param.11) | copy-start | bytes 49156
  22.4 47.1 %all-to-all-start.1 = ((bf16[32,4,8,256]{3,2,1,0:T(8,128)(2,1)}), bf16[32,4,8,256]{3,2,1,0:T(8,128)(2,1)S(1)}, u32[]{:S(2)}, u32[]{:S(2)}) async-start(bf16[32,4,8,256]{3,2,1,0:T(8,128)(2,1)} %bitcast.4), calls=%async_computation.1 | async-start | bytes 1048576 | tf_op jit(solution)/shard_map/all_to_all | solution.py:222
  96.4 10.7 %all-to-all-start.3 = ((bf16[16,2,8,128]{3,2,1,0:T(8,128)(2,1)}), bf16[16,2,8,128]{3,2,1,0:T(8,128)(2,1)S(1)}, u32[]{:S(2)}, u32[]{:S(2)}) async-start(bf16[16,2,8,128]{3,2,1,0:T(8,128)(2,1)} %bitcast.6), calls=%async_computation.3 | async-start | bytes 131072 | tf_op jit(solution)/shard_map/all_to_all | solution.py:222
  99.9 0.7 copy-start.10
  100.6 6.5 %copy-start.5 = (bf16[16,8,128]{2,1,0:T(8,128)(2,1)S(1)}, bf16[16,8,128]{2,1,0:T(8,128)(2,1)}, u32[]{:S(2)}) copy-start(bf16[16,8,128]{2,1,0:T(8,128)(2,1)} %param.10) | copy-start | bytes 98308
  100.6 6.5 %copy-start.7 = (bf16[16,8,128]{2,1,0:T(8,128)(2,1)S(1)}, bf16[16,8,128]{2,1,0:T(8,128)(2,1)}, u32[]{:S(2)}) copy-start(bf16[16,8,128]{2,1,0:T(8,128)(2,1)} %param.9) | copy-start | bytes 98308
  100.6 6.5 %copy-start.8 = (bf16[2,128,128]{2,1,0:T(8,128)(2,1)S(1)}, bf16[2,128,128]{2,1,0:T(8,128)(2,1)}, u32[]{:S(2)}) copy-start(bf16[2,128,128]{2,1,0:T(8,128)(2,1)} %w_final.1) | copy-start | bytes 196612
  119.0 26.7 %all-to-all-start.5 = ((bf16[32,2,8,256]{3,2,1,0:T(8,128)(2,1)}), bf16[32,2,8,256]{3,2,1,0:T(8,128)(2,1)S(1)}, u32[]{:S(2)}, u32[]{:S(2)}) async-start(bf16[32,2,8,256]{3,2,1,0:T(8,128)(2,1)} %bitcast.9), calls=%async_computation.5 | async-start | bytes 524288 | tf_op jit(solution)/shard_map/all_to_all | solution.py:222
  171.8 13.0 %copy-start.1 = (bf16[128,512]{1,0:T(8,128)(2,1)S(1)}, bf16[128,512]{1,0:T(8,128)(2,1)}, u32[]{:S(2)}) copy-start(bf16[128,512]{1,0:T(8,128)(2,1)} %w_out.3) | copy-start | bytes 393220
  171.8 13.0 %copy-start.3 = (bf16[128,512]{1,0:T(8,128)(2,1)S(1)}, bf16[128,512]{1,0:T(8,128)(2,1)}, u32[]{:S(2)}) copy-start(bf16[128,512]{1,0:T(8,128)(2,1)} %w_in.3) | copy-start | bytes 393220

commit v2 on v1

--- a/solution.py
+++ b/solution.py
@@ -1,3 +1,5 @@
+import functools
+
 import jax
 import jax.numpy as jnp
 from jax import lax
@@ -68,34 +70,70 @@
     return rows
 
 
-def spread_kernel(got, send, held):
+def lower_lanes(shape):
+    return lax.broadcasted_iota(jnp.int32, shape, len(shape) - 1) < 64
+
+
+def spread_kernel(full, parts, got, send, held_full, held_parts):
     amount = got.shape[1]
+    low = lower_lanes((8, 128))
     for half in range(2):
         rows = swap_groups(
             [got[8 * half + r].astype(F32).reshape(amount * 8, 128) for r in range(8)]
         )
         for q in range(8):
-            for a in range(amount):
-                held[:, a, q, 128 * half : 128 * half + 128] = rows[q][8 * a : 8 * a + 8]
-    values = held[...].astype(BF)
+            pieces = [rows[q][8 * a : 8 * a + 8] for a in range(amount)]
+            held_full[:, q, 128 * half : 128 * half + 128] = pieces[full]
+            for n, pair in enumerate(parts):
+                first, second = pieces[pair[0]], pieces[pair[-1]]
+                lanes = slice(128 * n, 128 * n + 128)
+                held_parts[:, 2 * half, q, lanes] = jnp.where(
+                    low, first, pltpu.roll(second, 64, 1)
+                )
+                held_parts[:, 2 * half + 1, q, lanes] = jnp.where(
+                    low, pltpu.roll(first, 64, 1), second
+                )
+    values = held_full[...].astype(BF)
     for mate in range(4):
-        send[:, mate] = values
-
-
-def collect_kernel(got, send, held, out):
+        send[:, mate, :, 0:256] = values
+    send[:, :, :, 256:] = held_parts[...].astype(BF)
+
+
+def collect_kernel(full, parts, got, send, held, out):
     held[...] = got[...].astype(F32)
-    for mate in range(4):
-        for tile in range(got.shape[3] // 128):
-            rows = swap_groups(
-                [held[:, mate, q, 128 * tile : 128 * tile + 128] for q in range(8)]
-            )
-            for g in range(8):
-                out[mate, g & 3, 2 * tile + (g >> 2)] = rows[g]
+    low = lower_lanes((8, 128))
+    for half in range(2):
+        rows = []
+        for q in range(8):
+            lanes = slice(128 * half, 128 * half + 128)
+            total = held[:, 0, q, lanes]
+            for mate in range(1, 4):
+                total = total + held[:, mate, q, lanes]
+            rows.append(total)
+        for g, values in enumerate(swap_groups(rows)):
+            out[8 * half + g, full] = values
+        for n, pair in enumerate(parts):
+            lanes = slice(256 + 128 * n, 384 + 128 * n)
+            for place, array in enumerate(pair):
+                rows = []
+                for q in range(8):
+                    x = held[:, 2 * half, q, lanes]
+                    y = held[:, 2 * half + 1, q, lanes]
+                    if place == 0:
+                        rows.append(jnp.where(low, x, pltpu.roll(y, 64, 1)))
+                    else:
+                        rows.append(jnp.where(low, pltpu.roll(x, 64, 1), y))
+                for g, values in enumerate(swap_groups(rows)):
+                    out[8 * half + g, array] = values
     send[...] = out[...].astype(BF)
 
 
-def whole(got, a):
-    return got[:, a].astype(F32).reshape(256, 256).astype(BF)
+def whole(got):
+    return got[:, :, 0:256].astype(F32).reshape(256, 256)
+
+
+def quarters(got, n):
+    return got[:, :, 256 + 128 * n : 384 + 128 * n].astype(F32).reshape(256, 128).T.astype(BF)
 
 
 def block_table():
@@ -104,61 +142,58 @@
     return (place == label).astype(F32).astype(BF)
 
 
-def masked(values, table, layer, flip):
-    side = dot(table, layer, ((1,), (1 if flip else 0,))).astype(BF)
-    return values * dot(side, table, ((1,), (1,))).astype(BF)
-
-
-def quarter(values, mate):
-    place = lax.broadcasted_iota(jnp.int32, (64, 256), 0) + 64 * mate
-    label = lax.broadcasted_iota(jnp.int32, (64, 256), 1)
-    return dot((place == label).astype(F32).astype(BF), values, ((1,), (1,))).astype(BF)
-
-
-def own_rows(got, a, mate):
-    return got[pl.ds(8 * mate, 8), a].astype(F32).reshape(64, 256).astype(BF)
+def spread_mask(table, layer):
+    side = dot(table, layer, NT).astype(BF)
+    return dot(side, table, NT)
 
 
 NN = ((1,), (0,))
 NT = ((1,), (1,))
-
-
-def forward_kernel(spot, got, by_i, send):
+TN = ((0,), (0,))
+
+
+def forward_kernel(spot, got, by_i, by_k, send):
     mate = spot[0]
     table = block_table()
-    right_out, right_in = whole(got, 1), whole(got, 3)
-    left_out = quarter(whole(got, 0), mate)
-    left_in = own_rows(got, 2, mate)
-    outs, ins = [], []
+    right_out = whole(got).astype(BF)
+    mixed = quarters(got, 0)
+    left_out, left_in = mixed[0:64], mixed[64:128]
+    right_in = quarters(got, 1)[0:64]
+    outs, ins = [], None
     for t in range(4):
-        layer = by_i[4 * mate + t]
         part = slice(16 * t, 16 * t + 16)
-        outs.append(dot(left_out[part], masked(right_out, table, layer, True), NN))
-        ins.append(dot(left_in[part], masked(right_in, table, layer, False), NT))
-    send[...] = jnp.concatenate(outs + ins, axis=0).T.reshape(32, 8, 128).astype(BF)
-
-
-def backward_kernel(spot, got, grads, by_i, by_j, by_k, send):
+        mask = spread_mask(table, by_i[4 * mate + t]).astype(BF)
+        outs.append(dot(left_out[part], right_out * mask, NN))
+        mask = spread_mask(table, by_k[4 * mate + t])
+        term = dot(right_in[part], left_in[part], TN) * mask
+        ins = term if ins is None else ins + term
+    outs = jnp.concatenate(outs + [jnp.zeros((64, 256), F32)], axis=0).T
+    send[:, :, 0:256] = ins.reshape(32, 8, 256).astype(BF)
+    send[:, :, 256:384] = outs.reshape(32, 8, 128).astype(BF)
+
+
+def backward_kernel(spot, got, grads, by_i, by_k, send):
     mate = spot[0]
     table = block_table()
-    left_out, right_out = whole(got, 0), whole(got, 1)
-    left_in = quarter(whole(got, 2), mate)
-    right_in = quarter(whole(got, 3), mate)
-    grad_out_i = quarter(whole(grads, 0), mate)
-    grad_out_j = own_rows(grads, 0, mate)
-    grad_in = whole(grads, 1)
-    results = [[], [], [], []]
+    right_out = whole(got).astype(BF)
+    mixed = quarters(got, 0)
+    left_out, left_in = mixed[0:64], mixed[64:128]
+    right_in = quarters(got, 1)[0:64]
+    grad_in = whole(grads).astype(BF)
+    grad_out = quarters(grads, 0)[0:64]
+    grad_left_out, grad_left_in, grad_right_in, grad_right_out = [], [], [], None
     for t in range(4):
         part = slice(16 * t, 16 * t + 16)
-        over_j = masked(right_out, table, by_i[4 * mate + t], True)
-        results[0].append(dot(grad_out_i[part], over_j, NT))
-        over_i = masked(left_out, table, by_j[4 * mate + t], True)
-        results[1].append(dot(grad_out_j[part], over_i, NT))
-        both = masked(grad_in, table, by_k[4 * mate + t], True)
-        results[2].append(dot(right_in[part], both, NN))
-        results[3].append(dot(left_in[part], both, NT))
-    stacked = jnp.concatenate(results[0] + results[1] + results[2] + results[3], axis=0)
-    send[...] = stacked.T.reshape(32, 8, 256).astype(BF)
+        mask = spread_mask(table, by_i[4 * mate + t])
+        grad_left_out.append(dot(grad_out[part], right_out * mask.astype(BF), NT))
+        term = dot(left_out[part], grad_out[part], TN) * mask
+        grad_right_out = term if grad_right_out is None else grad_right_out + term
+        both = grad_in * spread_mask(table, by_k[4 * mate + t]).astype(BF)
+        grad_left_in.append(dot(right_in[part], both, NN))
+        grad_right_in.append(dot(left_in[part], both, NT))
+    rest = grad_left_out + grad_left_in + grad_right_in + [jnp.zeros((64, 256), F32)]
+    send[:, :, 0:256] = grad_right_out.reshape(32, 8, 256).astype(BF)
+    send[:, :, 256:512] = jnp.concatenate(rest, axis=0).T.reshape(32, 8, 256).astype(BF)
 
 
 def middle_kernel(pair, cotangent, got, gates, gain, w_final, updated, send, grad_gate):
@@ -222,29 +257,29 @@
     return lax.all_to_all(values, axis, 0, 0, tiled=True)
 
 
-def to_channels(send):
-    amount = send.shape[1]
+def to_channels(send, full, parts):
     got = exchange(send, "row")
+    width = 256 + 128 * len(parts)
     spread = call(
-        spread_kernel,
-        ((8, 4, amount, 8, 256), BF),
+        functools.partial(spread_kernel, full, parts),
+        ((8, 4, 8, width), BF),
         got,
-        scratch=[(8, amount, 8, 256)],
-    )
-    return exchange(spread.reshape(32, amount, 8, 256), "col")
-
-
-def to_pairs(send):
+        scratch=[(8, 8, 256), (8, 4, 8, width - 256)],
+    )
+    return exchange(spread.reshape(32, 8, width), "col")
+
+
+def to_pairs(send, full, parts):
     width = send.shape[2]
-    amount = width // 64
+    amount = 1 + sum(len(pair) for pair in parts)
     got = exchange(send, "col").reshape(8, 4, 8, width)
     back = call(
-        collect_kernel,
-        ((4, 4, amount, 8, 128), BF),
+        functools.partial(collect_kernel, full, parts),
+        ((16, amount, 8, 128), BF),
         got,
-        scratch=[(8, 4, 8, width), (4, 4, amount, 8, 128)],
-    )
-    return exchange(back.reshape(16, amount, 8, 128), "row")
+        scratch=[(8, 4, 8, width), (16, amount, 8, 128)],
+    )
+    return exchange(back, "row")
 
 
 def on_device(
@@ -256,7 +291,6 @@
     update = update_gain.reshape(2, 128, 1)
     mate = (lax.axis_index("col") & 3).reshape(1)
     by_i = contact.astype(BF)
-    by_j = jnp.transpose(by_i, (1, 0, 2))
     by_k = jnp.transpose(by_i, (2, 0, 1))
 
     send, proj, gates, scaled_t, inv = call(
@@ -274,26 +308,25 @@
         w_in_proj,
         w_gate,
     )
-    sides = to_channels(send)
-    triangles = call(forward_kernel, ((32, 8, 128), BF), mate, sides, by_i, spot=True)
+    sides = to_channels(send, 1, ((0, 2), (3,)))
+    triangles = call(forward_kernel, ((32, 8, 384), BF), mate, sides, by_i, by_k, spot=True)
     updated, send, grad_gate = call(
         middle_kernel,
         [((128, 128), BF), ((16, 2, 8, 128), BF), ((256, 128), BF)],
         pair,
         upstream,
-        to_pairs(triangles),
+        to_pairs(triangles, 1, ((0,),)),
         gates,
         update,
         w_final,
     )
     grads = call(
         backward_kernel,
-        ((32, 8, 256), BF),
+        ((32, 8, 512), BF),
         mate,
         sides,
-        to_channels(send),
+        to_channels(send, 1, ((0,),)),
         by_i,
-        by_j,
         by_k,
         spot=True,
     )
@@ -301,7 +334,7 @@
         last_kernel,
         ((128, 128), BF),
         upstream,
-        to_pairs(grads),
+        to_pairs(grads, 1, ((0, 2), (3,))),
         proj,
         grad_gate,
         scaled_t,

time: 187 us -> 181 us (0.968)
  blocking collectives: 85.1 us -> 116 us
  waiting for transfers between devices: 55.9 us -> 26.4 us
  starting transfers between devices: 27.2 us -> 22.3 us
    all_to_all x5 -> x6, blocking collectives: 85.1 us -> 116 us  [exchange(): return lax.all_to_all(values, axis, 0, 0, tiled=True)]
    all_to_all x3 -> x2, waiting for transfers between devices: 55.9 us -> 26.4 us  [exchange(): return lax.all_to_all(values, axis, 0, 0, tiled=True)]
    all_to_all x3 -> x2, starting transfers between devices: 27.2 us -> 22.3 us  [exchange(): return lax.all_to_all(values, axis, 0, 0, tiled=True)]
  transfers between devices with their start and end apart: 3 -> 2, of which waited for: 3 -> 2; matrix products, arithmetic and copies ran while one was open for 0% -> 0% of each run, Pallas kernels for 0% -> 0%
where the time goes in v2:
time: 181 us; the launch traced here: 180 us
  blocking collectives  116 us (64%)
  waiting for transfers between devices  26.4 us (15%)
  starting transfers between devices  22.3 us (12%)
  Pallas kernels  10.5 us (6%)
  local copies, waits for them, and re-layouts  4.48 us (2%)
    all_to_all x6, blocking collectives, exchange(): return lax.all_to_all(values, axis, 0, 0, tiled=True)  116 us
    all_to_all x2, waiting for transfers between devices, exchange(): return lax.all_to_all(values, axis, 0, 0, tiled=True)  26.4 us
    all_to_all x2, starting transfers between devices, exchange(): return lax.all_to_all(values, axis, 0, 0, tiled=True)  22.3 us
    pallas_call x9, Pallas kernels, call(): pl.pallas_call(kernel, out_shape=shapes, in_specs=specs, out_specs=outs,...  10.5 us
    unnamed x25, local copies, waits for them, and re-layouts  4.1 us
  transfers between devices with their start and end apart: 2, of which 2 were waited for; matrix products, arithmetic and copies ran while one was open for 0% of the time, Pallas kernels for 0%

profile of v2, /device:TPU:1, one launch (start us, length us, event | category | flops | bytes accessed | tf_op | source)
XLA Modules:
  0.0 180.2 jit_solution(16964660136899305977)
XLA Ops:
  0.6 0.0 copy-start.11
  0.6 0.0 copy-start.4
  0.6 0.6 copy-done.11
  1.3 0.1 copy.16.gain
  1.4 0.1 copy-done.4
  1.5 0.0 copy-start
  1.5 0.9 copy-done
  2.4 0.0 copy-start.2
  2.4 0.9 copy-done.2
  3.3 0.0 copy-start.6
  3.3 0.8 copy-done.6
  4.1 0.5 shard_map.104
  4.5 16.7 %all_to_all.40.got = bf16[16,4,8,128]{3,2,1,0:T(8,128)(2,1)S(1)} all-to-all(bf16[16,4,8,128]{3,2,1,0:T(8,128)(2,1)S(1)} %get-tuple-element.10), channel_id=1, replica_groups=mesh['row'=16,'col'=32] {'row'}, dimensions={0} | all-to-all | bytes 262144 | tf_op jit(solution)/shard_map/all_to_all | solution.py:257
  21.2 1.3 shard_map.105
  22.5 0.0 copy-start.9
  22.5 17.4 %all-to-all-start.1 = ((bf16[32,8,512]{2,1,0:T(8,128)(2,1)}), bf16[32,8,512]{2,1,0:T(8,128)(2,1)S(1)}, u32[]{:S(2)}, u32[]{:S(2)}) async-start(bf16[32,8,512]{2,1,0:T(8,128)(2,1)} %bitcast.4), calls=%async_computation.1 | async-start | bytes 524288 | tf_op jit(solution)/shard_map/all_to_all | solution.py:257
  39.9 0.0 copy-done.9
  39.9 0.1 copy.17
  40.0 0.1 copy.18.by_i
  40.2 19.9 %all-to-all-done.1.got = bf16[32,8,512]{2,1,0:T(8,128)(2,1)S(1)} async-done(((bf16[32,8,512]{2,1,0:T(8,128)(2,1)}), bf16[32,8,512]{2,1,0:T(8,128)(2,1)S(1)}, u32[]{:S(2)}, u32[]{:S(2)}) %all-to-all-start.1) | async-done | bytes 262176 | tf_op jit(solution)/shard_map/all_to_all | solution.py:257
  60.1 2.1 %shard_map.106 = bf16[32,8,384]{2,1,0:T(8,128)(2,1)S(1)} custom-call(s32[1]{0:T(128)} %bitcast.2.spot, bf16[32,8,512]{2,1,0:T(8,128)(2,1)S(1)} %all-to-all-done.1.got, bf16[16,16,16]{2,1,0:T(8,128)(2,1)S(1)} %copy.18.by_i, bf16[16,16,16]{2,1,0:T(8,128)(2,1)S(1)} %convert_bitcast_fusion.by_k), custom_call_target="tpu_custom_call" | custom-call | tf_op jit(solution)/shard_map/pallas_call | solution.py:245
  62.2 25.2 %all_to_all.41 = bf16[32,8,384]{2,1,0:T(8,128)(2,1)S(1)} all-to-all(bf16[32,8,384]{2,1,0:T(8,128)(2,1)S(1)} %shard_map.106), channel_id=1, replica_groups=mesh['row'=16,'col'=32] {'col'}, dimensions={0} | all-to-all | bytes 393216 | tf_op jit(solution)/shard_map/all_to_all | solution.py:257
  87.4 1.0 shard_map.107
  88.4 4.9 %all-to-all-start.3 = ((bf16[16,2,8,128]{3,2,1,0:T(8,128)(2,1)}), bf16[16,2,8,128]{3,2,1,0:T(8,128)(2,1)S(1)}, u32[]{:S(2)}, u32[]{:S(2)}) async-start(bf16[16,2,8,128]{3,2,1,0:T(8,128)(2,1)} %shard_map.107), calls=%async_computation.3 | async-start | bytes 131072 | tf_op jit(solution)/shard_map/all_to_all | solution.py:257
  93.3 0.0 copy-start.10
  93.4 0.7 copy-done.10
  94.0 0.0 copy-start.5
  94.0 0.0 copy-start.7
  94.0 0.0 copy-start.8
  94.0 0.1 copy.19.gain
  94.2 6.4 %all-to-all-done.3.got = bf16[16,2,8,128]{3,2,1,0:T(8,128)(2,1)S(1)} async-done(((bf16[16,2,8,128]{3,2,1,0:T(8,128)(2,1)}), bf16[16,2,8,128]{3,2,1,0:T(8,128)(2,1)S(1)}, u32[]{:S(2)}, u32[]{:S(2)}) %all-to-all-start.3) | async-done | bytes 65568 | tf_op jit(solution)/shard_map/all_to_all | solution.py:257
  100.6 0.0 copy-done.5
  100.6 0.0 copy-done.7
  100.6 0.0 copy-done.8
  100.6 1.1 shard_map.108
  101.7 9.9 %all_to_all.42.got = bf16[16,2,8,128]{3,2,1,0:T(8,128)(2,1)S(1)} all-to-all(bf16[16,2,8,128]{3,2,1,0:T(8,128)(2,1)S(1)} %get-tuple-element.13), channel_id=1, replica_groups=mesh['row'=16,'col'=32] {'row'}, dimensions={0} | all-to-all | bytes 131072 | tf_op jit(solution)/shard_map/all_to_all | solution.py:257
  111.6 0.4 shard_map.109
  112.0 24.2 %all_to_all.43.grads = bf16[32,8,384]{2,1,0:T(8,128)(2,1)S(1)} all-to-all(bf16[32,8,384]{2,1,0:T(8,128)(2,1)S(1)} %bitcast.15), channel_id=1, replica_groups=mesh['row'=16,'col'=32] {'col'}, dimensions={0} | all-to-all | bytes 393216 | tf_op jit(solution)/shard_map/all_to_all | solution.py:257
  136.2 2.6 %shard_map.110 = bf16[32,8,512]{2,1,0:T(8,128)(2,1)S(1)} custom-call(s32[1]{0:T(128)} %bitcast.2.spot, bf16[32,8,512]{2,1,0:T(8,128)(2,1)S(1)} %all-to-all-done.1.got, bf16[32,8,384]{2,1,0:T(8,128)(2,1)S(1)} %all_to_all.43.grads, bf16[16,16,16]{2,1,0:T(8,128)(2,1)S(1)} %copy.18.by_i, bf16[16,16,16]{2,1,0:T(8,128)(2,1)S(1)} %convert_bitcast_fusion.by_k), custom_call_target="tpu_custom_call" | custom-call | tf_op jit(solution)/shard_map/pallas_call | solution.py:245
  138.8 25.7 %all_to_all.44 = bf16[32,8,512]{2,1,0:T(8,128)(2,1)S(1)} all-to-all(bf16[32,8,512]{2,1,0:T(8,128)(2,1)S(1)} %shard_map.110), channel_id=1, replica_groups=mesh['row'=16,'col'=32] {'col'}, dimensions={0} | all-to-all | bytes 524288 | tf_op jit(solution)/shard_map/all_to_all | solution.py:257
  164.5 0.5 shard_map.111
  165.0 0.0 copy-start.1
  165.0 0.0 copy-start.3
  165.0 14.1 %all_to_all.45.got = bf16[16,4,8,128]{3,2,1,0:T(8,128)(2,1)S(1)} all-to-all(bf16[16,4,8,128]{3,2,1,0:T(8,128)(2,1)S(1)} %shard_map.111), channel_id=1, replica_groups=mesh['row'=16,'col'=32] {'row'}, dimensions={0} | all-to-all | bytes 262144 | tf_op jit(solution)/shard_map/all_to_all | solution.py:257
  179.1 0.0 copy-done.1
  179.1 0.0 copy-done.3
  179.1 1.1 shard_map.112
  (2 shorter events, 0.0 us)
Async XLA Ops:
  0.6 0.7 copy-start.11
  0.6 0.8 copy-start.4
  1.5 0.9 copy-start
  2.4 0.9 copy-start.2
  3.3 0.8 copy-start.6
  22.5 17.4 %copy-start.9 = (s32[16,16,16]{2,1,0:T(8,128)S(1)}, s32[16,16,16]{2,1,0:T(8,128)}, u32[]{:S(2)}) copy-start(s32[16,16,16]{2,1,0:T(8,128)} %param.11) | copy-start | bytes 49156
  22.5 37.6 %all-to-all-start.1 = ((bf16[32,8,512]{2,1,0:T(8,128)(2,1)}), bf16[32,8,512]{2,1,0:T(8,128)(2,1)S(1)}, u32[]{:S(2)}, u32[]{:S(2)}) async-start(bf16[32,8,512]{2,1,0:T(8,128)(2,1)} %bitcast.4), calls=%async_computation.1 | async-start | bytes 524288 | tf_op jit(solution)/shard_map/all_to_all | solution.py:257
  88.4 12.2 %all-to-all-start.3 = ((bf16[16,2,8,128]{3,2,1,0:T(8,128)(2,1)}), bf16[16,2,8,128]{3,2,1,0:T(8,128)(2,1)S(1)}, u32[]{:S(2)}, u32[]{:S(2)}) async-start(bf16[16,2,8,128]{3,2,1,0:T(8,128)(2,1)} %shard_map.107), calls=%async_computation.3 | async-start | bytes 131072 | tf_op jit(solution)/shard_map/all_to_all | solution.py:257
  93.3 0.7 copy-start.10
  94.0 6.6 %copy-start.5 = (bf16[16,8,128]{2,1,0:T(8,128)(2,1)S(1)}, bf16[16,8,128]{2,1,0:T(8,128)(2,1)}, u32[]{:S(2)}) copy-start(bf16[16,8,128]{2,1,0:T(8,128)(2,1)} %param.10) | copy-start | bytes 98308
  94.0 6.6 %copy-start.7 = (bf16[16,8,128]{2,1,0:T(8,128)(2,1)S(1)}, bf16[16,8,128]{2,1,0:T(8,128)(2,1)}, u32[]{:S(2)}) copy-start(bf16[16,8,128]{2,1,0:T(8,128)(2,1)} %param.9) | copy-start | bytes 98308
  94.0 6.6 %copy-start.8 = (bf16[2,128,128]{2,1,0:T(8,128)(2,1)S(1)}, bf16[2,128,128]{2,1,0:T(8,128)(2,1)}, u32[]{:S(2)}) copy-start(bf16[2,128,128]{2,1,0:T(8,128)(2,1)} %w_final.1) | copy-start | bytes 196612
  165.0 14.1 %copy-start.1 = (bf16[128,512]{1,0:T(8,128)(2,1)S(1)}, bf16[128,512]{1,0:T(8,128)(2,1)}, u32[]{:S(2)}) copy-start(bf16[128,512]{1,0:T(8,128)(2,1)} %w_out.3) | copy-start | bytes 393220
  165.0 14.1 %copy-start.3 = (bf16[128,512]{1,0:T(8,128)(2,1)S(1)}, bf16[128,512]{1,0:T(8,128)(2,1)}, u32[]{:S(2)}) copy-start(bf16[128,512]{1,0:T(8,128)(2,1)} %w_in.3) | copy-start | bytes 393220

commit v3 on v2

v3 whole, which is shorter than its diff:
```python
import functools

import jax
import jax.numpy as jnp
from jax import lax
from jax.experimental import pallas as pl
from jax.experimental.pallas import tpu as pltpu
from jax.sharding import Mesh
from jax.sharding import PartitionSpec as P


PLANE = ("x", "y", "core")
DEPTH = ("zl", "zh")
EPSILON = 1e-05
BF = jnp.bfloat16
F32 = jnp.float32


def dot(a, b, dims=((1,), (0,))):
    return lax.dot_general(a, b, (dims, ((), ())), preferred_element_type=F32)


def norm(values):
    center = jnp.mean(values, axis=0, keepdims=True)
    shifted = values - center
    inverse = lax.rsqrt(jnp.mean(shifted * shifted, axis=0, keepdims=True) + EPSILON)
    return shifted * inverse, inverse


def norm_back(weighted, scaled, inverse):
    first = jnp.mean(weighted, axis=0, keepdims=True)
    second = jnp.mean(weighted * scaled, axis=0, keepdims=True)
    return inverse * (weighted - first - scaled * second)


def pair_order():
    here = lax.broadcasted_iota(jnp.int32, (128, 128), 0)
    there = lax.broadcasted_iota(jnp.int32, (128, 128), 1)
    same = (here >> 3 == (there & 15)) & ((here & 7) == there >> 4)
    return same.astype(F32).astype(BF)


def column(gain):
    return jnp.broadcast_to(gain, (128, 128)).T


def put(held, array, values):
    for n in range(4):
        held[:, 4 * array + n] = values[32 * n : 32 * n + 32]


def take(got, array):
    return jnp.concatenate([got[:, 4 * array + n] for n in range(4)], axis=0)


def fetch(pairs, arrived):
    copies = [
        pltpu.make_async_copy(there, here, arrived.at[n]) for n, (there, here) in enumerate(pairs)
    ]
    for copy in copies:
        copy.start()
    return copies


def first_kernel(*refs):
    far, (send, proj, gates, scaled_t, inv), near = refs[:5], refs[5:10], refs[10:15]
    held, arrived = refs[15:]
    copies = fetch(list(zip(far, near)), arrived)
    pair, gain, w_out, w_in, w_gate = near
    copies[0].wait()
    pair_t = dot(pair[...], pair_order(), ((0,), (0,)))
    scaled, inverse = norm(pair_t)
    copies[1].wait()
    normed = (scaled * column(gain[...])).astype(BF)
    scaled_t[...] = scaled
    inv[...] = inverse
    for half, weights in enumerate((w_out, w_in)):
        copies[2 + half].wait()
        p = dot(weights[...], normed, ((0,), (0,)))
        proj[half] = p
        put(held, 2 * half, jax.nn.sigmoid(p[0:128]) * p[128:256])
        put(held, 2 * half + 1, jax.nn.sigmoid(p[256:384]) * p[384:512])
    send[...] = held[...].astype(BF)
    copies[4].wait()
    gates[...] = jax.nn.sigmoid(dot(w_gate[...], normed, ((0,), (0,))))


def swap_groups(rows):
    rows = list(rows)
    group = lax.broadcasted_iota(jnp.int32, rows[0].shape, 1) >> 4
    step = len(rows) // 2
    while step:
        low = (group & step) == 0
        for a in range(len(rows)):
            if a & step:
                continue
            x, y = rows[a], rows[a + step]
            rows[a] = jnp.where(low, x, pltpu.roll(y, 16 * step, 1))
            rows[a + step] = jnp.where(low, pltpu.roll(x, 128 - 16 * step, 1), y)
        step //= 2
    return rows


def spread_kernel(full, parts, got, send, held_full, held_parts):
    by_y = []
    for y in range(4):
        rows = swap_groups(
            [got[8 * x + 2 * y + core].astype(F32) for core in range(2) for x in range(4)]
        )
        for q in range(8):
            held_full[:, 8 * y + q] = rows[q][4 * full : 4 * full + 4]
        by_y.append(rows)
    for q in range(8):
        for mate, rows in enumerate(swap_groups([by_y[y][q] for y in range(4)])):
            for n, a in enumerate(parts):
                held_parts[:, mate, 8 * n + q] = rows[4 * a : 4 * a + 4]
    values = held_full[...].astype(BF)
    for mate in range(4):
        send[:, mate, 0:32] = values
    send[:, :, 32:] = held_parts[...].astype(BF)


def collect_kernel(full, parts, got, send, held, held_parts, out):
    values = got[...].astype(F32)
    held[...] = values[:, 0, 0:32] + values[:, 1, 0:32] + values[:, 2, 0:32] + values[:, 3, 0:32]
    held_parts[...] = values[:, :, 32:]
    for a in (full, *parts):
        by_q = []
        for q in range(8):
            if a == full:
                by_q.append([held[:, 8 * y + q] for y in range(4)])
            else:
                row = 8 * parts.index(a) + q
                by_q.append(swap_groups([held_parts[:, mate, row] for mate in range(4)]))
        for y in range(4):
            for g, rows in enumerate(swap_groups([by_q[q][y] for q in range(8)])):
                out[8 * (g & 3) + 2 * y + (g >> 2), 4 * a : 4 * a + 4] = rows
    send[...] = out[...].astype(BF)


def swap_halves(first, second):
    low = lax.broadcasted_iota(jnp.int32, first.shape, 1) < 64
    return (
        jnp.where(low, first, pltpu.roll(second, 64, 1)),
        jnp.where(low, pltpu.roll(first, 64, 1), second),
    )


def reorder():
    residue = lax.broadcasted_iota(jnp.int32, (256, 256), 0)
    place = lax.broadcasted_iota(jnp.int32, (256, 256), 1)
    return one_hot(residue, q_block(place) * 16 + (place >> 7) * 8 + (place & 7))


def whole(got):
    tiles = [got[zl, :, 0:32].astype(F32).reshape(128, 128) for zl in range(4)]
    left = swap_halves(tiles[0], tiles[1])
    right = swap_halves(tiles[2], tiles[3])
    values = jnp.concatenate(
        [jnp.concatenate([left[core], right[core]], axis=1) for core in range(2)], axis=0
    )
    return dot(values.astype(BF), reorder()).astype(BF)


def quarter(got, n):
    by_zh = []
    for zh in range(4):
        tiles = [got[zl, zh, 32 + 8 * n : 40 + 8 * n].astype(F32) for zl in range(4)]
        by_zh += swap_groups(tiles)
    turned = jnp.concatenate(by_zh, axis=0).T
    return jnp.concatenate([turned[0:64], turned[64:128]], axis=1).astype(BF)


def send_whole(send, values):
    values = dot(values.astype(BF), reorder(), NT)
    for half in range(2):
        lanes = slice(128 * half, 128 * half + 128)
        tiles = swap_halves(values[0:128, lanes], values[128:256, lanes])
        for n in range(2):
            send[2 * half + n, :, 0:32] = tiles[n].reshape(4, 32, 128).astype(BF)


def send_quarter(send, n, held, values):
    turned = jnp.concatenate([values[:, 0:128], values[:, 128:256]], axis=0).T
    for zh in range(4):
        rows = [turned[32 * zh + 8 * y : 32 * zh + 8 * y + 8] for y in range(4)]
        for zl, tile in enumerate(swap_groups(rows)):
            held[zl, zh, 8 * n : 8 * n + 8] = tile


NN = ((1,), (0,))
NT = ((1,), (1,))
TN = ((0,), (0,))


def one_hot(label, values):
    return (label == values).astype(F32).astype(BF)


def q_block(place):
    return ((place >> 3) & 3) * 4 + ((place >> 5) & 3)


def mask_tables():
    place = lax.broadcasted_iota(jnp.int32, (256, 16), 0)
    label = lax.broadcasted_iota(jnp.int32, (256, 16), 1)
    q_table = one_hot(label, q_block(place))
    place = lax.broadcasted_iota(jnp.int32, (256, 256), 0)
    label = lax.broadcasted_iota(jnp.int32, (256, 256), 1)
    j_table, i_table = one_hot(label & 15, q_block(place)), one_hot(label >> 4, q_block(place))
    return q_table, j_table, i_table


def mask_out(tables, contact, i):
    side = dot(tables[0], contact[i].astype(F32).astype(BF), NT).astype(BF)
    return dot(side, tables[0], NT)


def mask_in(tables, by_k, k):
    return dot(tables[1] * by_k[pl.ds(k, 1)].astype(BF), tables[2], NT)


def forward_kernel(spot, got, contact, flat, send, by_k, held):
    mate = spot[0]
    tables = mask_tables()
    by_k[...] = flat[...].astype(F32).T
    right_out = whole(got)
    left_out, left_in, right_in = [quarter(got, n) for n in range(3)]
    outs, ins = [], None
    for t in range(4):
        part = slice(16 * t, 16 * t + 16)
        mask = mask_out(tables, contact, 4 * t + mate).astype(BF)
        outs.append(dot(left_out[part], right_out * mask, NN))
        mask = mask_in(tables, by_k, 4 * t + mate)
        term = dot(right_in[part], left_in[part], TN) * mask
        ins = term if ins is None else ins + term
    send_whole(send, ins)
    send_quarter(send, 0, held, jnp.concatenate(outs, axis=0))
    send[:, :, 32:] = held[...].astype(BF)


def backward_kernel(spot, got, grads, contact, flat, send, by_k, held):
    mate = spot[0]
    tables = mask_tables()
    by_k[...] = flat[...].astype(F32).T
    right_out = whole(got)
    left_out, left_in, right_in = [quarter(got, n) for n in range(3)]
    grad_in = whole(grads)
    grad_out = quarter(grads, 0)
    grad_left_out, grad_left_in, grad_right_in, grad_right_out = [], [], [], None
    for t in range(4):
        part = slice(16 * t, 16 * t + 16)
        mask = mask_out(tables, contact, 4 * t + mate)
        grad_left_out.append(dot(grad_out[part], right_out * mask.astype(BF), NT))
        term = dot(left_out[part], grad_out[part], TN) * mask
        grad_right_out = term if grad_right_out is None else grad_right_out + term
        both = grad_in * mask_in(tables, by_k, 4 * t + mate).astype(BF)
        grad_left_in.append(dot(right_in[part], both, NN))
        grad_right_in.append(dot(left_in[part], both, NT))
    send_whole(send, grad_right_out)
    for n, values in enumerate((grad_left_out, grad_left_in, grad_right_in)):
        send_quarter(send, n, held, jnp.concatenate(values, axis=0))
    send[:, :, 32:] = held[...].astype(BF)


def middle_kernel(pair, cotangent, got, gates, gain, w_final, updated, send, grad_gate, held):
    order = pair_order()
    upstream = dot(cotangent[...], order, TN)
    total = dot(pair[...], order, TN)
    arrived = got[...].astype(F32)
    for t in range(2):
        scaled, inverse = norm(take(arrived, t))
        gain_t = column(gain[t : t + 1])
        normed = (scaled * gain_t).astype(BF)
        gate = gates[128 * t : 128 * t + 128]
        final = dot(w_final[t], normed, TN)
        total = total + gate * final
        grad_final = (upstream * gate).astype(BF)
        grad_gate[128 * t : 128 * t + 128] = (upstream * final * gate * (1.0 - gate)).astype(BF)
        weighted = dot(w_final[t], grad_final) * gain_t
        put(held, t, norm_back(weighted, scaled, inverse))
    send[...] = held[...].astype(BF)
    updated[...] = dot(order, total.astype(BF), NT).astype(BF)


def last_kernel(
    cotangent, got, proj, grad_gate, scaled_t, inv, gain, w_out, w_in, w_gate, grad_pair
):
    order = pair_order()
    upstream = dot(cotangent[...], order, TN)
    arrived = got[...].astype(F32)
    grad_normed = dot(w_gate[...], grad_gate[...])
    for half, weights in enumerate((w_out, w_in)):
        p = proj[half]
        parts = []
        for side in range(2):
            grad = take(arrived, 2 * half + side)
            sig = jax.nn.sigmoid(p[256 * side : 256 * side + 128])
            parts.append(grad * p[256 * side + 128 : 256 * side + 256] * sig * (1.0 - sig))
            parts.append(grad * sig)
        grad_normed = grad_normed + dot(
            weights[...], jnp.concatenate(parts, axis=0).astype(BF)
        )
    back = norm_back(grad_normed * column(gain[...]), scaled_t[...], inv[...])
    grad_pair[...] = dot(order, (upstream + back).astype(BF), NT).astype(BF)


def call(kernel, out, *args, scratch=(), spot=False, far=False):
    place = pl.ANY if far else pltpu.VMEM
    specs = [pl.BlockSpec(memory_space=place)] * len(args)
    if spot:
        specs[0] = pl.BlockSpec(memory_space=pltpu.SMEM)
    multi = isinstance(out, list)
    shapes = [jax.ShapeDtypeStruct(s, d) for s, d in (out if multi else [out])]
    outs = [pl.BlockSpec(memory_space=pltpu.VMEM)] * len(shapes)
    buffers = [pltpu.VMEM(s, F32) for s in scratch]
    params = pltpu.CompilerParams(vmem_limit_bytes=32 * 1024 * 1024)
    if far:
        buffers = [pltpu.VMEM(x.shape, x.dtype) for x in args] + buffers
        buffers.append(pltpu.SemaphoreType.DMA((len(args),)))
        params = None
    result = pl.pallas_call(
        kernel,
        out_shape=shapes,
        in_specs=specs,
        out_specs=outs,
        scratch_shapes=buffers,
        compiler_params=params,
    )(*args)
    return result if multi else result[0]


def exchange(values, axis):
    return lax.all_to_all(values, axis, 0, 0, tiled=True)


def to_channels(send, full, parts):
    rows = 32 + 8 * len(parts)
    spread = call(
        functools.partial(spread_kernel, full, parts),
        ((4, 4, rows, 128), BF),
        exchange(send, PLANE),
        scratch=[(4, 32, 128), (4, 4, rows - 32, 128)],
    )
    return exchange(spread.reshape(16, rows, 128), DEPTH).reshape(4, 4, rows, 128)


def to_pairs(send, full, parts):
    rows = 32 + 8 * len(parts)
    amount = 1 + len(parts)
    back = call(
        functools.partial(collect_kernel, full, parts),
        ((32, 4 * amount, 128), BF),
        exchange(send.reshape(16, rows, 128), DEPTH).reshape(4, 4, rows, 128),
        scratch=[(4, 32, 128), (4, 4, rows - 32, 128), (32, 4 * amount, 128)],
    )
    return exchange(back, PLANE)


def my_mate():
    return lax.axis_index("zh")


def on_device(
    pair_rep, cotangent, contact, norm_gain, w_out_proj, w_in_proj, update_gain, w_gate, w_final
):
    pair = pair_rep.reshape(128, 128)
    upstream = cotangent.reshape(128, 128)
    gain = norm_gain.reshape(1, 128)
    mate = my_mate().reshape(1)
    flat = contact.reshape(256, 16)

    send, proj, gates, scaled_t, inv = call(
        first_kernel,
        [
            ((32, 16, 128), BF),
            ((2, 512, 128), F32),
            ((256, 128), F32),
            ((128, 128), F32),
            ((1, 128), F32),
        ],
        pair,
        gain,
        w_out_proj,
        w_in_proj,
        w_gate,
        scratch=[(32, 16, 128)],
        far=True,
    )
    sides = to_channels(send, 1, (0, 2, 3))
    triangles = call(
        forward_kernel,
        ((4, 4, 40, 128), BF),
        mate,
        sides,
        contact,
        flat,
        scratch=[(16, 256), (4, 4, 8, 128)],
        spot=True,
    )
    updated, send, grad_gate = call(
        middle_kernel,
        [((128, 128), BF), ((32, 8, 128), BF), ((256, 128), BF)],
        pair,
        upstream,
        to_pairs(triangles, 1, (0,)),
        gates,
        update_gain,
        w_final,
        scratch=[(32, 8, 128)],
    )
    grads = call(
        backward_kernel,
        ((4, 4, 56, 128), BF),
        mate,
        sides,
        to_channels(send, 1, (0,)),
        contact,
        flat,
        scratch=[(16, 256), (4, 4, 24, 128)],
        spot=True,
    )
    grad_pair = call(
        last_kernel,
        ((128, 128), BF),
        upstream,
        to_pairs(grads, 1, (0, 2, 3)),
        proj,
        grad_gate,
        scaled_t,
        inv,
        gain,
        w_out_proj,
        w_in_proj,
        w_gate,
    )
    return (updated.reshape(pair_rep.shape), grad_pair.reshape(pair_rep.shape))


def solution(mesh):
    fine = Mesh(mesh.devices.reshape(4, 4, 4, 4, 2), ("zl", "x", "y", "zh", "core"))
    block = P(("zl", "x"), ("y", "zh", "core"), None)
    in_specs = (block, block, P(), P(), P(), P(), P(), P(), P())
    return jax.shard_map(
        on_device, mesh=fine, in_specs=in_specs, out_specs=(block, block), check_vma=False
    )
```

time: 181 us -> 160 us (0.88)
  waiting for transfers between devices: 26.4 us -> 15.2 us
  starting transfers between devices: 22.3 us -> 13.2 us
  local copies, waits for them, and re-layouts: 4.48 us -> 1.33 us
  Pallas kernels: 10.5 us -> 13.1 us
    all_to_all x2 -> x1, waiting for transfers between devices: 26.4 us -> 15.2 us  [exchange(): return lax.all_to_all(values, axis, 0, 0, tiled=True)]
    all_to_all x2 -> x1, starting transfers between devices: 22.3 us -> 13.2 us  [exchange(): return lax.all_to_all(values, axis, 0, 0, tiled=True)]
    unnamed x25 -> x26, local copies, waits for them, and re-layouts: 4.1 us -> 1.33 us
    pallas_call x9, Pallas kernels: 10.5 us -> 13.1 us  [call(): pl.pallas_call(kernel, out_shape=shapes, in_specs=specs, out_specs=outs,...]
    all_to_all x6 -> x7, blocking collectives: 116 us -> 115 us  [exchange(): return lax.all_to_all(values, axis, 0, 0, tiled=True)]
  transfers between devices with their start and end apart: 2 -> 1, of which waited for: 2 -> 1; matrix products, arithmetic and copies ran while one was open for 0% -> 0% of each run, Pallas kernels for 0% -> 0%
where the time goes in v3:
time: 160 us; the launch traced here: 159 us
  blocking collectives  115 us (72%)
  waiting for transfers between devices  15.2 us (10%)
  starting transfers between devices  13.2 us (8%)
  Pallas kernels  13.1 us (8%)
    all_to_all x7, blocking collectives, exchange(): return lax.all_to_all(values, axis, 0, 0, tiled=True)  115 us
    all_to_all x1, waiting for transfers between devices, exchange(): return lax.all_to_all(values, axis, 0, 0, tiled=True)  15.2 us
    all_to_all x1, starting transfers between devices, exchange(): return lax.all_to_all(values, axis, 0, 0, tiled=True)  13.2 us
    pallas_call x9, Pallas kernels, call(): pl.pallas_call(kernel, out_shape=shapes, in_specs=specs, out_specs=outs,...  13.1 us
  transfers between devices with their start and end apart: 1, of which 1 were waited for; matrix products, arithmetic and copies ran while one was open for 0% of the time, Pallas kernels for 0%

profile of v3, /device:TPU:1, one launch (start us, length us, event | category | flops | bytes accessed | tf_op | source)
XLA Modules:
  0.0 158.5 jit_solution(11132185220021971907)
XLA Ops:
  0.6 2.6 %shard_map.104 = (bf16[32,16,128]{2,1,0:T(8,128)(2,1)}, f32[2,512,128]{2,1,0:T(8,128)}, f32[256,128]{1,0:T(8,128)}, f32[128,128]{1,0:T(8,128)}, f32[1,128]{1,0:T(1,128)}) custom-call(bf16[128,128]{1,0:T(8,128)(2,1)} %bitcast.27, f32[1,128]{1,0:T(1,128)} %bitcast.29, bf16[128,512]{1,0:T(8,128)(2,1)} %w_out.1, bf16[128,512]{1,0:T(8,128)(2,1)} %w_in.1, ...), custom_call_target="tpu_custom_call" | custom-call | tf_op jit(solution)/shard_map/pallas_call | solution.py:322
  3.3 18.2 %all_to_all.40.got = bf16[32,16,128]{2,1,0:T(8,128)(2,1)S(1)} all-to-all(bf16[32,16,128]{2,1,0:T(8,128)(2,1)} %get-tuple-element.10), channel_id=1, replica_groups=mesh['zl'=4,'x'=4,'y'=4,'zh'=4,'core'=2] {'x','y','core'}, dimensions={0} | all-to-all | bytes 262144 | tf_op jit(solution)/shard_map/all_to_all | solution.py:334
  21.5 1.2 shard_map.105
  22.7 0.0 copy-start
  22.7 13.2 %all-to-all-start.1 = ((bf16[16,56,128]{2,1,0:T(8,128)(2,1)}), bf16[16,56,128]{2,1,0:T(8,128)(2,1)S(1)}, u32[]{:S(2)}, u32[]{:S(2)}) async-start(bf16[16,56,128]{2,1,0:T(8,128)(2,1)} %bitcast.4), calls=%async_computation.1 | async-start | bytes 458752 | tf_op jit(solution)/shard_map/all_to_all | solution.py:334
  35.9 15.2 %all-to-all-done.1 = bf16[16,56,128]{2,1,0:T(8,128)(2,1)S(1)} async-done(((bf16[16,56,128]{2,1,0:T(8,128)(2,1)}), bf16[16,56,128]{2,1,0:T(8,128)(2,1)S(1)}, u32[]{:S(2)}, u32[]{:S(2)}) %all-to-all-start.1) | async-done | bytes 229408 | tf_op jit(solution)/shard_map/all_to_all | solution.py:334
  51.1 0.0 copy-done
  51.1 2.0 %shard_map.106 = bf16[4,4,40,128]{3,2,1,0:T(8,128)(2,1)S(1)} custom-call(s32[1]{0:T(128)} %bitcast.2.spot, bf16[4,4,56,128]{3,2,1,0:T(8,128)(2,1)S(1)} %bitcast.17, s32[16,16,16]{2,1,0:T(8,128)S(1)} %copy-done, s32[256,16]{1,0:T(8,128)S(1)} %bitcast.15), custom_call_target="tpu_custom_call" | custom-call | tf_op jit(solution)/shard_map/pallas_call | solution.py:322
  53.1 19.3 %all_to_all.41 = bf16[16,40,128]{2,1,0:T(8,128)(2,1)S(1)} all-to-all(bf16[16,40,128]{2,1,0:T(8,128)(2,1)S(1)} %bitcast.24), channel_id=1, replica_groups=mesh['zl'=4,'x'=4,'y'=4,'zh'=4,'core'=2] {'zl','zh'}, dimensions={0} | all-to-all | bytes 327680 | tf_op jit(solution)/shard_map/all_to_all | solution.py:334
  72.4 0.0 copy-start.6
  72.4 0.5 shard_map.107
  72.9 0.0 copy-start.5
  72.9 0.0 copy-start.7
  72.9 0.0 copy-start.8
  72.9 14.7 %all_to_all.42.got = bf16[32,8,128]{2,1,0:T(8,128)(2,1)S(1)} all-to-all(bf16[32,8,128]{2,1,0:T(8,128)(2,1)S(1)} %shard_map.107), channel_id=1, replica_groups=mesh['zl'=4,'x'=4,'y'=4,'zh'=4,'core'=2] {'x','y','core'}, dimensions={0} | all-to-all | bytes 131072 | tf_op jit(solution)/shard_map/all_to_all | solution.py:334
  87.6 0.0 copy-start.11
  87.6 0.0 copy-done.6
  87.6 0.0 copy-done.5
  87.6 0.0 copy-done.7
  87.6 0.0 copy-done.8
  87.6 0.7 copy-done.11
  88.3 1.1 shard_map.108
  89.4 10.9 %all_to_all.43.got = bf16[32,8,128]{2,1,0:T(8,128)(2,1)S(1)} all-to-all(bf16[32,8,128]{2,1,0:T(8,128)(2,1)S(1)} %get-tuple-element.13), channel_id=1, replica_groups=mesh['zl'=4,'x'=4,'y'=4,'zh'=4,'core'=2] {'x','y','core'}, dimensions={0} | all-to-all | bytes 131072 | tf_op jit(solution)/shard_map/all_to_all | solution.py:334
  100.2 0.4 shard_map.109
  100.6 16.5 %all_to_all.44 = bf16[16,40,128]{2,1,0:T(8,128)(2,1)S(1)} all-to-all(bf16[16,40,128]{2,1,0:T(8,128)(2,1)S(1)} %bitcast.22), channel_id=1, replica_groups=mesh['zl'=4,'x'=4,'y'=4,'zh'=4,'core'=2] {'zl','zh'}, dimensions={0} | all-to-all | bytes 327680 | tf_op jit(solution)/shard_map/all_to_all | solution.py:334
  117.1 2.2 %shard_map.110 = bf16[4,4,56,128]{3,2,1,0:T(8,128)(2,1)S(1)} custom-call(s32[1]{0:T(128)} %bitcast.2.spot, bf16[4,4,56,128]{3,2,1,0:T(8,128)(2,1)S(1)} %bitcast.18, bf16[4,4,40,128]{3,2,1,0:T(8,128)(2,1)S(1)} %bitcast.23, s32[16,16,16]{2,1,0:T(8,128)S(1)} %copy-done, s32[256,16]{1,0:T(8,128)S(1)} %bitcast.16), custom_call_target="tpu_custom_call" | custom-call | tf_op jit(solution)/shard_map/pallas_call | solution.py:322
  119.3 0.0 copy-start.1
  119.3 19.4 %all_to_all.45 = bf16[16,56,128]{2,1,0:T(8,128)(2,1)S(1)} all-to-all(bf16[16,56,128]{2,1,0:T(8,128)(2,1)S(1)} %bitcast.19), channel_id=1, replica_groups=mesh['zl'=4,'x'=4,'y'=4,'zh'=4,'core'=2] {'zl','zh'}, dimensions={0} | all-to-all | bytes 458752 | tf_op jit(solution)/shard_map/all_to_all | solution.py:334
  138.7 0.0 copy-start.4
  138.8 0.0 copy-start.9
  138.8 1.9 %shard_map.111 = bf16[32,16,128]{2,1,0:T(8,128)(2,1)S(1)} custom-call(bf16[4,4,56,128]{3,2,1,0:T(8,128)(2,1)S(1)} %bitcast.20), custom_call_target="tpu_custom_call" | custom-call | tf_op jit(solution)/shard_map/pallas_call | solution.py:322
  140.6 0.0 copy-start.2
  140.6 0.0 copy-start.3
  140.6 16.1 %all_to_all.46.got = bf16[32,16,128]{2,1,0:T(8,128)(2,1)S(1)} all-to-all(bf16[32,16,128]{2,1,0:T(8,128)(2,1)S(1)} %shard_map.111), channel_id=1, replica_groups=mesh['zl'=4,'x'=4,'y'=4,'zh'=4,'core'=2] {'x','y','core'}, dimensions={0} | all-to-all | bytes 262144 | tf_op jit(solution)/shard_map/all_to_all | solution.py:334
  156.7 0.0 copy-start.10
  156.7 0.0 copy-start.12
  156.7 0.0 copy-done.1
  156.7 0.0 copy-done.4
  156.7 0.0 copy-done.9
  156.7 0.0 copy-done.2
  156.7 0.0 copy-done.3
  156.7 0.6 copy-done.10
  157.4 0.0 copy-done.12
  157.4 1.2 shard_map.112
Async XLA Ops:
  22.7 28.3 %copy-start = (s32[16,16,16]{2,1,0:T(8,128)S(1)}, s32[16,16,16]{2,1,0:T(8,128)}, u32[]{:S(2)}) copy-start(s32[16,16,16]{2,1,0:T(8,128)} %contact.3) | copy-start | bytes 49156
  22.7 28.3 %all-to-all-start.1 = ((bf16[16,56,128]{2,1,0:T(8,128)(2,1)}), bf16[16,56,128]{2,1,0:T(8,128)(2,1)S(1)}, u32[]{:S(2)}, u32[]{:S(2)}) async-start(bf16[16,56,128]{2,1,0:T(8,128)(2,1)} %bitcast.4), calls=%async_computation.1 | async-start | bytes 458752 | tf_op jit(solution)/shard_map/all_to_all | solution.py:334
  72.4 15.2 %copy-start.6 = (f32[256,128]{1,0:T(8,128)S(1)}, f32[256,128]{1,0:T(8,128)}, u32[]{:S(2)}) copy-start(f32[256,128]{1,0:T(8,128)} %get-tuple-element.11.gates) | copy-start | bytes 393220
  72.9 14.7 %copy-start.5 = (bf16[16,8,128]{2,1,0:T(8,128)(2,1)S(1)}, bf16[16,8,128]{2,1,0:T(8,128)(2,1)}, u32[]{:S(2)}) copy-start(bf16[16,8,128]{2,1,0:T(8,128)(2,1)} %param.10) | copy-start | bytes 98308
  72.9 14.7 %copy-start.7 = (bf16[16,8,128]{2,1,0:T(8,128)(2,1)S(1)}, bf16[16,8,128]{2,1,0:T(8,128)(2,1)}, u32[]{:S(2)}) copy-start(bf16[16,8,128]{2,1,0:T(8,128)(2,1)} %param.9) | copy-start | bytes 98308
  72.9 14.7 %copy-start.8 = (bf16[2,128,128]{2,1,0:T(8,128)(2,1)S(1)}, bf16[2,128,128]{2,1,0:T(8,128)(2,1)}, u32[]{:S(2)}) copy-start(bf16[2,128,128]{2,1,0:T(8,128)(2,1)} %w_final.1) | copy-start | bytes 196612
  87.6 0.7 copy-start.11
  119.3 37.4 %copy-start.1 = (f32[2,512,128]{2,1,0:T(8,128)S(1)}, f32[2,512,128]{2,1,0:T(8,128)}, u32[]{:S(2)}) copy-start(f32[2,512,128]{2,1,0:T(8,128)} %get-tuple-element.14.proj) | copy-start | bytes 1572868
  138.7 18.0 %copy-start.4 = (bf16[128,256]{1,0:T(8,128)(2,1)S(1)}, bf16[128,256]{1,0:T(8,128)(2,1)}, u32[]{:S(2)}) copy-start(bf16[128,256]{1,0:T(8,128)(2,1)} %w_gate.1) | copy-start | bytes 196612
  138.8 18.0 %copy-start.9 = (f32[128,128]{1,0:T(8,128)S(1)}, f32[128,128]{1,0:T(8,128)}, u32[]{:S(2)}) copy-start(f32[128,128]{1,0:T(8,128)} %get-tuple-element.16.scaled_t) | copy-start | bytes 196612
  140.6 16.1 %copy-start.2 = (bf16[128,512]{1,0:T(8,128)(2,1)S(1)}, bf16[128,512]{1,0:T(8,128)(2,1)}, u32[]{:S(2)}) copy-start(bf16[128,512]{1,0:T(8,128)(2,1)} %w_out.1) | copy-start | bytes 393220
  140.6 16.1 %copy-start.3 = (bf16[128,512]{1,0:T(8,128)(2,1)S(1)}, bf16[128,512]{1,0:T(8,128)(2,1)}, u32[]{:S(2)}) copy-start(bf16[128,512]{1,0:T(8,128)(2,1)} %w_in.1) | copy-start | bytes 393220
  156.7 0.7 copy-start.10
  156.7 0.7 copy-start.12

commit v4 on v3

v4 whole, which is shorter than its diff:
```python
import functools

import jax
import jax.numpy as jnp
from jax import lax
from jax.experimental import pallas as pl
from jax.experimental.pallas import tpu as pltpu
from jax.sharding import Mesh
from jax.sharding import PartitionSpec as P


PLANE = ("x", "y", "core")
DEPTH = ("zl", "zh")
EPSILON = 1e-05
BF = jnp.bfloat16
F32 = jnp.float32


def dot(a, b, dims=((1,), (0,))):
    return lax.dot_general(a, b, (dims, ((), ())), preferred_element_type=F32)


def norm(values):
    center = jnp.mean(values, axis=0, keepdims=True)
    shifted = values - center
    inverse = lax.rsqrt(jnp.mean(shifted * shifted, axis=0, keepdims=True) + EPSILON)
    return shifted * inverse, inverse


def norm_back(weighted, scaled, inverse):
    first = jnp.mean(weighted, axis=0, keepdims=True)
    second = jnp.mean(weighted * scaled, axis=0, keepdims=True)
    return inverse * (weighted - first - scaled * second)


def pair_order():
    here = lax.broadcasted_iota(jnp.int32, (128, 128), 0)
    there = lax.broadcasted_iota(jnp.int32, (128, 128), 1)
    same = (here >> 3 == (there & 15)) & ((here & 7) == there >> 4)
    return same.astype(F32).astype(BF)


def column(gain):
    return jnp.broadcast_to(gain, (128, 128)).T


def groups(values):
    return values.reshape(16, 8, 128).astype(BF)


def take(got, array):
    return got[:, 8 * array : 8 * array + 8].astype(F32).reshape(128, 128)


def fetch(pairs, arrived):
    copies = [
        pltpu.make_async_copy(there, here, arrived.at[n]) for n, (there, here) in enumerate(pairs)
    ]
    for copy in copies:
        copy.start()
    return copies


def first_kernel(*refs):
    far, (send, proj, gates, scaled_t), near = refs[:6], refs[6:10], refs[10:16]
    copies = fetch(list(zip(far, near)), refs[16])
    pair, gain, w_out, w_in, w_gate, update = near
    copies[0].wait()
    pair_t = dot(pair[...], pair_order(), ((0,), (0,)))
    scaled, inverse = norm(pair_t)
    copies[1].wait()
    normed = (scaled * column(gain[...])).astype(BF)
    scaled_t[0:128] = scaled
    scaled_t[128:129] = inverse
    scaled_t[129:130] = gain[...]
    for half, weights in enumerate((w_out, w_in)):
        copies[2 + half].wait()
        p = dot(weights[...], normed, ((0,), (0,)))
        proj[half] = p
        for side in range(2):
            part = 256 * side
            gated = jax.nn.sigmoid(p[part : part + 128]) * p[part + 128 : part + 256]
            row = 16 * half + 8 * side
            send[:, row : row + 8] = groups(gated)
    copies[4].wait()
    copies[5].wait()
    gates[0:256] = jax.nn.sigmoid(dot(w_gate[...], normed, ((0,), (0,))))
    gates[256:258] = update[...]


def swap_groups(rows):
    rows = list(rows)
    group = lax.broadcasted_iota(jnp.int32, rows[0].shape, 1) >> 4
    step = len(rows) // 2
    while step:
        low = (group & step) == 0
        for a in range(len(rows)):
            if a & step:
                continue
            x, y = rows[a], rows[a + step]
            rows[a] = jnp.where(low, x, pltpu.roll(y, 16 * step, 1))
            rows[a + step] = jnp.where(low, pltpu.roll(x, 128 - 16 * step, 1), y)
        step //= 2
    return rows


def spread_kernel(full, parts, got, send, held_full, held_parts):
    for high in range(2):
        rows = swap_groups(
            [got[4 * zl + 2 * high + low].astype(F32) for low in range(2) for zl in range(4)]
        )
        for q in range(8):
            held_full[:, 8 * high + q] = rows[q][8 * full : 8 * full + 8]
            pieces = swap_groups([rows[q][8 * a : 8 * a + 8] for a in parts])
            for mate in range(4):
                held_parts[:, mate, 8 * high + q] = pieces[mate]
    values = held_full[...].astype(BF)
    for mate in range(4):
        send[:, mate, 0:16] = values
    send[:, :, 16:32] = held_parts[...].astype(BF)


def collect_kernel(full, parts, got, send, held, held_parts, out):
    values = got[...].astype(F32)
    held[...] = values[:, 0, 0:16] + values[:, 1, 0:16] + values[:, 2, 0:16] + values[:, 3, 0:16]
    held_parts[...] = values[:, :, 16:32]
    for high in range(2):
        by_q = []
        for q in range(8):
            row = 8 * high + q
            pieces = swap_groups([held_parts[:, mate, row] for mate in range(4)])
            by_q.append({full: held[:, row], **dict(zip(parts, pieces))})
        for a in (full, *parts):
            for g, rows in enumerate(swap_groups([by_q[q][a] for q in range(8)])):
                zh = 2 * high + (g >> 2)
                out[4 * (g & 3) + zh, 8 * a : 8 * a + 8] = rows
    send[...] = out[...].astype(BF)


def swap_halves(first, second):
    low = lax.broadcasted_iota(jnp.int32, first.shape, 1) < 64
    return (
        jnp.where(low, first, pltpu.roll(second, 64, 1)),
        jnp.where(low, pltpu.roll(first, 64, 1), second),
    )


def reorder():
    p = lax.broadcasted_iota(jnp.int32, (256, 256), 0)
    q = lax.broadcasted_iota(jnp.int32, (256, 256), 1)
    residue = ((p >> 4) & 3) * 64 + (p >> 6) * 16 + (p & 15)
    return one_hot(residue, q_block(q) * 16 + ((q >> 4) & 1) * 8 + (q & 7))


def whole(got):
    tiles = [got[x, :, 0:16].astype(F32).reshape(128, 128) for x in range(4)]
    left = swap_halves(tiles[0], tiles[1])
    right = swap_halves(tiles[2], tiles[3])
    values = jnp.concatenate(
        [jnp.concatenate([left[low], right[low]], axis=1) for low in range(2)], axis=0
    )
    return dot(values.astype(BF), reorder()).astype(BF)


def quarters(got, amount):
    tiles = [got[x, :, 16:32].astype(F32).reshape(128, 128) for x in range(4)]
    turned = [values.T for values in swap_groups(tiles)[:amount]]
    return [jnp.concatenate([t[0:64], t[64:128]], axis=1).astype(BF) for t in turned]


def send_whole(send, values):
    values = dot(values.astype(BF), reorder(), NT)
    for half in range(2):
        lanes = slice(128 * half, 128 * half + 128)
        tiles = swap_halves(values[0:128, lanes], values[128:256, lanes])
        for n in range(2):
            send[2 * half + n, :, 0:16] = tiles[n].reshape(8, 16, 128).astype(BF)


def send_quarters(send, arrays):
    rows = []
    for pieces in arrays:
        values = jnp.concatenate(pieces, axis=0)
        rows.append(jnp.concatenate([values[:, 0:128], values[:, 128:256]], axis=0).T)
    while len(rows) < 4:
        rows.append(jnp.zeros((128, 128), F32))
    for x, tile in enumerate(swap_groups(rows)):
        send[x, :, 16:32] = tile.reshape(8, 16, 128).astype(BF)


NN = ((1,), (0,))
NT = ((1,), (1,))
TN = ((0,), (0,))


def one_hot(label, values):
    return (label == values).astype(F32).astype(BF)


def q_block(place):
    return ((place >> 5) & 3) * 4 + ((place >> 3) & 1) * 2 + (place >> 7)


def mask_tables():
    place = lax.broadcasted_iota(jnp.int32, (256, 16), 0)
    label = lax.broadcasted_iota(jnp.int32, (256, 16), 1)
    q_table = one_hot(label, q_block(place))
    place = lax.broadcasted_iota(jnp.int32, (256, 256), 0)
    label = lax.broadcasted_iota(jnp.int32, (256, 256), 1)
    j_table, i_table = one_hot(label & 15, q_block(place)), one_hot(label >> 4, q_block(place))
    return q_table, j_table, i_table


def mask_out(tables, contact, i):
    side = dot(tables[0], contact[i].astype(F32).astype(BF), NT).astype(BF)
    return dot(side, tables[0], NT)


def mask_in(tables, by_k, k):
    return dot(tables[1] * by_k[pl.ds(k, 1)].astype(BF), tables[2], NT)


def forward_kernel(spot, got, contact, flat, send, near, by_k, arrived):
    copies = fetch([(contact, near)], arrived)
    mate = spot[0]
    tables = mask_tables()
    by_k[...] = flat[...].astype(F32).T
    right_out = whole(got)
    left_out, left_in, right_in = quarters(got, 3)
    copies[0].wait()
    outs, ins = [], None
    for t in range(4):
        part = slice(16 * t, 16 * t + 16)
        mask = mask_out(tables, near, 4 * mate + t).astype(BF)
        outs.append(dot(left_out[part], right_out * mask, NN))
        mask = mask_in(tables, by_k, 4 * mate + t)
        term = dot(right_in[part], left_in[part], TN) * mask
        ins = term if ins is None else ins + term
    send_whole(send, ins)
    send_quarters(send, [outs])


def backward_kernel(spot, got, grads, contact, flat, send, near, by_k, arrived):
    copies = fetch([(contact, near)], arrived)
    mate = spot[0]
    tables = mask_tables()
    by_k[...] = flat[...].astype(F32).T
    right_out = whole(got)
    left_out, left_in, right_in = quarters(got, 3)
    grad_in = whole(grads)
    grad_out = quarters(grads, 1)[0]
    copies[0].wait()
    grad_left_out, grad_left_in, grad_right_in, grad_right_out = [], [], [], None
    for t in range(4):
        part = slice(16 * t, 16 * t + 16)
        mask = mask_out(tables, near, 4 * mate + t)
        grad_left_out.append(dot(grad_out[part], right_out * mask.astype(BF), NT))
        term = dot(left_out[part], grad_out[part], TN) * mask
        grad_right_out = term if grad_right_out is None else grad_right_out + term
        both = grad_in * mask_in(tables, by_k, 4 * mate + t).astype(BF)
        grad_left_in.append(dot(right_in[part], both, NN))
        grad_right_in.append(dot(left_in[part], both, NT))
    send_whole(send, grad_right_out)
    send_quarters(send, [grad_left_out, grad_left_in, grad_right_in])


def middle_kernel(pair, cotangent, got, gates, w_final, updated, send, grad_gate):
    order = pair_order()
    upstream = dot(cotangent[...], order, TN)
    total = dot(pair[...], order, TN)
    for t in range(2):
        scaled, inverse = norm(take(got, t))
        gain_t = column(gates[256 + t : 257 + t])
        normed = (scaled * gain_t).astype(BF)
        gate = gates[128 * t : 128 * t + 128]
        final = dot(w_final[t], normed, TN)
        total = total + gate * final
        grad_final = (upstream * gate).astype(BF)
        grad_gate[128 * t : 128 * t + 128] = (upstream * final * gate * (1.0 - gate)).astype(BF)
        weighted = dot(w_final[t], grad_final) * gain_t
        send[:, 8 * t : 8 * t + 8] = groups(norm_back(weighted, scaled, inverse))
    updated[...] = dot(order, total.astype(BF), NT).astype(BF)


def last_kernel(cotangent, got, proj, grad_gate, scaled_t, w_out, w_in, w_gate, grad_pair):
    order = pair_order()
    upstream = dot(cotangent[...], order, TN)
    grad_normed = dot(w_gate[...], grad_gate[...])
    for half, weights in enumerate((w_out, w_in)):
        p = proj[half]
        parts = []
        for side in range(2):
            grad = take(got, 2 * half + side)
            sig = jax.nn.sigmoid(p[256 * side : 256 * side + 128])
            parts.append(grad * p[256 * side + 128 : 256 * side + 256] * sig * (1.0 - sig))
            parts.append(grad * sig)
        grad_normed = grad_normed + dot(
            weights[...], jnp.concatenate(parts, axis=0).astype(BF)
        )
    weighted = grad_normed * column(scaled_t[129:130])
    back = norm_back(weighted, scaled_t[0:128], scaled_t[128:129])
    grad_pair[...] = dot(order, (upstream + back).astype(BF), NT).astype(BF)


def call(kernel, out, *args, scratch=(), spot=False, far=()):
    specs = [pl.BlockSpec(memory_space=pltpu.VMEM)] * len(args)
    for n in far:
        specs[n] = pl.BlockSpec(memory_space=pl.ANY)
    if spot:
        specs[0] = pl.BlockSpec(memory_space=pltpu.SMEM)
    multi = isinstance(out, list)
    shapes = [jax.ShapeDtypeStruct(s, d) for s, d in (out if multi else [out])]
    outs = [pl.BlockSpec(memory_space=pltpu.VMEM)] * len(shapes)
    buffers = [pltpu.VMEM(args[n].shape, args[n].dtype) for n in far]
    buffers += [pltpu.VMEM(s, F32) for s in scratch]
    if far:
        buffers.append(pltpu.SemaphoreType.DMA((len(far),)))
    params = pltpu.CompilerParams(vmem_limit_bytes=32 * 1024 * 1024)
    if len(far) == len(args):
        params = None
    result = pl.pallas_call(
        kernel,
        out_shape=shapes,
        in_specs=specs,
        out_specs=outs,
        scratch_shapes=buffers,
        compiler_params=params,
    )(*args)
    return result if multi else result[0]


def exchange(values, axis):
    return lax.all_to_all(values, axis, 0, 0, tiled=True)


def to_channels(send, full, parts):
    spread = call(
        functools.partial(spread_kernel, full, parts),
        ((8, 4, 32, 128), BF),
        exchange(send, DEPTH),
        scratch=[(8, 16, 128), (8, 4, 16, 128)],
    )
    return exchange(spread.reshape(32, 32, 128), PLANE).reshape(4, 8, 32, 128)


def to_pairs(send, full, parts):
    rows = 8 + 8 * len(parts)
    back = call(
        functools.partial(collect_kernel, full, parts),
        ((16, rows, 128), BF),
        exchange(send.reshape(32, 32, 128), PLANE).reshape(8, 4, 32, 128),
        scratch=[(8, 16, 128), (8, 4, 16, 128), (16, rows, 128)],
    )
    return exchange(back, DEPTH)


def my_mate():
    return lax.axis_index(PLANE) & 3


def on_device(
    pair_rep, cotangent, contact, norm_gain, w_out_proj, w_in_proj, update_gain, w_gate, w_final
):
    pair = pair_rep.reshape(128, 128)
    upstream = cotangent.reshape(128, 128)
    mate = my_mate().reshape(1)
    flat = contact.reshape(256, 16)

    send, proj, gates, scaled_t = call(
        first_kernel,
        [
            ((16, 32, 128), BF),
            ((2, 512, 128), F32),
            ((264, 128), F32),
            ((136, 128), F32),
        ],
        pair,
        norm_gain.reshape(1, 128),
        w_out_proj,
        w_in_proj,
        w_gate,
        update_gain,
        far=range(6),
    )
    sides = to_channels(send, 1, (0, 2, 3, 1))
    triangles = call(
        forward_kernel,
        ((4, 8, 32, 128), BF),
        mate,
        sides,
        contact,
        flat,
        scratch=[(16, 256)],
        spot=True,
        far=(2,),
    )
    updated, send, grad_gate = call(
        middle_kernel,
        [((128, 128), BF), ((16, 16, 128), BF), ((256, 128), BF)],
        pair,
        upstream,
        to_pairs(triangles, 1, (0,)),
        gates,
        w_final,
    )
    grads = call(
        backward_kernel,
        ((4, 8, 32, 128), BF),
        mate,
        sides,
        to_channels(send, 1, (0, 0, 0, 0)),
        contact,
        flat,
        scratch=[(16, 256)],
        spot=True,
        far=(3,),
    )
    grad_pair = call(
        last_kernel,
        ((128, 128), BF),
        upstream,
        to_pairs(grads, 1, (0, 2, 3)),
        proj,
        grad_gate,
        scaled_t,
        w_out_proj,
        w_in_proj,
        w_gate,
    )
    return (updated.reshape(pair_rep.shape), grad_pair.reshape(pair_rep.shape))


def solution(mesh):
    fine = Mesh(mesh.devices.reshape(4, 4, 4, 4, 2), ("zl", "x", "y", "zh", "core"))
    block = P(("zl", "x"), ("y", "zh", "core"), None)
    in_specs = (block, block, P(), P(), P(), P(), P(), P(), P())
    return jax.shard_map(
        on_device, mesh=fine, in_specs=in_specs, out_specs=(block, block), check_vma=False
    )
```

time: 160 us -> 149 us (0.931)
  waiting for transfers between devices: 15.2 us -> 8.98 us
  starting transfers between devices: 13.2 us -> 10.4 us
    all_to_all x1, waiting for transfers between devices: 15.2 us -> 8.98 us  [exchange(): return lax.all_to_all(values, axis, 0, 0, tiled=True)]
    all_to_all x1, starting transfers between devices: 13.2 us -> 10.4 us  [exchange(): return lax.all_to_all(values, axis, 0, 0, tiled=True)]
where the time goes in v4:
time: 149 us; the launch traced here: 147 us
  blocking collectives  114 us (77%)
  Pallas kernels  12.8 us (9%)
  starting transfers between devices  10.4 us (7%)
  waiting for transfers between devices  8.98 us (6%)
    all_to_all x7, blocking collectives, exchange(): return lax.all_to_all(values, axis, 0, 0, tiled=True)  114 us
    pallas_call x9, Pallas kernels, call(): pl.pallas_call(kernel, out_shape=shapes, in_specs=specs, out_specs=outs,...  12.8 us
    all_to_all x1, starting transfers between devices, exchange(): return lax.all_to_all(values, axis, 0, 0, tiled=True)  10.4 us
    all_to_all x1, waiting for transfers between devices, exchange(): return lax.all_to_all(values, axis, 0, 0, tiled=True)  8.98 us
  transfers between devices with their start and end apart: 1, of which 1 were waited for; matrix products, arithmetic and copies ran while one was open for 0% of the time, Pallas kernels for 0%

profile of v4, /device:TPU:1, one launch (start us, length us, event | category | flops | bytes accessed | tf_op | source)
XLA Modules:
  0.0 146.7 jit_solution(15640732228949873408)
XLA Ops:
  0.6 2.6 %shard_map.104 = (bf16[16,32,128]{2,1,0:T(8,128)(2,1)}, f32[2,512,128]{2,1,0:T(8,128)}, f32[264,128]{1,0:T(8,128)}, f32[136,128]{1,0:T(8,128)}) custom-call(bf16[128,128]{1,0:T(8,128)(2,1)} %bitcast.27, f32[1,128]{1,0:T(1,128)} %bitcast.30, bf16[128,512]{1,0:T(8,128)(2,1)} %w_out.1, bf16[128,512]{1,0:T(8,128)(2,1)} %w_in.1, bf16[128,256]{1,0:T(8,128)(2,1)} %w_gate.1, ...), custom_call_target="tpu_custom_call" | custom-call | tf_op jit(solution)/shard_map/pallas_call | solution.py:321
  3.2 28.1 %all_to_all.40.got = bf16[16,32,128]{2,1,0:T(8,128)(2,1)S(1)} all-to-all(bf16[16,32,128]{2,1,0:T(8,128)(2,1)} %get-tuple-element.9), channel_id=1, replica_groups=mesh['zl'=4,'x'=4,'y'=4,'zh'=4,'core'=2] {'zl','zh'}, dimensions={0} | all-to-all | bytes 262144 | tf_op jit(solution)/shard_map/all_to_all | solution.py:333
  31.3 1.4 shard_map.105
  32.7 0.0 copy-start
  32.7 10.4 %all-to-all-start.1 = ((bf16[32,32,128]{2,1,0:T(8,128)(2,1)}), bf16[32,32,128]{2,1,0:T(8,128)(2,1)S(1)}, u32[]{:S(2)}, u32[]{:S(2)}) async-start(bf16[32,32,128]{2,1,0:T(8,128)(2,1)} %bitcast.4), calls=%async_computation.1 | async-start | bytes 524288 | tf_op jit(solution)/shard_map/all_to_all | solution.py:333
  43.1 9.0 %all-to-all-done.1 = bf16[32,32,128]{2,1,0:T(8,128)(2,1)S(1)} async-done(((bf16[32,32,128]{2,1,0:T(8,128)(2,1)}), bf16[32,32,128]{2,1,0:T(8,128)(2,1)S(1)}, u32[]{:S(2)}, u32[]{:S(2)}) %all-to-all-start.1) | async-done | bytes 262176 | tf_op jit(solution)/shard_map/all_to_all | solution.py:333
  52.1 0.0 copy-done
  52.1 2.4 %shard_map.106 = bf16[4,8,32,128]{3,2,1,0:T(8,128)(2,1)S(1)} custom-call(s32[1]{0:T(128)} %bitcast.2.spot, bf16[4,8,32,128]{3,2,1,0:T(8,128)(2,1)S(1)} %bitcast.15, s32[16,16,16]{2,1,0:T(8,128)S(1)} %copy-done, s32[256,16]{1,0:T(8,128)S(1)} %bitcast.17), custom_call_target="tpu_custom_call" | custom-call | tf_op jit(solution)/shard_map/pallas_call | solution.py:321
  54.5 12.5 %all_to_all.41 = bf16[32,32,128]{2,1,0:T(8,128)(2,1)S(1)} all-to-all(bf16[32,32,128]{2,1,0:T(8,128)(2,1)S(1)} %bitcast.24), channel_id=1, replica_groups=mesh['zl'=4,'x'=4,'y'=4,'zh'=4,'core'=2] {'x','y','core'}, dimensions={0} | all-to-all | bytes 524288 | tf_op jit(solution)/shard_map/all_to_all | solution.py:333
  67.0 0.0 copy-start.5
  67.0 0.4 shard_map.107
  67.4 0.0 copy-start.6
  67.4 0.0 copy-start.7
  67.4 0.0 copy-start.9
  67.5 15.3 %all_to_all.42.got = bf16[16,16,128]{2,1,0:T(8,128)(2,1)S(1)} all-to-all(bf16[16,16,128]{2,1,0:T(8,128)(2,1)S(1)} %shard_map.107), channel_id=1, replica_groups=mesh['zl'=4,'x'=4,'y'=4,'zh'=4,'core'=2] {'zl','zh'}, dimensions={0} | all-to-all | bytes 131072 | tf_op jit(solution)/shard_map/all_to_all | solution.py:333
  82.8 0.0 copy-done.5
  82.8 0.0 copy-done.6
  82.8 0.0 copy-done.7
  82.8 0.0 copy-done.9
  82.8 1.0 shard_map.108
  83.8 15.1 %all_to_all.43.got = bf16[16,16,128]{2,1,0:T(8,128)(2,1)S(1)} all-to-all(bf16[16,16,128]{2,1,0:T(8,128)(2,1)S(1)} %get-tuple-element.12), channel_id=1, replica_groups=mesh['zl'=4,'x'=4,'y'=4,'zh'=4,'core'=2] {'zl','zh'}, dimensions={0} | all-to-all | bytes 131072 | tf_op jit(solution)/shard_map/all_to_all | solution.py:333
  98.9 0.6 shard_map.109
  99.5 14.9 %all_to_all.44 = bf16[32,32,128]{2,1,0:T(8,128)(2,1)S(1)} all-to-all(bf16[32,32,128]{2,1,0:T(8,128)(2,1)S(1)} %bitcast.20), channel_id=1, replica_groups=mesh['zl'=4,'x'=4,'y'=4,'zh'=4,'core'=2] {'x','y','core'}, dimensions={0} | all-to-all | bytes 524288 | tf_op jit(solution)/shard_map/all_to_all | solution.py:333
  114.4 2.7 %shard_map.110 = bf16[4,8,32,128]{3,2,1,0:T(8,128)(2,1)S(1)} custom-call(s32[1]{0:T(128)} %bitcast.2.spot, bf16[4,8,32,128]{3,2,1,0:T(8,128)(2,1)S(1)} %bitcast.16, bf16[4,8,32,128]{3,2,1,0:T(8,128)(2,1)S(1)} %bitcast.22, s32[16,16,16]{2,1,0:T(8,128)S(1)} %copy-done, s32[256,16]{1,0:T(8,128)S(1)} %bitcast.18), custom_call_target="tpu_custom_call" | custom-call | tf_op jit(solution)/shard_map/pallas_call | solution.py:321
  117.1 0.0 copy-start.3
  117.1 12.6 %all_to_all.45 = bf16[32,32,128]{2,1,0:T(8,128)(2,1)S(1)} all-to-all(bf16[32,32,128]{2,1,0:T(8,128)(2,1)S(1)} %bitcast.23), channel_id=1, replica_groups=mesh['zl'=4,'x'=4,'y'=4,'zh'=4,'core'=2] {'x','y','core'}, dimensions={0} | all-to-all | bytes 524288 | tf_op jit(solution)/shard_map/all_to_all | solution.py:333
  129.7 0.0 copy-start.4
  129.7 0.0 copy-start.8
  129.7 0.7 shard_map.111
  130.4 0.0 copy-start.1
  130.4 0.0 copy-start.2
  130.4 15.2 %all_to_all.46.got = bf16[16,32,128]{2,1,0:T(8,128)(2,1)S(1)} all-to-all(bf16[16,32,128]{2,1,0:T(8,128)(2,1)S(1)} %shard_map.111), channel_id=1, replica_groups=mesh['zl'=4,'x'=4,'y'=4,'zh'=4,'core'=2] {'zl','zh'}, dimensions={0} | all-to-all | bytes 262144 | tf_op jit(solution)/shard_map/all_to_all | solution.py:333
  145.6 0.0 copy-done.3
  145.6 0.0 copy-done.4
  145.6 0.0 copy-done.8
  145.6 0.0 copy-done.1
  145.6 0.0 copy-done.2
  145.6 1.1 shard_map.112
Async XLA Ops:
  32.7 19.4 %copy-start = (s32[16,16,16]{2,1,0:T(8,128)S(1)}, s32[16,16,16]{2,1,0:T(8,128)}, u32[]{:S(2)}) copy-start(s32[16,16,16]{2,1,0:T(8,128)} %contact.3) | copy-start | bytes 49156
  32.7 19.4 %all-to-all-start.1 = ((bf16[32,32,128]{2,1,0:T(8,128)(2,1)}), bf16[32,32,128]{2,1,0:T(8,128)(2,1)S(1)}, u32[]{:S(2)}, u32[]{:S(2)}) async-start(bf16[32,32,128]{2,1,0:T(8,128)(2,1)} %bitcast.4), calls=%async_computation.1 | async-start | bytes 524288 | tf_op jit(solution)/shard_map/all_to_all | solution.py:333
  67.0 15.8 %copy-start.5 = (f32[264,128]{1,0:T(8,128)S(1)}, f32[264,128]{1,0:T(8,128)}, u32[]{:S(2)}) copy-start(f32[264,128]{1,0:T(8,128)} %get-tuple-element.10.gates) | copy-start | bytes 405508
  67.4 15.4 %copy-start.6 = (bf16[16,8,128]{2,1,0:T(8,128)(2,1)S(1)}, bf16[16,8,128]{2,1,0:T(8,128)(2,1)}, u32[]{:S(2)}) copy-start(bf16[16,8,128]{2,1,0:T(8,128)(2,1)} %param.10) | copy-start | bytes 98308
  67.4 15.3 %copy-start.7 = (bf16[16,8,128]{2,1,0:T(8,128)(2,1)S(1)}, bf16[16,8,128]{2,1,0:T(8,128)(2,1)}, u32[]{:S(2)}) copy-start(bf16[16,8,128]{2,1,0:T(8,128)(2,1)} %param.9) | copy-start | bytes 98308
  67.4 15.3 %copy-start.9 = (bf16[2,128,128]{2,1,0:T(8,128)(2,1)S(1)}, bf16[2,128,128]{2,1,0:T(8,128)(2,1)}, u32[]{:S(2)}) copy-start(bf16[2,128,128]{2,1,0:T(8,128)(2,1)} %w_final.1) | copy-start | bytes 196612
  117.1 28.5 %copy-start.3 = (f32[2,512,128]{2,1,0:T(8,128)S(1)}, f32[2,512,128]{2,1,0:T(8,128)}, u32[]{:S(2)}) copy-start(f32[2,512,128]{2,1,0:T(8,128)} %get-tuple-element.13.proj) | copy-start | bytes 1572868
  129.7 15.9 %copy-start.4 = (bf16[128,256]{1,0:T(8,128)(2,1)S(1)}, bf16[128,256]{1,0:T(8,128)(2,1)}, u32[]{:S(2)}) copy-start(bf16[128,256]{1,0:T(8,128)(2,1)} %w_gate.1) | copy-start | bytes 196612
  129.7 15.9 %copy-start.8 = (f32[136,128]{1,0:T(8,128)S(1)}, f32[136,128]{1,0:T(8,128)}, u32[]{:S(2)}) copy-start(f32[136,128]{1,0:T(8,128)} %get-tuple-element.15.scaled_t) | copy-start | bytes 208900
  130.4 15.2 %copy-start.1 = (bf16[128,512]{1,0:T(8,128)(2,1)S(1)}, bf16[128,512]{1,0:T(8,128)(2,1)}, u32[]{:S(2)}) copy-start(bf16[128,512]{1,0:T(8,128)(2,1)} %w_out.1) | copy-start | bytes 393220
  130.4 15.2 %copy-start.2 = (bf16[128,512]{1,0:T(8,128)(2,1)S(1)}, bf16[128,512]{1,0:T(8,128)(2,1)}, u32[]{:S(2)}) copy-start(bf16[128,512]{1,0:T(8,128)(2,1)} %w_in.1) | copy-start | bytes 393220

commit v5 on v4

--- a/solution.py
+++ b/solution.py
@@ -62,8 +62,10 @@
 
 
 def first_kernel(*refs):
-    far, (send, proj, gates, scaled_t), near = refs[:6], refs[6:10], refs[10:16]
-    copies = fetch(list(zip(far, near)), refs[16])
+    spot, far, near = refs[0], refs[1:7], refs[12:18]
+    send, proj, gates, scaled_t, mate = refs[7:12]
+    copies = fetch(list(zip(far, near)), refs[18])
+    mate[0] = spot[0]
     pair, gain, w_out, w_in, w_gate, update = near
     copies[0].wait()
     pair_t = dot(pair[...], pair_order(), ((0,), (0,)))
@@ -159,7 +161,7 @@
     values = jnp.concatenate(
         [jnp.concatenate([left[low], right[low]], axis=1) for low in range(2)], axis=0
     )
-    return dot(values.astype(BF), reorder()).astype(BF)
+    return dot(values.astype(BF), reorder())
 
 
 def quarters(got, amount):
@@ -201,63 +203,67 @@
     return ((place >> 5) & 3) * 4 + ((place >> 3) & 1) * 2 + (place >> 7)
 
 
-def mask_tables():
+def masks(contact, flat, mate):
+    place = lax.broadcasted_iota(jnp.int32, (32, 16), 0) << 3
+    label = lax.broadcasted_iota(jnp.int32, (32, 16), 1)
+    short = one_hot(label, q_block(place))
     place = lax.broadcasted_iota(jnp.int32, (256, 16), 0)
     label = lax.broadcasted_iota(jnp.int32, (256, 16), 1)
-    q_table = one_hot(label, q_block(place))
+    table = one_hot(label, q_block(place))
+    place = lax.broadcasted_iota(jnp.int32, (32, 256), 0) << 3
+    label = lax.broadcasted_iota(jnp.int32, (32, 256), 1)
+    j_short = (label & 15 == q_block(place)).astype(F32)
     place = lax.broadcasted_iota(jnp.int32, (256, 256), 0)
     label = lax.broadcasted_iota(jnp.int32, (256, 256), 1)
-    j_table, i_table = one_hot(label & 15, q_block(place)), one_hot(label >> 4, q_block(place))
-    return q_table, j_table, i_table
-
-
-def mask_out(tables, contact, i):
-    side = dot(tables[0], contact[i].astype(F32).astype(BF), NT).astype(BF)
-    return dot(side, tables[0], NT)
-
-
-def mask_in(tables, by_k, k):
-    return dot(tables[1] * by_k[pl.ds(k, 1)].astype(BF), tables[2], NT)
-
-
-def forward_kernel(spot, got, contact, flat, send, near, by_k, arrived):
+    i_table = one_hot(label >> 4, q_block(place))
+    by_k = flat[...].astype(F32)
+    wanted = lax.broadcasted_iota(jnp.int32, (4, 16), 0) + 4 * mate
+    label = lax.broadcasted_iota(jnp.int32, (4, 16), 1)
+    by_k = dot(one_hot(label, wanted), by_k.astype(BF), NT)
+    for_out = [
+        dot(short, contact[4 * mate + t].astype(F32).astype(BF), NT).astype(BF) for t in range(4)
+    ]
+    for_in = [(j_short * by_k[t : t + 1]).astype(BF) for t in range(4)]
+    mask_out = dot(jnp.concatenate(for_out, axis=0), table, NT)
+    mask_in = dot(jnp.concatenate(for_in, axis=0), i_table, NT)
+    return mask_out.reshape(4, 32, 1, 256), mask_in.reshape(4, 32, 1, 256)
+
+
+def apply(mask, values):
+    return (values.reshape(32, 8, 256) * mask).reshape(256, 256)
+
+
+def forward_kernel(spot, got, contact, flat, send, near, arrived):
     copies = fetch([(contact, near)], arrived)
-    mate = spot[0]
-    tables = mask_tables()
-    by_k[...] = flat[...].astype(F32).T
     right_out = whole(got)
     left_out, left_in, right_in = quarters(got, 3)
     copies[0].wait()
+    mask_out, mask_in = masks(near, flat, spot[0])
     outs, ins = [], None
     for t in range(4):
         part = slice(16 * t, 16 * t + 16)
-        mask = mask_out(tables, near, 4 * mate + t).astype(BF)
-        outs.append(dot(left_out[part], right_out * mask, NN))
-        mask = mask_in(tables, by_k, 4 * mate + t)
-        term = dot(right_in[part], left_in[part], TN) * mask
+        outs.append(dot(left_out[part], apply(mask_out[t], right_out).astype(BF), NN))
+        term = apply(mask_in[t], dot(right_in[part], left_in[part], TN))
         ins = term if ins is None else ins + term
     send_whole(send, ins)
     send_quarters(send, [outs])
 
 
-def backward_kernel(spot, got, grads, contact, flat, send, near, by_k, arrived):
+def backward_kernel(spot, got, grads, contact, flat, send, near, arrived):
     copies = fetch([(contact, near)], arrived)
-    mate = spot[0]
-    tables = mask_tables()
-    by_k[...] = flat[...].astype(F32).T
     right_out = whole(got)
     left_out, left_in, right_in = quarters(got, 3)
     grad_in = whole(grads)
     grad_out = quarters(grads, 1)[0]
     copies[0].wait()
+    mask_out, mask_in = masks(near, flat, spot[0])
     grad_left_out, grad_left_in, grad_right_in, grad_right_out = [], [], [], None
     for t in range(4):
         part = slice(16 * t, 16 * t + 16)
-        mask = mask_out(tables, near, 4 * mate + t)
-        grad_left_out.append(dot(grad_out[part], right_out * mask.astype(BF), NT))
-        term = dot(left_out[part], grad_out[part], TN) * mask
+        grad_left_out.append(dot(grad_out[part], apply(mask_out[t], right_out).astype(BF), NT))
+        term = apply(mask_out[t], dot(left_out[part], grad_out[part], TN))
         grad_right_out = term if grad_right_out is None else grad_right_out + term
-        both = grad_in * mask_in(tables, by_k, 4 * mate + t).astype(BF)
+        both = apply(mask_in[t], grad_in).astype(BF)
         grad_left_in.append(dot(right_in[part], both, NN))
         grad_right_in.append(dot(left_in[part], both, NT))
     send_whole(send, grad_right_out)
@@ -305,19 +311,20 @@
 def call(kernel, out, *args, scratch=(), spot=False, far=()):
     specs = [pl.BlockSpec(memory_space=pltpu.VMEM)] * len(args)
     for n in far:
-        specs[n] = pl.BlockSpec(memory_space=pl.ANY)
+        specs[n] = pl.BlockSpec(memory_space=pltpu.HBM)
     if spot:
         specs[0] = pl.BlockSpec(memory_space=pltpu.SMEM)
     multi = isinstance(out, list)
     shapes = [jax.ShapeDtypeStruct(s, d) for s, d in (out if multi else [out])]
-    outs = [pl.BlockSpec(memory_space=pltpu.VMEM)] * len(shapes)
+    outs = [
+        pl.BlockSpec(memory_space=pltpu.SMEM if x.dtype == jnp.int32 else pltpu.VMEM)
+        for x in shapes
+    ]
     buffers = [pltpu.VMEM(args[n].shape, args[n].dtype) for n in far]
     buffers += [pltpu.VMEM(s, F32) for s in scratch]
     if far:
         buffers.append(pltpu.SemaphoreType.DMA((len(far),)))
     params = pltpu.CompilerParams(vmem_limit_bytes=32 * 1024 * 1024)
-    if len(far) == len(args):
-        params = None
     result = pl.pallas_call(
         kernel,
         out_shape=shapes,
@@ -363,24 +370,26 @@
 ):
     pair = pair_rep.reshape(128, 128)
     upstream = cotangent.reshape(128, 128)
-    mate = my_mate().reshape(1)
     flat = contact.reshape(256, 16)
 
-    send, proj, gates, scaled_t = call(
+    send, proj, gates, scaled_t, mate = call(
         first_kernel,
         [
             ((16, 32, 128), BF),
             ((2, 512, 128), F32),
             ((264, 128), F32),
             ((136, 128), F32),
+            ((1,), jnp.int32),
         ],
+        my_mate().reshape(1),
         pair,
         norm_gain.reshape(1, 128),
         w_out_proj,
         w_in_proj,
         w_gate,
         update_gain,
-        far=range(6),
+        spot=True,
+        far=range(1, 7),
     )
     sides = to_channels(send, 1, (0, 2, 3, 1))
     triangles = call(
@@ -390,7 +399,6 @@
         sides,
         contact,
         flat,
-        scratch=[(16, 256)],
         spot=True,
         far=(2,),
     )
@@ -411,7 +419,6 @@
         to_channels(send, 1, (0, 0, 0, 0)),
         contact,
         flat,
-        scratch=[(16, 256)],
         spot=True,
         far=(3,),
     )

time: 149 us -> 151 us (1.013)
  blocking collectives: 114 us -> 133 us
  starting transfers between devices: 10.4 us -> 0 us
  waiting for transfers between devices: 8.98 us -> 0 us
  local copies, waits for them, and re-layouts: 0.05 us -> 4.76 us
  Pallas kernels: 12.8 us -> 10.7 us
    all_to_all x7 -> x8, blocking collectives: 114 us -> 133 us  [exchange(): return lax.all_to_all(values, axis, 0, 0, tiled=True)]
    all_to_all x1 -> x0, starting transfers between devices: 10.4 us -> none  [exchange(): return lax.all_to_all(values, axis, 0, 0, tiled=True)]
    all_to_all x1 -> x0, waiting for transfers between devices: 8.98 us -> none  [exchange(): return lax.all_to_all(values, axis, 0, 0, tiled=True)]
    unnamed x20 -> x24, local copies, waits for them, and re-layouts: 0.05 us -> 4.76 us
    pallas_call x9, Pallas kernels: 12.8 us -> 10.7 us  [call(): pl.pallas_call(kernel, out_shape=shapes, in_specs=specs, out_specs=outs,...]
  transfers between devices with their start and end apart: 1 -> 0, of which waited for: 1 -> 0; matrix products, arithmetic and copies ran while one was open for 0% -> 0% of each run, Pallas kernels for 0% -> 0%
where the time goes in v5:
time: 151 us; the launch traced here: 149 us
  blocking collectives  133 us (88%)
  Pallas kernels  10.7 us (7%)
  local copies, waits for them, and re-layouts  4.76 us (3%)
    all_to_all x8, blocking collectives, exchange(): return lax.all_to_all(values, axis, 0, 0, tiled=True)  133 us
    pallas_call x9, Pallas kernels, call(): pl.pallas_call(kernel, out_shape=shapes, in_specs=specs, out_specs=outs,...  10.7 us
    unnamed x24, local copies, waits for them, and re-layouts  4.76 us

profile of v5, /device:TPU:1, one launch (start us, length us, event | category | flops | bytes accessed | tf_op | source)
XLA Modules:
  0.0 148.7 jit_solution(8345972211500177482)
XLA Ops:
  0.6 0.0 copy-start.8
  0.6 0.7 copy-done.8
  1.4 0.0 copy-start.1
  1.4 0.9 copy-done.1
  2.3 0.0 copy-start.3
  2.3 0.9 copy-done.3
  3.2 0.0 copy-start.5
  3.2 0.8 copy-done.5
  4.0 0.0 copy-start.10
  4.0 0.7 copy-done.10
  4.7 0.0 copy-start.11
  4.7 0.7 copy-done.11
  5.4 1.8 %shard_map.104 = (bf16[16,32,128]{2,1,0:T(8,128)(2,1)S(1)}, f32[2,512,128]{2,1,0:T(8,128)S(1)}, f32[264,128]{1,0:T(8,128)S(1)}, f32[136,128]{1,0:T(8,128)S(1)}, s32[1]{0:T(128)}) custom-call(s32[1]{0:T(128)} %bitcast.2.refs_0_, bf16[128,128]{1,0:T(8,128)(2,1)S(1)} %bitcast.28, f32[1,128]{1,0:T(1,128)S(1)} %bitcast.30, bf16[128,512]{1,0:T(8,128)(2,1)S(1)} %copy-done.1, ...), custom_call_target="tpu_custom_call" | custom-call | tf_op jit(solution)/shard_map/pallas_call | solution.py:328
  7.2 27.9 %all_to_all.40.got = bf16[16,32,128]{2,1,0:T(8,128)(2,1)S(1)} all-to-all(bf16[16,32,128]{2,1,0:T(8,128)(2,1)S(1)} %get-tuple-element.11), channel_id=1, replica_groups=mesh['zl'=4,'x'=4,'y'=4,'zh'=4,'core'=2] {'zl','zh'}, dimensions={0} | all-to-all | bytes 262144 | tf_op jit(solution)/shard_map/all_to_all | solution.py:340
  35.1 0.7 shard_map.105
  35.8 0.0 copy-start
  35.9 19.2 %all_to_all.41 = bf16[32,32,128]{2,1,0:T(8,128)(2,1)S(1)} all-to-all(bf16[32,32,128]{2,1,0:T(8,128)(2,1)S(1)} %bitcast.21), channel_id=1, replica_groups=mesh['zl'=4,'x'=4,'y'=4,'zh'=4,'core'=2] {'x','y','core'}, dimensions={0} | all-to-all | bytes 524288 | tf_op jit(solution)/shard_map/all_to_all | solution.py:340
  55.0 0.0 copy-done
  55.0 1.9 %shard_map.106 = bf16[4,8,32,128]{3,2,1,0:T(8,128)(2,1)S(1)} custom-call(s32[1]{0:T(128)} %get-tuple-element.10.spot, bf16[4,8,32,128]{3,2,1,0:T(8,128)(2,1)S(1)} %bitcast.15, s32[16,16,16]{2,1,0:T(8,128)S(1)} %copy-done, s32[256,16]{1,0:T(8,128)S(1)} %bitcast.17), custom_call_target="tpu_custom_call" | custom-call | tf_op jit(solution)/shard_map/pallas_call | solution.py:328
  57.0 12.5 %all_to_all.42 = bf16[32,32,128]{2,1,0:T(8,128)(2,1)S(1)} all-to-all(bf16[32,32,128]{2,1,0:T(8,128)(2,1)S(1)} %bitcast.25), channel_id=1, replica_groups=mesh['zl'=4,'x'=4,'y'=4,'zh'=4,'core'=2] {'x','y','core'}, dimensions={0} | all-to-all | bytes 524288 | tf_op jit(solution)/shard_map/all_to_all | solution.py:340
  69.4 0.4 shard_map.107
  69.9 0.0 copy-start.7
  69.9 0.0 copy-start.9
  69.9 15.3 %all_to_all.43.got = bf16[16,16,128]{2,1,0:T(8,128)(2,1)S(1)} all-to-all(bf16[16,16,128]{2,1,0:T(8,128)(2,1)S(1)} %shard_map.107), channel_id=1, replica_groups=mesh['zl'=4,'x'=4,'y'=4,'zh'=4,'core'=2] {'zl','zh'}, dimensions={0} | all-to-all | bytes 131072 | tf_op jit(solution)/shard_map/all_to_all | solution.py:340
  85.2 0.0 copy-done.7
  85.2 0.0 copy-done.9
  85.2 1.0 shard_map.108
  86.3 15.1 %all_to_all.44.got = bf16[16,16,128]{2,1,0:T(8,128)(2,1)S(1)} all-to-all(bf16[16,16,128]{2,1,0:T(8,128)(2,1)S(1)} %get-tuple-element.14), channel_id=1, replica_groups=mesh['zl'=4,'x'=4,'y'=4,'zh'=4,'core'=2] {'zl','zh'}, dimensions={0} | all-to-all | bytes 131072 | tf_op jit(solution)/shard_map/all_to_all | solution.py:340
  101.3 0.6 shard_map.109
  102.0 14.9 %all_to_all.45 = bf16[32,32,128]{2,1,0:T(8,128)(2,1)S(1)} all-to-all(bf16[32,32,128]{2,1,0:T(8,128)(2,1)S(1)} %bitcast.20), channel_id=1, replica_groups=mesh['zl'=4,'x'=4,'y'=4,'zh'=4,'core'=2] {'x','y','core'}, dimensions={0} | all-to-all | bytes 524288 | tf_op jit(solution)/shard_map/all_to_all | solution.py:340
  116.9 2.4 %shard_map.110 = bf16[4,8,32,128]{3,2,1,0:T(8,128)(2,1)S(1)} custom-call(s32[1]{0:T(128)} %get-tuple-element.10.spot, bf16[4,8,32,128]{3,2,1,0:T(8,128)(2,1)S(1)} %bitcast.16, bf16[4,8,32,128]{3,2,1,0:T(8,128)(2,1)S(1)} %bitcast.23, s32[16,16,16]{2,1,0:T(8,128)S(1)} %copy-done, s32[256,16]{1,0:T(8,128)S(1)} %bitcast.18), custom_call_target="tpu_custom_call" | custom-call | tf_op jit(solution)/shard_map/pallas_call | solution.py:328
  119.2 12.5 %all_to_all.46 = bf16[32,32,128]{2,1,0:T(8,128)(2,1)S(1)} all-to-all(bf16[32,32,128]{2,1,0:T(8,128)(2,1)S(1)} %bitcast.24), channel_id=1, replica_groups=mesh['zl'=4,'x'=4,'y'=4,'zh'=4,'core'=2] {'x','y','core'}, dimensions={0} | all-to-all | bytes 524288 | tf_op jit(solution)/shard_map/all_to_all | solution.py:340
  131.7 0.0 copy-start.6
  131.7 0.7 shard_map.111
  132.4 0.0 copy-start.2
  132.4 0.0 copy-start.4
  132.4 15.2 %all_to_all.47.got = bf16[16,32,128]{2,1,0:T(8,128)(2,1)S(1)} all-to-all(bf16[16,32,128]{2,1,0:T(8,128)(2,1)S(1)} %shard_map.111), channel_id=1, replica_groups=mesh['zl'=4,'x'=4,'y'=4,'zh'=4,'core'=2] {'zl','zh'}, dimensions={0} | all-to-all | bytes 262144 | tf_op jit(solution)/shard_map/all_to_all | solution.py:340
  147.6 0.0 copy-done.6
  147.6 0.0 copy-done.2
  147.6 0.0 copy-done.4
  147.6 1.1 shard_map.112
Async XLA Ops:
  0.6 0.8 copy-start.8
  1.4 0.9 copy-start.1
  2.3 0.9 copy-start.3
  3.2 0.8 copy-start.5
  4.0 0.7 copy-start.10
  4.7 0.7 copy-start.11
  35.8 19.2 %copy-start = (s32[16,16,16]{2,1,0:T(8,128)S(1)}, s32[16,16,16]{2,1,0:T(8,128)}, u32[]{:S(2)}) copy-start(s32[16,16,16]{2,1,0:T(8,128)} %contact.3) | copy-start | bytes 49156
  69.9 15.3 %copy-start.7 = (bf16[16,8,128]{2,1,0:T(8,128)(2,1)S(1)}, bf16[16,8,128]{2,1,0:T(8,128)(2,1)}, u32[]{:S(2)}) copy-start(bf16[16,8,128]{2,1,0:T(8,128)(2,1)} %param.10) | copy-start | bytes 98308
  69.9 15.3 %copy-start.9 = (bf16[2,128,128]{2,1,0:T(8,128)(2,1)S(1)}, bf16[2,128,128]{2,1,0:T(8,128)(2,1)}, u32[]{:S(2)}) copy-start(bf16[2,128,128]{2,1,0:T(8,128)(2,1)} %w_final.1) | copy-start | bytes 196612
  131.7 15.9 %copy-start.6 = (bf16[128,256]{1,0:T(8,128)(2,1)S(1)}, bf16[128,256]{1,0:T(8,128)(2,1)}, u32[]{:S(2)}) copy-start(bf16[128,256]{1,0:T(8,128)(2,1)} %w_gate.1) | copy-start | bytes 196612
  132.4 15.2 %copy-start.2 = (bf16[128,512]{1,0:T(8,128)(2,1)S(1)}, bf16[128,512]{1,0:T(8,128)(2,1)}, u32[]{:S(2)}) copy-start(bf16[128,512]{1,0:T(8,128)(2,1)} %w_out.1) | copy-start | bytes 393220
  132.4 15.2 %copy-start.4 = (bf16[128,512]{1,0:T(8,128)(2,1)S(1)}, bf16[128,512]{1,0:T(8,128)(2,1)}, u32[]{:S(2)}) copy-start(bf16[128,512]{1,0:T(8,128)(2,1)} %w_in.1) | copy-start | bytes 393220

commit v6 on v5

--- a/solution.py
+++ b/solution.py
@@ -107,35 +107,43 @@
 
 
 def spread_kernel(full, parts, got, send, held_full, held_parts):
+    pieces = []
     for high in range(2):
         rows = swap_groups(
             [got[4 * zl + 2 * high + low].astype(F32) for low in range(2) for zl in range(4)]
         )
         for q in range(8):
             held_full[:, 8 * high + q] = rows[q][8 * full : 8 * full + 8]
-            pieces = swap_groups([rows[q][8 * a : 8 * a + 8] for a in parts])
-            for mate in range(4):
-                held_parts[:, mate, 8 * high + q] = pieces[mate]
+            pieces.append([rows[q][8 * a : 8 * a + 8] for a in parts])
+    if len(parts) == 1:
+        pieces = [pieces[q] + pieces[8 + q] for q in range(8)]
+    for row, arrays in enumerate(pieces):
+        for mate, values in enumerate(swap_groups(arrays + arrays[: 4 - len(arrays)])):
+            held_parts[:, mate, row] = values
     values = held_full[...].astype(BF)
     for mate in range(4):
         send[:, mate, 0:16] = values
-    send[:, :, 16:32] = held_parts[...].astype(BF)
+    send[:, :, 16:] = held_parts[...].astype(BF)
 
 
 def collect_kernel(full, parts, got, send, held, held_parts, out):
     values = got[...].astype(F32)
     held[...] = values[:, 0, 0:16] + values[:, 1, 0:16] + values[:, 2, 0:16] + values[:, 3, 0:16]
-    held_parts[...] = values[:, :, 16:32]
+    held_parts[...] = values[:, :, 16:]
+    pieces = [
+        swap_groups([held_parts[:, mate, row] for mate in range(4)])
+        for row in range(got.shape[2] - 16)
+    ]
+    if len(parts) == 1:
+        pieces = [[values[high]] for high in range(2) for values in pieces]
     for high in range(2):
-        by_q = []
-        for q in range(8):
-            row = 8 * high + q
-            pieces = swap_groups([held_parts[:, mate, row] for mate in range(4)])
-            by_q.append({full: held[:, row], **dict(zip(parts, pieces))})
-        for a in (full, *parts):
-            for g, rows in enumerate(swap_groups([by_q[q][a] for q in range(8)])):
+        arrays = {full: [held[:, 8 * high + q] for q in range(8)]}
+        for n, a in enumerate(parts):
+            arrays[a] = [pieces[8 * high + q][n] for q in range(8)]
+        for a, rows in arrays.items():
+            for g, values in enumerate(swap_groups(rows)):
                 zh = 2 * high + (g >> 2)
-                out[4 * (g & 3) + zh, 8 * a : 8 * a + 8] = rows
+                out[4 * (g & 3) + zh, 8 * a : 8 * a + 8] = values
     send[...] = out[...].astype(BF)
 
 
@@ -147,31 +155,40 @@
     )
 
 
-def reorder():
-    p = lax.broadcasted_iota(jnp.int32, (256, 256), 0)
-    q = lax.broadcasted_iota(jnp.int32, (256, 256), 1)
-    residue = ((p >> 4) & 3) * 64 + (p >> 6) * 16 + (p & 15)
+def p_block(place):
+    return ((place >> 4) & 3) * 4 + (place >> 6)
+
+
+def reorder(turned=False):
+    p = lax.broadcasted_iota(jnp.int32, (256, 256), 1 if turned else 0)
+    q = lax.broadcasted_iota(jnp.int32, (256, 256), 0 if turned else 1)
+    residue = p_block(p) * 16 + (p & 15)
     return one_hot(residue, q_block(q) * 16 + ((q >> 4) & 1) * 8 + (q & 7))
 
 
-def whole(got):
+def whole(got, order):
     tiles = [got[x, :, 0:16].astype(F32).reshape(128, 128) for x in range(4)]
     left = swap_halves(tiles[0], tiles[1])
     right = swap_halves(tiles[2], tiles[3])
     values = jnp.concatenate(
         [jnp.concatenate([left[low], right[low]], axis=1) for low in range(2)], axis=0
     )
-    return dot(values.astype(BF), reorder())
-
-
-def quarters(got, amount):
-    tiles = [got[x, :, 16:32].astype(F32).reshape(128, 128) for x in range(4)]
-    turned = [values.T for values in swap_groups(tiles)[:amount]]
+    return dot(values.astype(BF), order)
+
+
+def quarters(got):
+    rows = got.shape[2] - 16
+    tiles = [got[x, :, 16:].astype(F32).reshape(8 * rows, 128) for x in range(4)]
+    arrays = swap_groups(tiles)
+    if rows == 8:
+        highs = [values.reshape(8, 1, 8, 128) for values in arrays[:2]]
+        arrays = [jnp.concatenate(highs, axis=1).reshape(128, 128)]
+    turned = [values.T for values in arrays[:3]]
     return [jnp.concatenate([t[0:64], t[64:128]], axis=1).astype(BF) for t in turned]
 
 
-def send_whole(send, values):
-    values = dot(values.astype(BF), reorder(), NT)
+def send_whole(send, values, back):
+    values = dot(values.astype(BF), back)
     for half in range(2):
         lanes = slice(128 * half, 128 * half + 128)
         tiles = swap_halves(values[0:128, lanes], values[128:256, lanes])
@@ -180,14 +197,15 @@
 
 
 def send_quarters(send, arrays):
-    rows = []
-    for pieces in arrays:
-        values = jnp.concatenate(pieces, axis=0)
-        rows.append(jnp.concatenate([values[:, 0:128], values[:, 128:256]], axis=0).T)
-    while len(rows) < 4:
-        rows.append(jnp.zeros((128, 128), F32))
+    rows = [
+        jnp.concatenate([values[:, 0:128], values[:, 128:256]], axis=0).T for values in arrays
+    ]
+    if len(rows) == 1:
+        highs = rows[0].reshape(8, 2, 8, 128)
+        rows = [highs[:, n].reshape(64, 128) for n in range(2)]
+    rows += rows[: 4 - len(rows)]
     for x, tile in enumerate(swap_groups(rows)):
-        send[x, :, 16:32] = tile.reshape(8, 16, 128).astype(BF)
+        send[x, :, 16:] = tile.reshape(8, send.shape[2] - 16, 128).astype(BF)
 
 
 NN = ((1,), (0,))
@@ -233,10 +251,15 @@
     return (values.reshape(32, 8, 256) * mask).reshape(256, 256)
 
 
+def join(pieces):
+    return jnp.concatenate(pieces, axis=0)
+
+
 def forward_kernel(spot, got, contact, flat, send, near, arrived):
     copies = fetch([(contact, near)], arrived)
-    right_out = whole(got)
-    left_out, left_in, right_in = quarters(got, 3)
+    order, back = reorder(), reorder(True)
+    left_out, left_in, right_in = quarters(got)
+    right_out = whole(got, order)
     copies[0].wait()
     mask_out, mask_in = masks(near, flat, spot[0])
     outs, ins = [], None
@@ -245,16 +268,17 @@
         outs.append(dot(left_out[part], apply(mask_out[t], right_out).astype(BF), NN))
         term = apply(mask_in[t], dot(right_in[part], left_in[part], TN))
         ins = term if ins is None else ins + term
-    send_whole(send, ins)
-    send_quarters(send, [outs])
+    send_whole(send, ins, back)
+    send_quarters(send, [join(outs)])
 
 
 def backward_kernel(spot, got, grads, contact, flat, send, near, arrived):
     copies = fetch([(contact, near)], arrived)
-    right_out = whole(got)
-    left_out, left_in, right_in = quarters(got, 3)
-    grad_in = whole(grads)
-    grad_out = quarters(grads, 1)[0]
+    order, back = reorder(), reorder(True)
+    left_out, left_in, right_in = quarters(got)
+    grad_out = quarters(grads)[0]
+    right_out = whole(got, order)
+    grad_in = whole(grads, order)
     copies[0].wait()
     mask_out, mask_in = masks(near, flat, spot[0])
     grad_left_out, grad_left_in, grad_right_in, grad_right_out = [], [], [], None
@@ -266,8 +290,8 @@
         both = apply(mask_in[t], grad_in).astype(BF)
         grad_left_in.append(dot(right_in[part], both, NN))
         grad_right_in.append(dot(left_in[part], both, NT))
-    send_whole(send, grad_right_out)
-    send_quarters(send, [grad_left_out, grad_left_in, grad_right_in])
+    send_whole(send, grad_right_out, back)
+    send_quarters(send, [join(grad_left_out), join(grad_left_in), join(grad_right_in)])
 
 
 def middle_kernel(pair, cotangent, got, gates, w_final, updated, send, grad_gate):
@@ -325,6 +349,8 @@
     if far:
         buffers.append(pltpu.SemaphoreType.DMA((len(far),)))
     params = pltpu.CompilerParams(vmem_limit_bytes=32 * 1024 * 1024)
+    if len(far) > 1:
+        params = None
     result = pl.pallas_call(
         kernel,
         out_shape=shapes,
@@ -341,22 +367,24 @@
 
 
 def to_channels(send, full, parts):
+    rows = 24 if len(parts) == 1 else 32
     spread = call(
         functools.partial(spread_kernel, full, parts),
-        ((8, 4, 32, 128), BF),
+        ((8, 4, rows, 128), BF),
         exchange(send, DEPTH),
-        scratch=[(8, 16, 128), (8, 4, 16, 128)],
-    )
-    return exchange(spread.reshape(32, 32, 128), PLANE).reshape(4, 8, 32, 128)
+        scratch=[(8, 16, 128), (8, 4, rows - 16, 128)],
+    )
+    return exchange(spread.reshape(32, rows, 128), PLANE).reshape(4, 8, rows, 128)
 
 
 def to_pairs(send, full, parts):
-    rows = 8 + 8 * len(parts)
+    rows = send.shape[2]
+    amount = 8 + 8 * len(parts)
     back = call(
         functools.partial(collect_kernel, full, parts),
-        ((16, rows, 128), BF),
-        exchange(send.reshape(32, 32, 128), PLANE).reshape(8, 4, 32, 128),
-        scratch=[(8, 16, 128), (8, 4, 16, 128), (16, rows, 128)],
+        ((16, amount, 128), BF),
+        exchange(send.reshape(32, rows, 128), PLANE).reshape(8, 4, rows, 128),
+        scratch=[(8, 16, 128), (8, 4, rows - 16, 128), (16, amount, 128)],
     )
     return exchange(back, DEPTH)
 
@@ -391,10 +419,10 @@
         spot=True,
         far=range(1, 7),
     )
-    sides = to_channels(send, 1, (0, 2, 3, 1))
+    sides = to_channels(send, 1, (0, 2, 3))
     triangles = call(
         forward_kernel,
-        ((4, 8, 32, 128), BF),
+        ((4, 8, 24, 128), BF),
         mate,
         sides,
         contact,
@@ -416,7 +444,7 @@
         ((4, 8, 32, 128), BF),
         mate,
         sides,
-        to_channels(send, 1, (0, 0, 0, 0)),
+        to_channels(send, 1, (0,)),
         contact,
         flat,
         spot=True,

time: 151 us -> 145 us (0.960)
  local copies, waits for them, and re-layouts: 4.76 us -> 0.05 us
  blocking collectives: 133 us -> 131 us
    unnamed x24 -> x20, local copies, waits for them, and re-layouts: 4.76 us -> 0.05 us
where the time goes in v6:
time: 145 us; the launch traced here: 144 us
  blocking collectives  131 us (90%)
  Pallas kernels  11.2 us (8%)
    all_to_all x8, blocking collectives, exchange(): return lax.all_to_all(values, axis, 0, 0, tiled=True)  131 us
    pallas_call x9, Pallas kernels, call(): pl.pallas_call(kernel, out_shape=shapes, in_specs=specs, out_specs=outs,...  11.2 us

profile of v6, /device:TPU:1, one launch (start us, length us, event | category | flops | bytes accessed | tf_op | source)
XLA Modules:
  0.0 143.5 jit_solution(3521284981917199232)
XLA Ops:
  0.6 2.6 %shard_map.104 = (bf16[16,32,128]{2,1,0:T(8,128)(2,1)}, f32[2,512,128]{2,1,0:T(8,128)}, f32[264,128]{1,0:T(8,128)}, f32[136,128]{1,0:T(8,128)}, s32[1]{0:T(128)}) custom-call(s32[1]{0:T(128)} %bitcast.2.refs_0_, bf16[128,128]{1,0:T(8,128)(2,1)} %bitcast.28, f32[1,128]{1,0:T(1,128)} %bitcast.31, bf16[128,512]{1,0:T(8,128)(2,1)} %w_out.1, ...), custom_call_target="tpu_custom_call" | custom-call | tf_op jit(solution)/shard_map/pallas_call | solution.py:354
  3.2 28.1 %all_to_all.40.got = bf16[16,32,128]{2,1,0:T(8,128)(2,1)S(1)} all-to-all(bf16[16,32,128]{2,1,0:T(8,128)(2,1)} %get-tuple-element.11), channel_id=1, replica_groups=mesh['zl'=4,'x'=4,'y'=4,'zh'=4,'core'=2] {'zl','zh'}, dimensions={0} | all-to-all | bytes 262144 | tf_op jit(solution)/shard_map/all_to_all | solution.py:366
  31.3 0.6 shard_map.105
  31.9 0.0 copy-start
  32.0 19.2 %all_to_all.41 = bf16[32,32,128]{2,1,0:T(8,128)(2,1)S(1)} all-to-all(bf16[32,32,128]{2,1,0:T(8,128)(2,1)S(1)} %bitcast.20), channel_id=1, replica_groups=mesh['zl'=4,'x'=4,'y'=4,'zh'=4,'core'=2] {'x','y','core'}, dimensions={0} | all-to-all | bytes 524288 | tf_op jit(solution)/shard_map/all_to_all | solution.py:366
  51.1 0.0 copy-done
  51.1 2.0 %shard_map.106 = bf16[4,8,24,128]{3,2,1,0:T(8,128)(2,1)S(1)} custom-call(s32[1]{0:T(128)} %get-tuple-element.10.spot, bf16[4,8,32,128]{3,2,1,0:T(8,128)(2,1)S(1)} %bitcast.15, s32[16,16,16]{2,1,0:T(8,128)S(1)} %copy-done, s32[256,16]{1,0:T(8,128)S(1)} %bitcast.17), custom_call_target="tpu_custom_call" | custom-call | tf_op jit(solution)/shard_map/pallas_call | solution.py:354
  53.2 11.8 %all_to_all.42 = bf16[32,24,128]{2,1,0:T(8,128)(2,1)S(1)} all-to-all(bf16[32,24,128]{2,1,0:T(8,128)(2,1)S(1)} %bitcast.25), channel_id=1, replica_groups=mesh['zl'=4,'x'=4,'y'=4,'zh'=4,'core'=2] {'x','y','core'}, dimensions={0} | all-to-all | bytes 393216 | tf_op jit(solution)/shard_map/all_to_all | solution.py:366
  65.0 0.0 copy-start.5
  65.0 0.4 shard_map.107
  65.4 0.0 copy-start.6
  65.4 0.0 copy-start.7
  65.4 0.0 copy-start.9
  65.4 15.3 %all_to_all.43.got = bf16[16,16,128]{2,1,0:T(8,128)(2,1)S(1)} all-to-all(bf16[16,16,128]{2,1,0:T(8,128)(2,1)S(1)} %shard_map.107), channel_id=1, replica_groups=mesh['zl'=4,'x'=4,'y'=4,'zh'=4,'core'=2] {'zl','zh'}, dimensions={0} | all-to-all | bytes 131072 | tf_op jit(solution)/shard_map/all_to_all | solution.py:366
  80.7 0.0 copy-done.5
  80.7 0.0 copy-done.6
  80.7 0.0 copy-done.7
  80.7 0.0 copy-done.9
  80.7 1.0 shard_map.108
  81.8 15.2 %all_to_all.44.got = bf16[16,16,128]{2,1,0:T(8,128)(2,1)S(1)} all-to-all(bf16[16,16,128]{2,1,0:T(8,128)(2,1)S(1)} %get-tuple-element.14), channel_id=1, replica_groups=mesh['zl'=4,'x'=4,'y'=4,'zh'=4,'core'=2] {'zl','zh'}, dimensions={0} | all-to-all | bytes 131072 | tf_op jit(solution)/shard_map/all_to_all | solution.py:366
  96.9 0.5 shard_map.109
  97.5 14.1 %all_to_all.45 = bf16[32,24,128]{2,1,0:T(8,128)(2,1)S(1)} all-to-all(bf16[32,24,128]{2,1,0:T(8,128)(2,1)S(1)} %bitcast.24), channel_id=1, replica_groups=mesh['zl'=4,'x'=4,'y'=4,'zh'=4,'core'=2] {'x','y','core'}, dimensions={0} | all-to-all | bytes 393216 | tf_op jit(solution)/shard_map/all_to_all | solution.py:366
  111.6 2.4 %shard_map.110 = bf16[4,8,32,128]{3,2,1,0:T(8,128)(2,1)S(1)} custom-call(s32[1]{0:T(128)} %get-tuple-element.10.spot, bf16[4,8,32,128]{3,2,1,0:T(8,128)(2,1)S(1)} %bitcast.16, bf16[4,8,24,128]{3,2,1,0:T(8,128)(2,1)S(1)} %bitcast.22, s32[16,16,16]{2,1,0:T(8,128)S(1)} %copy-done, s32[256,16]{1,0:T(8,128)S(1)} %bitcast.18), custom_call_target="tpu_custom_call" | custom-call | tf_op jit(solution)/shard_map/pallas_call | solution.py:354
  114.0 0.0 copy-start.1
  114.0 12.7 %all_to_all.46 = bf16[32,32,128]{2,1,0:T(8,128)(2,1)S(1)} all-to-all(bf16[32,32,128]{2,1,0:T(8,128)(2,1)S(1)} %bitcast.19), channel_id=1, replica_groups=mesh['zl'=4,'x'=4,'y'=4,'zh'=4,'core'=2] {'x','y','core'}, dimensions={0} | all-to-all | bytes 524288 | tf_op jit(solution)/shard_map/all_to_all | solution.py:366
  126.7 0.0 copy-start.4
  126.7 0.0 copy-start.8
  126.7 0.5 shard_map.111
  127.2 0.0 copy-start.2
  127.3 0.0 copy-start.3
  127.3 15.2 %all_to_all.47.got = bf16[16,32,128]{2,1,0:T(8,128)(2,1)S(1)} all-to-all(bf16[16,32,128]{2,1,0:T(8,128)(2,1)S(1)} %shard_map.111), channel_id=1, replica_groups=mesh['zl'=4,'x'=4,'y'=4,'zh'=4,'core'=2] {'zl','zh'}, dimensions={0} | all-to-all | bytes 262144 | tf_op jit(solution)/shard_map/all_to_all | solution.py:366
  142.4 0.0 copy-done.1
  142.5 0.0 copy-done.4
  142.5 0.0 copy-done.8
  142.5 0.0 copy-done.2
  142.5 0.0 copy-done.3
  142.5 1.1 shard_map.112
Async XLA Ops:
  31.9 19.2 %copy-start = (s32[16,16,16]{2,1,0:T(8,128)S(1)}, s32[16,16,16]{2,1,0:T(8,128)}, u32[]{:S(2)}) copy-start(s32[16,16,16]{2,1,0:T(8,128)} %contact.3) | copy-start | bytes 49156
  65.0 15.7 %copy-start.5 = (f32[264,128]{1,0:T(8,128)S(1)}, f32[264,128]{1,0:T(8,128)}, u32[]{:S(2)}) copy-start(f32[264,128]{1,0:T(8,128)} %get-tuple-element.12.gates) | copy-start | bytes 405508
  65.4 15.3 %copy-start.6 = (bf16[16,8,128]{2,1,0:T(8,128)(2,1)S(1)}, bf16[16,8,128]{2,1,0:T(8,128)(2,1)}, u32[]{:S(2)}) copy-start(bf16[16,8,128]{2,1,0:T(8,128)(2,1)} %param.10) | copy-start | bytes 98308
  65.4 15.3 %copy-start.7 = (bf16[16,8,128]{2,1,0:T(8,128)(2,1)S(1)}, bf16[16,8,128]{2,1,0:T(8,128)(2,1)}, u32[]{:S(2)}) copy-start(bf16[16,8,128]{2,1,0:T(8,128)(2,1)} %param.9) | copy-start | bytes 98308
  65.4 15.3 %copy-start.9 = (bf16[2,128,128]{2,1,0:T(8,128)(2,1)S(1)}, bf16[2,128,128]{2,1,0:T(8,128)(2,1)}, u32[]{:S(2)}) copy-start(bf16[2,128,128]{2,1,0:T(8,128)(2,1)} %w_final.1) | copy-start | bytes 196612
  114.0 28.4 %copy-start.1 = (f32[2,512,128]{2,1,0:T(8,128)S(1)}, f32[2,512,128]{2,1,0:T(8,128)}, u32[]{:S(2)}) copy-start(f32[2,512,128]{2,1,0:T(8,128)} %get-tuple-element.15.proj) | copy-start | bytes 1572868
  126.7 15.8 %copy-start.4 = (bf16[128,256]{1,0:T(8,128)(2,1)S(1)}, bf16[128,256]{1,0:T(8,128)(2,1)}, u32[]{:S(2)}) copy-start(bf16[128,256]{1,0:T(8,128)(2,1)} %w_gate.1) | copy-start | bytes 196612
  126.7 15.8 %copy-start.8 = (f32[136,128]{1,0:T(8,128)S(1)}, f32[136,128]{1,0:T(8,128)}, u32[]{:S(2)}) copy-start(f32[136,128]{1,0:T(8,128)} %get-tuple-element.17.scaled_t) | copy-start | bytes 208900
  127.2 15.2 %copy-start.2 = (bf16[128,512]{1,0:T(8,128)(2,1)S(1)}, bf16[128,512]{1,0:T(8,128)(2,1)}, u32[]{:S(2)}) copy-start(bf16[128,512]{1,0:T(8,128)(2,1)} %w_out.1) | copy-start | bytes 393220
  127.3 15.2 %copy-start.3 = (bf16[128,512]{1,0:T(8,128)(2,1)S(1)}, bf16[128,512]{1,0:T(8,128)(2,1)}, u32[]{:S(2)}) copy-start(bf16[128,512]{1,0:T(8,128)(2,1)} %w_in.1) | copy-start | bytes 393220

commit v7 on v6

--- a/solution.py
+++ b/solution.py
@@ -2,6 +2,8 @@
 
 import jax
 import jax.numpy as jnp
+import ml_dtypes
+import numpy as np
 from jax import lax
 from jax.experimental import pallas as pl
 from jax.experimental.pallas import tpu as pltpu
@@ -61,33 +63,21 @@
     return copies
 
 
-def first_kernel(*refs):
-    spot, far, near = refs[0], refs[1:7], refs[12:18]
-    send, proj, gates, scaled_t, mate = refs[7:12]
-    copies = fetch(list(zip(far, near)), refs[18])
+def first_kernel(spot, pair, gain, w_out, w_in, update, send, rest, mate):
     mate[0] = spot[0]
-    pair, gain, w_out, w_in, w_gate, update = near
-    copies[0].wait()
-    pair_t = dot(pair[...], pair_order(), ((0,), (0,)))
-    scaled, inverse = norm(pair_t)
-    copies[1].wait()
+    scaled, inverse = norm(dot(pair[...], pair_order(), ((0,), (0,))))
     normed = (scaled * column(gain[...])).astype(BF)
-    scaled_t[0:128] = scaled
-    scaled_t[128:129] = inverse
-    scaled_t[129:130] = gain[...]
+    rest[0:128] = scaled
+    rest[128:129] = inverse
+    rest[129:130] = gain[...]
     for half, weights in enumerate((w_out, w_in)):
-        copies[2 + half].wait()
         p = dot(weights[...], normed, ((0,), (0,)))
-        proj[half] = p
         for side in range(2):
             part = 256 * side
             gated = jax.nn.sigmoid(p[part : part + 128]) * p[part + 128 : part + 256]
             row = 16 * half + 8 * side
             send[:, row : row + 8] = groups(gated)
-    copies[4].wait()
-    copies[5].wait()
-    gates[0:256] = jax.nn.sigmoid(dot(w_gate[...], normed, ((0,), (0,))))
-    gates[256:258] = update[...]
+    rest[130:132] = update[...]
 
 
 def swap_groups(rows):
@@ -155,25 +145,14 @@
     )
 
 
-def p_block(place):
-    return ((place >> 4) & 3) * 4 + (place >> 6)
-
-
-def reorder(turned=False):
-    p = lax.broadcasted_iota(jnp.int32, (256, 256), 1 if turned else 0)
-    q = lax.broadcasted_iota(jnp.int32, (256, 256), 0 if turned else 1)
-    residue = p_block(p) * 16 + (p & 15)
-    return one_hot(residue, q_block(q) * 16 + ((q >> 4) & 1) * 8 + (q & 7))
-
-
-def whole(got, order):
+def whole(got, big):
     tiles = [got[x, :, 0:16].astype(F32).reshape(128, 128) for x in range(4)]
     left = swap_halves(tiles[0], tiles[1])
     right = swap_halves(tiles[2], tiles[3])
     values = jnp.concatenate(
         [jnp.concatenate([left[low], right[low]], axis=1) for low in range(2)], axis=0
     )
-    return dot(values.astype(BF), order)
+    return dot(values.astype(BF), big[0:256])
 
 
 def quarters(got):
@@ -187,8 +166,8 @@
     return [jnp.concatenate([t[0:64], t[64:128]], axis=1).astype(BF) for t in turned]
 
 
-def send_whole(send, values, back):
-    values = dot(values.astype(BF), back)
+def send_whole(send, values, big):
+    values = dot(values.astype(BF), big[256:512])
     for half in range(2):
         lanes = slice(128 * half, 128 * half + 128)
         tiles = swap_halves(values[0:128, lanes], values[128:256, lanes])
@@ -208,99 +187,97 @@
         send[x, :, 16:] = tile.reshape(8, send.shape[2] - 16, 128).astype(BF)
 
 
+def join(pieces):
+    return jnp.concatenate(pieces, axis=0)
+
+
 NN = ((1,), (0,))
 NT = ((1,), (1,))
 TN = ((0,), (0,))
 
 
-def one_hot(label, values):
-    return (label == values).astype(F32).astype(BF)
-
-
 def q_block(place):
     return ((place >> 5) & 3) * 4 + ((place >> 3) & 1) * 2 + (place >> 7)
 
 
-def masks(contact, flat, mate):
-    place = lax.broadcasted_iota(jnp.int32, (32, 16), 0) << 3
-    label = lax.broadcasted_iota(jnp.int32, (32, 16), 1)
-    short = one_hot(label, q_block(place))
-    place = lax.broadcasted_iota(jnp.int32, (256, 16), 0)
-    label = lax.broadcasted_iota(jnp.int32, (256, 16), 1)
-    table = one_hot(label, q_block(place))
-    place = lax.broadcasted_iota(jnp.int32, (32, 256), 0) << 3
-    label = lax.broadcasted_iota(jnp.int32, (32, 256), 1)
-    j_short = (label & 15 == q_block(place)).astype(F32)
-    place = lax.broadcasted_iota(jnp.int32, (256, 256), 0)
-    label = lax.broadcasted_iota(jnp.int32, (256, 256), 1)
-    i_table = one_hot(label >> 4, q_block(place))
+def tables():
+    place = np.arange(256)
+    residue_p = (((place >> 4) & 3) * 4 + (place >> 6)) * 16 + (place & 15)
+    residue_q = q_block(place) * 16 + ((place >> 4) & 1) * 8 + (place & 7)
+    order = residue_p[:, None] == residue_q[None, :]
+    blocks = q_block(place)[:, None] == place[None, :] >> 4
+    long = q_block(place)[:, None] == np.arange(16)[None, :]
+    wide = q_block(place)[::8, None] == (place & 15)[None, :]
+    big = np.concatenate([order, order.T, blocks], axis=0).astype(ml_dtypes.bfloat16)
+    small = np.concatenate([long, long[::8]], axis=0).astype(ml_dtypes.bfloat16)
+    return jnp.asarray(big), jnp.asarray(small), jnp.asarray(wide.astype(np.float32))
+
+
+def masks(contact, flat, mate, big, small, wide):
     by_k = flat[...].astype(F32)
     wanted = lax.broadcasted_iota(jnp.int32, (4, 16), 0) + 4 * mate
     label = lax.broadcasted_iota(jnp.int32, (4, 16), 1)
-    by_k = dot(one_hot(label, wanted), by_k.astype(BF), NT)
+    by_k = dot((label == wanted).astype(F32).astype(BF), by_k.astype(BF), NT)
+    short, long = small[256:288], small[0:256]
     for_out = [
         dot(short, contact[4 * mate + t].astype(F32).astype(BF), NT).astype(BF) for t in range(4)
     ]
-    for_in = [(j_short * by_k[t : t + 1]).astype(BF) for t in range(4)]
-    mask_out = dot(jnp.concatenate(for_out, axis=0), table, NT)
-    mask_in = dot(jnp.concatenate(for_in, axis=0), i_table, NT)
-    return mask_out.reshape(4, 32, 1, 256), mask_in.reshape(4, 32, 1, 256)
-
-
-def apply(mask, values):
+    for_in = [(wide[...] * by_k[t : t + 1]).astype(BF) for t in range(4)]
+    return dot(join(for_out), long, NT), dot(join(for_in), big[512:768], NT)
+
+
+def apply(masks, t, values):
+    mask = masks[32 * t : 32 * t + 32].reshape(32, 1, 256)
     return (values.reshape(32, 8, 256) * mask).reshape(256, 256)
 
 
-def join(pieces):
-    return jnp.concatenate(pieces, axis=0)
-
-
-def forward_kernel(spot, got, contact, flat, send, near, arrived):
+def forward_kernel(spot, got, contact, flat, big, small, wide, send, made, near, arrived):
     copies = fetch([(contact, near)], arrived)
-    order, back = reorder(), reorder(True)
     left_out, left_in, right_in = quarters(got)
-    right_out = whole(got, order)
+    right_out = whole(got, big)
     copies[0].wait()
-    mask_out, mask_in = masks(near, flat, spot[0])
+    mask_out, mask_in = masks(near, flat, spot[0], big, small, wide)
+    made[0:128] = mask_out
+    made[128:256] = mask_in
     outs, ins = [], None
     for t in range(4):
         part = slice(16 * t, 16 * t + 16)
-        outs.append(dot(left_out[part], apply(mask_out[t], right_out).astype(BF), NN))
-        term = apply(mask_in[t], dot(right_in[part], left_in[part], TN))
+        outs.append(dot(left_out[part], apply(mask_out, t, right_out).astype(BF), NN))
+        term = apply(mask_in, t, dot(right_in[part], left_in[part], TN))
         ins = term if ins is None else ins + term
-    send_whole(send, ins, back)
+    send_whole(send, ins, big)
     send_quarters(send, [join(outs)])
 
 
-def backward_kernel(spot, got, grads, contact, flat, send, near, arrived):
-    copies = fetch([(contact, near)], arrived)
-    order, back = reorder(), reorder(True)
+def backward_kernel(got, grads, made, big, send):
     left_out, left_in, right_in = quarters(got)
     grad_out = quarters(grads)[0]
-    right_out = whole(got, order)
-    grad_in = whole(grads, order)
-    copies[0].wait()
-    mask_out, mask_in = masks(near, flat, spot[0])
+    right_out = whole(got, big)
+    grad_in = whole(grads, big)
+    mask_out, mask_in = made[0:128], made[128:256]
     grad_left_out, grad_left_in, grad_right_in, grad_right_out = [], [], [], None
     for t in range(4):
         part = slice(16 * t, 16 * t + 16)
-        grad_left_out.append(dot(grad_out[part], apply(mask_out[t], right_out).astype(BF), NT))
-        term = apply(mask_out[t], dot(left_out[part], grad_out[part], TN))
+        over_j = apply(mask_out, t, right_out).astype(BF)
+        grad_left_out.append(dot(grad_out[part], over_j, NT))
+        term = apply(mask_out, t, dot(left_out[part], grad_out[part], TN))
         grad_right_out = term if grad_right_out is None else grad_right_out + term
-        both = apply(mask_in[t], grad_in).astype(BF)
+        both = apply(mask_in, t, grad_in).astype(BF)
         grad_left_in.append(dot(right_in[part], both, NN))
         grad_right_in.append(dot(left_in[part], both, NT))
-    send_whole(send, grad_right_out, back)
+    send_whole(send, grad_right_out, big)
     send_quarters(send, [join(grad_left_out), join(grad_left_in), join(grad_right_in)])
 
 
-def middle_kernel(pair, cotangent, got, gates, w_final, updated, send, grad_gate):
+def middle_kernel(pair, cotangent, got, rest, w_gate, w_final, updated, send, grad_gate):
     order = pair_order()
     upstream = dot(cotangent[...], order, TN)
     total = dot(pair[...], order, TN)
+    normed_pair = (rest[0:128] * column(rest[129:130])).astype(BF)
+    gates = jax.nn.sigmoid(dot(w_gate[...], normed_pair, TN))
     for t in range(2):
         scaled, inverse = norm(take(got, t))
-        gain_t = column(gates[256 + t : 257 + t])
+        gain_t = column(rest[130 + t : 131 + t])
         normed = (scaled * gain_t).astype(BF)
         gate = gates[128 * t : 128 * t + 128]
         final = dot(w_final[t], normed, TN)
@@ -312,12 +289,14 @@
     updated[...] = dot(order, total.astype(BF), NT).astype(BF)
 
 
-def last_kernel(cotangent, got, proj, grad_gate, scaled_t, w_out, w_in, w_gate, grad_pair):
+def last_kernel(cotangent, got, grad_gate, rest, w_out, w_in, w_gate, grad_pair):
     order = pair_order()
     upstream = dot(cotangent[...], order, TN)
     grad_normed = dot(w_gate[...], grad_gate[...])
+    scaled, inverse, gain = rest[0:128], rest[128:129], column(rest[129:130])
+    normed = (scaled * gain).astype(BF)
     for half, weights in enumerate((w_out, w_in)):
-        p = proj[half]
+        p = dot(weights[...], normed, TN)
         parts = []
         for side in range(2):
             grad = take(got, 2 * half + side)
@@ -327,12 +306,11 @@
         grad_normed = grad_normed + dot(
             weights[...], jnp.concatenate(parts, axis=0).astype(BF)
         )
-    weighted = grad_normed * column(scaled_t[129:130])
-    back = norm_back(weighted, scaled_t[0:128], scaled_t[128:129])
+    back = norm_back(grad_normed * gain, scaled, inverse)
     grad_pair[...] = dot(order, (upstream + back).astype(BF), NT).astype(BF)
 
 
-def call(kernel, out, *args, scratch=(), spot=False, far=()):
+def call(kernel, out, *args, scratch=(), spot=False, far=(), limit=32 * 1024 * 1024):
     specs = [pl.BlockSpec(memory_space=pltpu.VMEM)] * len(args)
     for n in far:
         specs[n] = pl.BlockSpec(memory_space=pltpu.HBM)
@@ -348,9 +326,7 @@
     buffers += [pltpu.VMEM(s, F32) for s in scratch]
     if far:
         buffers.append(pltpu.SemaphoreType.DMA((len(far),)))
-    params = pltpu.CompilerParams(vmem_limit_bytes=32 * 1024 * 1024)
-    if len(far) > 1:
-        params = None
+    params = pltpu.CompilerParams(vmem_limit_bytes=limit) if limit else None
     result = pl.pallas_call(
         kernel,
         out_shape=shapes,
@@ -400,33 +376,30 @@
     upstream = cotangent.reshape(128, 128)
     flat = contact.reshape(256, 16)
 
-    send, proj, gates, scaled_t, mate = call(
+    send, rest, mate = call(
         first_kernel,
-        [
-            ((16, 32, 128), BF),
-            ((2, 512, 128), F32),
-            ((264, 128), F32),
-            ((136, 128), F32),
-            ((1,), jnp.int32),
-        ],
+        [((16, 32, 128), BF), ((136, 128), F32), ((1,), jnp.int32)],
         my_mate().reshape(1),
         pair,
         norm_gain.reshape(1, 128),
         w_out_proj,
         w_in_proj,
-        w_gate,
         update_gain,
         spot=True,
-        far=range(1, 7),
+        limit=None,
     )
     sides = to_channels(send, 1, (0, 2, 3))
-    triangles = call(
+    big, small, wide = tables()
+    triangles, made = call(
         forward_kernel,
-        ((4, 8, 24, 128), BF),
+        [((4, 8, 24, 128), BF), ((256, 256), F32)],
         mate,
         sides,
         contact,
         flat,
+        big,
+        small,
+        wide,
         spot=True,
         far=(2,),
     )
@@ -436,28 +409,25 @@
         pair,
         upstream,
         to_pairs(triangles, 1, (0,)),
-        gates,
+        rest,
+        w_gate,
         w_final,
     )
     grads = call(
         backward_kernel,
         ((4, 8, 32, 128), BF),
-        mate,
         sides,
         to_channels(send, 1, (0,)),
-        contact,
-        flat,
-        spot=True,
-        far=(3,),
+        made,
+        big,
     )
     grad_pair = call(
         last_kernel,
         ((128, 128), BF),
         upstream,
         to_pairs(grads, 1, (0, 2, 3)),
-        proj,
         grad_gate,
-        scaled_t,
+        rest,
         w_out_proj,
         w_in_proj,
         w_gate,

time: 145 us -> 144 us (level)
  no operation moved by 1% of the time
where the time goes in v7:
time: 144 us; the launch traced here: 143 us
  blocking collectives  131 us (91%)
  Pallas kernels  10.3 us (7%)
    all_to_all x8, blocking collectives, exchange(): return lax.all_to_all(values, axis, 0, 0, tiled=True)  131 us
    pallas_call x9, Pallas kernels, call(): pl.pallas_call(kernel, out_shape=shapes, in_specs=specs, out_specs=outs,...  10.3 us

profile of v7, /device:TPU:1, one launch (start us, length us, event | category | flops | bytes accessed | tf_op | source)
XLA Modules:
  0.0 142.5 jit_solution(10076882372830641617)
XLA Ops:
  0.6 2.1 %shard_map.131 = (bf16[16,32,128]{2,1,0:T(8,128)(2,1)}, f32[136,128]{1,0:T(8,128)}, s32[1]{0:T(128)}) custom-call(s32[1]{0:T(128)} %bitcast.2.spot, bf16[128,128]{1,0:T(8,128)(2,1)} %bitcast.25, f32[1,128]{1,0:T(1,128)} %bitcast.30, bf16[128,512]{1,0:T(8,128)(2,1)} %w_out.3, bf16[128,512]{1,0:T(8,128)(2,1)} %w_in.3, f32[2,128]{1,0:T(2,128)} %update.1), custom_call_target="tpu_custom_call" | custom-call | tf_op jit(solution)/shard_map/pallas_call | solution.py:330
  2.8 28.1 %all_to_all.40.got = bf16[16,32,128]{2,1,0:T(8,128)(2,1)S(1)} all-to-all(bf16[16,32,128]{2,1,0:T(8,128)(2,1)} %get-tuple-element.11), channel_id=1, replica_groups=mesh['zl'=4,'x'=4,'y'=4,'zh'=4,'core'=2] {'zl','zh'}, dimensions={0} | all-to-all | bytes 262144 | tf_op jit(solution)/shard_map/all_to_all | solution.py:342
  30.9 0.0 copy-start
  30.9 0.6 shard_map.132
  31.5 0.0 copy-start.1
  31.5 0.0 copy-start.8
  31.5 0.0 copy-start.10
  31.5 19.2 %all_to_all.41 = bf16[32,32,128]{2,1,0:T(8,128)(2,1)S(1)} all-to-all(bf16[32,32,128]{2,1,0:T(8,128)(2,1)S(1)} %bitcast.17), channel_id=1, replica_groups=mesh['zl'=4,'x'=4,'y'=4,'zh'=4,'core'=2] {'x','y','core'}, dimensions={0} | all-to-all | bytes 524288 | tf_op jit(solution)/shard_map/all_to_all | solution.py:342
  50.7 0.0 copy-done
  50.7 0.0 copy-done.1
  50.7 0.0 copy-done.8
  50.7 0.0 copy-done.10
  50.7 2.0 %shard_map.133 = (bf16[4,8,24,128]{3,2,1,0:T(8,128)(2,1)S(1)}, f32[256,256]{1,0:T(8,128)S(1)}) custom-call(s32[1]{0:T(128)} %get-tuple-element.10.spot, bf16[4,8,32,128]{3,2,1,0:T(8,128)(2,1)S(1)} %bitcast.15, s32[16,16,16]{2,1,0:T(8,128)S(1)} %copy-done.1, s32[256,16]{1,0:T(8,128)S(1)} %bitcast.23, bf16[768,256]{1,0:T(8,128)(2,1)S(1)} %copy-done, ...), custom_call_target="tpu_custom_call" | custom-call | tf_op jit(solution)/shard_map/pallas_call | solution.py:330
  52.8 11.8 %all_to_all.42 = bf16[32,24,128]{2,1,0:T(8,128)(2,1)S(1)} all-to-all(bf16[32,24,128]{2,1,0:T(8,128)(2,1)S(1)} %bitcast.24), channel_id=1, replica_groups=mesh['zl'=4,'x'=4,'y'=4,'zh'=4,'core'=2] {'x','y','core'}, dimensions={0} | all-to-all | bytes 393216 | tf_op jit(solution)/shard_map/all_to_all | solution.py:342
  64.6 0.0 copy-start.5
  64.6 0.0 copy-start.7
  64.6 0.0 copy-start.9
  64.6 0.4 shard_map.134
  65.0 0.0 copy-start.4
  65.0 0.0 copy-start.6
  65.0 15.3 %all_to_all.43.got = bf16[16,16,128]{2,1,0:T(8,128)(2,1)S(1)} all-to-all(bf16[16,16,128]{2,1,0:T(8,128)(2,1)S(1)} %shard_map.134), channel_id=1, replica_groups=mesh['zl'=4,'x'=4,'y'=4,'zh'=4,'core'=2] {'zl','zh'}, dimensions={0} | all-to-all | bytes 131072 | tf_op jit(solution)/shard_map/all_to_all | solution.py:342
  80.3 0.0 copy-done.5
  80.3 0.0 copy-done.7
  80.3 0.0 copy-done.9
  80.3 0.0 copy-done.4
  80.3 0.0 copy-done.6
  80.3 1.1 shard_map.135
  81.4 15.2 %all_to_all.44.got = bf16[16,16,128]{2,1,0:T(8,128)(2,1)S(1)} all-to-all(bf16[16,16,128]{2,1,0:T(8,128)(2,1)S(1)} %get-tuple-element.15), channel_id=1, replica_groups=mesh['zl'=4,'x'=4,'y'=4,'zh'=4,'core'=2] {'zl','zh'}, dimensions={0} | all-to-all | bytes 131072 | tf_op jit(solution)/shard_map/all_to_all | solution.py:342
  96.6 0.5 shard_map.136
  97.1 14.1 %all_to_all.45 = bf16[32,24,128]{2,1,0:T(8,128)(2,1)S(1)} all-to-all(bf16[32,24,128]{2,1,0:T(8,128)(2,1)S(1)} %bitcast.21), channel_id=1, replica_groups=mesh['zl'=4,'x'=4,'y'=4,'zh'=4,'core'=2] {'x','y','core'}, dimensions={0} | all-to-all | bytes 393216 | tf_op jit(solution)/shard_map/all_to_all | solution.py:342
  111.2 1.5 %shard_map.137 = bf16[4,8,32,128]{3,2,1,0:T(8,128)(2,1)S(1)} custom-call(bf16[4,8,32,128]{3,2,1,0:T(8,128)(2,1)S(1)} %bitcast.16, bf16[4,8,24,128]{3,2,1,0:T(8,128)(2,1)S(1)} %bitcast.22, f32[256,256]{1,0:T(8,128)S(1)} %get-tuple-element.16.made, bf16[768,256]{1,0:T(8,128)(2,1)S(1)} %copy-done), custom_call_target="tpu_custom_call" | custom-call | tf_op jit(solution)/shard_map/pallas_call | solution.py:330
  112.8 12.5 %all_to_all.46 = bf16[32,32,128]{2,1,0:T(8,128)(2,1)S(1)} all-to-all(bf16[32,32,128]{2,1,0:T(8,128)(2,1)S(1)} %bitcast.19), channel_id=1, replica_groups=mesh['zl'=4,'x'=4,'y'=4,'zh'=4,'core'=2] {'x','y','core'}, dimensions={0} | all-to-all | bytes 524288 | tf_op jit(solution)/shard_map/all_to_all | solution.py:342
  125.3 0.5 shard_map.138
  125.8 0.0 copy-start.2
  125.9 0.0 copy-start.3
  125.9 15.2 %all_to_all.47.got = bf16[16,32,128]{2,1,0:T(8,128)(2,1)S(1)} all-to-all(bf16[16,32,128]{2,1,0:T(8,128)(2,1)S(1)} %shard_map.138), channel_id=1, replica_groups=mesh['zl'=4,'x'=4,'y'=4,'zh'=4,'core'=2] {'zl','zh'}, dimensions={0} | all-to-all | bytes 262144 | tf_op jit(solution)/shard_map/all_to_all | solution.py:342
  141.0 0.0 copy-done.2
  141.0 0.0 copy-done.3
  141.0 1.5 %shard_map.139 = bf16[128,128]{1,0:T(8,128)(2,1)} custom-call(bf16[128,128]{1,0:T(8,128)(2,1)S(1)} %bitcast.28, bf16[16,32,128]{2,1,0:T(8,128)(2,1)S(1)} %all_to_all.47.got, bf16[256,128]{1,0:T(8,128)(2,1)S(1)} %get-tuple-element.17.grad_gate, f32[136,128]{1,0:T(8,128)S(1)} %copy-done.4, bf16[128,512]{1,0:T(8,128)(2,1)S(1)} %copy-done.2, ...), custom_call_target="tpu_custom_call" | custom-call | tf_op jit(solution)/shard_map/pallas_call | solution.py:330
Async XLA Ops:
  30.9 19.8 %copy-start = (bf16[768,256]{1,0:T(8,128)(2,1)S(1)}, bf16[768,256]{1,0:T(8,128)(2,1)}, u32[]{:S(2)}) copy-start(bf16[768,256]{1,0:T(8,128)(2,1)} %constant.25.clone.big) | copy-start | bytes 1179652
  31.5 19.2 %copy-start.1 = (s32[16,16,16]{2,1,0:T(8,128)S(1)}, s32[16,16,16]{2,1,0:T(8,128)}, u32[]{:S(2)}) copy-start(s32[16,16,16]{2,1,0:T(8,128)} %contact.1) | copy-start | bytes 49156
  31.5 19.2 %copy-start.8 = (bf16[288,16]{1,0:T(8,128)(2,1)S(1)}, bf16[288,16]{1,0:T(8,128)(2,1)}, u32[]{:S(2)}) copy-start(bf16[288,16]{1,0:T(8,128)(2,1)} %constant.26.clone.small) | copy-start | bytes 27652
  31.5 19.2 %copy-start.10 = (f32[32,256]{1,0:T(8,128)S(1)}, f32[32,256]{1,0:T(8,128)}, u32[]{:S(2)}) copy-start(f32[32,256]{1,0:T(8,128)} %constant.27.clone.wide) | copy-start | bytes 98308
  64.6 15.7 %copy-start.5 = (bf16[128,256]{1,0:T(8,128)(2,1)S(1)}, bf16[128,256]{1,0:T(8,128)(2,1)}, u32[]{:S(2)}) copy-start(bf16[128,256]{1,0:T(8,128)(2,1)} %w_gate.3) | copy-start | bytes 196612
  64.6 15.7 %copy-start.7 = (bf16[16,8,128]{2,1,0:T(8,128)(2,1)S(1)}, bf16[16,8,128]{2,1,0:T(8,128)(2,1)}, u32[]{:S(2)}) copy-start(bf16[16,8,128]{2,1,0:T(8,128)(2,1)} %param.13) | copy-start | bytes 98308
  64.6 15.7 %copy-start.9 = (bf16[2,128,128]{2,1,0:T(8,128)(2,1)S(1)}, bf16[2,128,128]{2,1,0:T(8,128)(2,1)}, u32[]{:S(2)}) copy-start(bf16[2,128,128]{2,1,0:T(8,128)(2,1)} %w_final.1) | copy-start | bytes 196612
  65.0 15.3 %copy-start.4 = (f32[136,128]{1,0:T(8,128)S(1)}, f32[136,128]{1,0:T(8,128)}, u32[]{:S(2)}) copy-start(f32[136,128]{1,0:T(8,128)} %get-tuple-element.13.rest) | copy-start | bytes 208900
  65.0 15.3 %copy-start.6 = (bf16[16,8,128]{2,1,0:T(8,128)(2,1)S(1)}, bf16[16,8,128]{2,1,0:T(8,128)(2,1)}, u32[]{:S(2)}) copy-start(bf16[16,8,128]{2,1,0:T(8,128)(2,1)} %param.12) | copy-start | bytes 98308
  125.8 15.2 %copy-start.2 = (bf16[128,512]{1,0:T(8,128)(2,1)S(1)}, bf16[128,512]{1,0:T(8,128)(2,1)}, u32[]{:S(2)}) copy-start(bf16[128,512]{1,0:T(8,128)(2,1)} %w_out.3) | copy-start | bytes 393220
  125.9 15.2 %copy-start.3 = (bf16[128,512]{1,0:T(8,128)(2,1)S(1)}, bf16[128,512]{1,0:T(8,128)(2,1)}, u32[]{:S(2)}) copy-start(bf16[128,512]{1,0:T(8,128)(2,1)} %w_in.3) | copy-start | bytes 393220

commit v8 on v7

--- a/solution.py
+++ b/solution.py
@@ -52,32 +52,6 @@
 
 def take(got, array):
     return got[:, 8 * array : 8 * array + 8].astype(F32).reshape(128, 128)
-
-
-def fetch(pairs, arrived):
-    copies = [
-        pltpu.make_async_copy(there, here, arrived.at[n]) for n, (there, here) in enumerate(pairs)
-    ]
-    for copy in copies:
-        copy.start()
-    return copies
-
-
-def first_kernel(spot, pair, gain, w_out, w_in, update, send, rest, mate):
-    mate[0] = spot[0]
-    scaled, inverse = norm(dot(pair[...], pair_order(), ((0,), (0,))))
-    normed = (scaled * column(gain[...])).astype(BF)
-    rest[0:128] = scaled
-    rest[128:129] = inverse
-    rest[129:130] = gain[...]
-    for half, weights in enumerate((w_out, w_in)):
-        p = dot(weights[...], normed, ((0,), (0,)))
-        for side in range(2):
-            part = 256 * side
-            gated = jax.nn.sigmoid(p[part : part + 128]) * p[part + 128 : part + 256]
-            row = 16 * half + 8 * side
-            send[:, row : row + 8] = groups(gated)
-    rest[130:132] = update[...]
 
 
 def swap_groups(rows):
@@ -208,12 +182,13 @@
     blocks = q_block(place)[:, None] == place[None, :] >> 4
     long = q_block(place)[:, None] == np.arange(16)[None, :]
     wide = q_block(place)[::8, None] == (place & 15)[None, :]
-    big = np.concatenate([order, order.T, blocks], axis=0).astype(ml_dtypes.bfloat16)
-    small = np.concatenate([long, long[::8]], axis=0).astype(ml_dtypes.bfloat16)
-    return jnp.asarray(big), jnp.asarray(small), jnp.asarray(wide.astype(np.float32))
-
-
-def masks(contact, flat, mate, big, small, wide):
+    big = np.concatenate([order, order.T], axis=0)
+    small = np.concatenate([long, long[::8]], axis=0)
+    big, blocks, small = (jnp.asarray(x.astype(ml_dtypes.bfloat16)) for x in (big, blocks, small))
+    return big, blocks, small, jnp.asarray(wide.astype(np.float32))
+
+
+def masks(contact, flat, mate, blocks, small, wide):
     by_k = flat[...].astype(F32)
     wanted = lax.broadcasted_iota(jnp.int32, (4, 16), 0) + 4 * mate
     label = lax.broadcasted_iota(jnp.int32, (4, 16), 1)
@@ -223,7 +198,7 @@
         dot(short, contact[4 * mate + t].astype(F32).astype(BF), NT).astype(BF) for t in range(4)
     ]
     for_in = [(wide[...] * by_k[t : t + 1]).astype(BF) for t in range(4)]
-    return dot(join(for_out), long, NT), dot(join(for_in), big[512:768], NT)
+    return dot(join(for_out), long, NT), dot(join(for_in), blocks[...], NT)
 
 
 def apply(masks, t, values):
@@ -231,14 +206,10 @@
     return (values.reshape(32, 8, 256) * mask).reshape(256, 256)
 
 
-def forward_kernel(spot, got, contact, flat, big, small, wide, send, made, near, arrived):
-    copies = fetch([(contact, near)], arrived)
+def forward_kernel(got, made, big, send):
     left_out, left_in, right_in = quarters(got)
     right_out = whole(got, big)
-    copies[0].wait()
-    mask_out, mask_in = masks(near, flat, spot[0], big, small, wide)
-    made[0:128] = mask_out
-    made[128:256] = mask_in
+    mask_out, mask_in = made[0:128], made[128:256]
     outs, ins = [], None
     for t in range(4):
         part = slice(16 * t, 16 * t + 16)
@@ -269,6 +240,28 @@
     send_quarters(send, [join(grad_left_out), join(grad_left_in), join(grad_right_in)])
 
 
+def first_kernel(
+    spot, pair, gain, w_out, w_in, update, contact, flat, blocks, small, wide, send, rest, made, proj
+):
+    scaled, inverse = norm(dot(pair[...], pair_order(), ((0,), (0,))))
+    normed = (scaled * column(gain[...])).astype(BF)
+    rest[0:128] = scaled
+    rest[128:129] = inverse
+    rest[129:130] = gain[...]
+    for half, weights in enumerate((w_out, w_in)):
+        p = dot(weights[...], normed, ((0,), (0,)))
+        proj[half] = p
+        for side in range(2):
+            part = 256 * side
+            gated = jax.nn.sigmoid(p[part : part + 128]) * p[part + 128 : part + 256]
+            row = 16 * half + 8 * side
+            send[:, row : row + 8] = groups(gated)
+    rest[130:132] = update[...]
+    mask_out, mask_in = masks(contact, flat, spot[0], blocks, small, wide)
+    made[0:128] = mask_out
+    made[128:256] = mask_in
+
+
 def middle_kernel(pair, cotangent, got, rest, w_gate, w_final, updated, send, grad_gate):
     order = pair_order()
     upstream = dot(cotangent[...], order, TN)
@@ -289,14 +282,13 @@
     updated[...] = dot(order, total.astype(BF), NT).astype(BF)
 
 
-def last_kernel(cotangent, got, grad_gate, rest, w_out, w_in, w_gate, grad_pair):
+def last_kernel(cotangent, got, grad_gate, rest, proj, w_out, w_in, w_gate, grad_pair):
     order = pair_order()
     upstream = dot(cotangent[...], order, TN)
     grad_normed = dot(w_gate[...], grad_gate[...])
     scaled, inverse, gain = rest[0:128], rest[128:129], column(rest[129:130])
-    normed = (scaled * gain).astype(BF)
     for half, weights in enumerate((w_out, w_in)):
-        p = dot(weights[...], normed, TN)
+        p = proj[half]
         parts = []
         for side in range(2):
             grad = take(got, 2 * half + side)
@@ -310,29 +302,20 @@
     grad_pair[...] = dot(order, (upstream + back).astype(BF), NT).astype(BF)
 
 
-def call(kernel, out, *args, scratch=(), spot=False, far=(), limit=32 * 1024 * 1024):
+def call(kernel, out, *args, scratch=(), spot=False, limit=32 * 1024 * 1024):
     specs = [pl.BlockSpec(memory_space=pltpu.VMEM)] * len(args)
-    for n in far:
-        specs[n] = pl.BlockSpec(memory_space=pltpu.HBM)
     if spot:
         specs[0] = pl.BlockSpec(memory_space=pltpu.SMEM)
     multi = isinstance(out, list)
     shapes = [jax.ShapeDtypeStruct(s, d) for s, d in (out if multi else [out])]
-    outs = [
-        pl.BlockSpec(memory_space=pltpu.SMEM if x.dtype == jnp.int32 else pltpu.VMEM)
-        for x in shapes
-    ]
-    buffers = [pltpu.VMEM(args[n].shape, args[n].dtype) for n in far]
-    buffers += [pltpu.VMEM(s, F32) for s in scratch]
-    if far:
-        buffers.append(pltpu.SemaphoreType.DMA((len(far),)))
+    outs = [pl.BlockSpec(memory_space=pltpu.VMEM)] * len(shapes)
     params = pltpu.CompilerParams(vmem_limit_bytes=limit) if limit else None
     result = pl.pallas_call(
         kernel,
         out_shape=shapes,
         in_specs=specs,
         out_specs=outs,
-        scratch_shapes=buffers,
+        scratch_shapes=[pltpu.VMEM(s, F32) for s in scratch],
         compiler_params=params,
     )(*args)
     return result if multi else result[0]
@@ -376,33 +359,31 @@
     upstream = cotangent.reshape(128, 128)
     flat = contact.reshape(256, 16)
 
-    send, rest, mate = call(
+    big, blocks, small, wide = tables()
+    send, rest, made, proj = call(
         first_kernel,
-        [((16, 32, 128), BF), ((136, 128), F32), ((1,), jnp.int32)],
+        [
+            ((16, 32, 128), BF),
+            ((136, 128), F32),
+            ((256, 256), F32),
+            ((2, 512, 128), F32),
+        ],
         my_mate().reshape(1),
         pair,
         norm_gain.reshape(1, 128),
         w_out_proj,
         w_in_proj,
         update_gain,
-        spot=True,
-        limit=None,
-    )
-    sides = to_channels(send, 1, (0, 2, 3))
-    big, small, wide = tables()
-    triangles, made = call(
-        forward_kernel,
-        [((4, 8, 24, 128), BF), ((256, 256), F32)],
-        mate,
-        sides,
         contact,
         flat,
-        big,
+        blocks,
         small,
         wide,
         spot=True,
-        far=(2,),
-    )
+        limit=None,
+    )
+    sides = to_channels(send, 1, (0, 2, 3))
+    triangles = call(forward_kernel, ((4, 8, 24, 128), BF), sides, made, big)
     updated, send, grad_gate = call(
         middle_kernel,
         [((128, 128), BF), ((16, 16, 128), BF), ((256, 128), BF)],
@@ -428,6 +409,7 @@
         to_pairs(grads, 1, (0, 2, 3)),
         grad_gate,
         rest,
+        proj,
         w_out_proj,
         w_in_proj,
         w_gate,

time: 144 us -> 143 us (level)
  no operation moved by 1% of the time
where the time goes in v8:
time: 143 us; the launch traced here: 142 us
  blocking collectives  131 us (92%)
  Pallas kernels  9.26 us (6%)
    all_to_all x8, blocking collectives, exchange(): return lax.all_to_all(values, axis, 0, 0, tiled=True)  131 us
    pallas_call x9, Pallas kernels, call(): pl.pallas_call(kernel, out_shape=shapes, in_specs=specs, out_specs=outs,...  9.26 us

profile of v8, /device:TPU:1, one launch (start us, length us, event | category | flops | bytes accessed | tf_op | source)
XLA Modules:
  0.0 141.5 jit_solution(14365563636509696649)
XLA Ops:
  0.6 2.7 %shard_map.140 = (bf16[16,32,128]{2,1,0:T(8,128)(2,1)}, f32[136,128]{1,0:T(8,128)}, f32[256,256]{1,0:T(8,128)}, f32[2,512,128]{2,1,0:T(8,128)}) custom-call(s32[1]{0:T(128)} %bitcast.2.spot, bf16[128,128]{1,0:T(8,128)(2,1)} %bitcast.24, f32[1,128]{1,0:T(1,128)} %bitcast.30, bf16[128,512]{1,0:T(8,128)(2,1)} %w_out.3, bf16[128,512]{1,0:T(8,128)(2,1)} %w_in.3, ...), custom_call_target="tpu_custom_call" | custom-call | tf_op jit(solution)/shard_map/pallas_call | solution.py:313
  3.3 28.1 %all_to_all.40.got = bf16[16,32,128]{2,1,0:T(8,128)(2,1)S(1)} all-to-all(bf16[16,32,128]{2,1,0:T(8,128)(2,1)} %get-tuple-element.9), channel_id=1, replica_groups=mesh['zl'=4,'x'=4,'y'=4,'zh'=4,'core'=2] {'zl','zh'}, dimensions={0} | all-to-all | bytes 262144 | tf_op jit(solution)/shard_map/all_to_all | solution.py:325
  31.4 0.6 shard_map.141
  32.0 0.0 copy-start
  32.0 0.0 copy-start.1
  32.1 19.2 %all_to_all.41 = bf16[32,32,128]{2,1,0:T(8,128)(2,1)S(1)} all-to-all(bf16[32,32,128]{2,1,0:T(8,128)(2,1)S(1)} %bitcast.18), channel_id=1, replica_groups=mesh['zl'=4,'x'=4,'y'=4,'zh'=4,'core'=2] {'x','y','core'}, dimensions={0} | all-to-all | bytes 524288 | tf_op jit(solution)/shard_map/all_to_all | solution.py:325
  51.2 0.0 copy-done
  51.2 0.0 copy-done.1
  51.2 0.8 shard_map.142
  52.1 11.8 %all_to_all.42 = bf16[32,24,128]{2,1,0:T(8,128)(2,1)S(1)} all-to-all(bf16[32,24,128]{2,1,0:T(8,128)(2,1)S(1)} %bitcast.23), channel_id=1, replica_groups=mesh['zl'=4,'x'=4,'y'=4,'zh'=4,'core'=2] {'x','y','core'}, dimensions={0} | all-to-all | bytes 393216 | tf_op jit(solution)/shard_map/all_to_all | solution.py:325
  63.9 0.0 copy-start.6
  63.9 0.0 copy-start.8
  63.9 0.0 copy-start.9
  63.9 0.4 shard_map.143
  64.3 0.0 copy-start.5
  64.3 0.0 copy-start.7
  64.3 15.3 %all_to_all.43.got = bf16[16,16,128]{2,1,0:T(8,128)(2,1)S(1)} all-to-all(bf16[16,16,128]{2,1,0:T(8,128)(2,1)S(1)} %shard_map.143), channel_id=1, replica_groups=mesh['zl'=4,'x'=4,'y'=4,'zh'=4,'core'=2] {'zl','zh'}, dimensions={0} | all-to-all | bytes 131072 | tf_op jit(solution)/shard_map/all_to_all | solution.py:325
  79.6 0.0 copy-done.6
  79.6 0.0 copy-done.8
  79.6 0.0 copy-done.9
  79.6 0.0 copy-done.5
  79.6 0.0 copy-done.7
  79.6 1.1 shard_map.144
  80.7 15.2 %all_to_all.44.got = bf16[16,16,128]{2,1,0:T(8,128)(2,1)S(1)} all-to-all(bf16[16,16,128]{2,1,0:T(8,128)(2,1)S(1)} %get-tuple-element.13), channel_id=1, replica_groups=mesh['zl'=4,'x'=4,'y'=4,'zh'=4,'core'=2] {'zl','zh'}, dimensions={0} | all-to-all | bytes 131072 | tf_op jit(solution)/shard_map/all_to_all | solution.py:325
  95.9 0.5 shard_map.145
  96.4 14.1 %all_to_all.45 = bf16[32,24,128]{2,1,0:T(8,128)(2,1)S(1)} all-to-all(bf16[32,24,128]{2,1,0:T(8,128)(2,1)S(1)} %bitcast.22), channel_id=1, replica_groups=mesh['zl'=4,'x'=4,'y'=4,'zh'=4,'core'=2] {'x','y','core'}, dimensions={0} | all-to-all | bytes 393216 | tf_op jit(solution)/shard_map/all_to_all | solution.py:325
  110.5 1.5 %shard_map.146 = bf16[4,8,32,128]{3,2,1,0:T(8,128)(2,1)S(1)} custom-call(bf16[4,8,32,128]{3,2,1,0:T(8,128)(2,1)S(1)} %bitcast.16, bf16[4,8,24,128]{3,2,1,0:T(8,128)(2,1)S(1)} %bitcast.20, f32[256,256]{1,0:T(8,128)S(1)} %copy-done.1, bf16[512,256]{1,0:T(8,128)(2,1)S(1)} %copy-done), custom_call_target="tpu_custom_call" | custom-call | tf_op jit(solution)/shard_map/pallas_call | solution.py:313
  112.1 0.0 copy-start.4
  112.1 12.7 %all_to_all.46 = bf16[32,32,128]{2,1,0:T(8,128)(2,1)S(1)} all-to-all(bf16[32,32,128]{2,1,0:T(8,128)(2,1)S(1)} %bitcast.17), channel_id=1, replica_groups=mesh['zl'=4,'x'=4,'y'=4,'zh'=4,'core'=2] {'x','y','core'}, dimensions={0} | all-to-all | bytes 524288 | tf_op jit(solution)/shard_map/all_to_all | solution.py:325
  124.7 0.5 shard_map.147
  125.3 0.0 copy-start.2
  125.3 0.0 copy-start.3
  125.3 15.2 %all_to_all.47.got = bf16[16,32,128]{2,1,0:T(8,128)(2,1)S(1)} all-to-all(bf16[16,32,128]{2,1,0:T(8,128)(2,1)S(1)} %shard_map.147), channel_id=1, replica_groups=mesh['zl'=4,'x'=4,'y'=4,'zh'=4,'core'=2] {'zl','zh'}, dimensions={0} | all-to-all | bytes 262144 | tf_op jit(solution)/shard_map/all_to_all | solution.py:325
  140.5 0.0 copy-done.4
  140.5 0.0 copy-done.2
  140.5 0.0 copy-done.3
  140.5 1.1 shard_map.148
Async XLA Ops:
  32.0 19.2 %copy-start = (bf16[512,256]{1,0:T(8,128)(2,1)S(1)}, bf16[512,256]{1,0:T(8,128)(2,1)}, u32[]{:S(2)}) copy-start(bf16[512,256]{1,0:T(8,128)(2,1)} %constant.27.clone.big) | copy-start | bytes 786436
  32.0 19.2 %copy-start.1 = (f32[256,256]{1,0:T(8,128)S(1)}, f32[256,256]{1,0:T(8,128)}, u32[]{:S(2)}) copy-start(f32[256,256]{1,0:T(8,128)} %get-tuple-element.10.made) | copy-start | bytes 786436
  63.9 15.7 %copy-start.6 = (bf16[128,256]{1,0:T(8,128)(2,1)S(1)}, bf16[128,256]{1,0:T(8,128)(2,1)}, u32[]{:S(2)}) copy-start(bf16[128,256]{1,0:T(8,128)(2,1)} %w_gate.3) | copy-start | bytes 196612
  63.9 15.7 %copy-start.8 = (bf16[16,8,128]{2,1,0:T(8,128)(2,1)S(1)}, bf16[16,8,128]{2,1,0:T(8,128)(2,1)}, u32[]{:S(2)}) copy-start(bf16[16,8,128]{2,1,0:T(8,128)(2,1)} %param.14) | copy-start | bytes 98308
  63.9 15.7 %copy-start.9 = (bf16[2,128,128]{2,1,0:T(8,128)(2,1)S(1)}, bf16[2,128,128]{2,1,0:T(8,128)(2,1)}, u32[]{:S(2)}) copy-start(bf16[2,128,128]{2,1,0:T(8,128)(2,1)} %w_final.1) | copy-start | bytes 196612
  64.3 15.3 %copy-start.5 = (f32[136,128]{1,0:T(8,128)S(1)}, f32[136,128]{1,0:T(8,128)}, u32[]{:S(2)}) copy-start(f32[136,128]{1,0:T(8,128)} %get-tuple-element.11.rest) | copy-start | bytes 208900
  64.3 15.3 %copy-start.7 = (bf16[16,8,128]{2,1,0:T(8,128)(2,1)S(1)}, bf16[16,8,128]{2,1,0:T(8,128)(2,1)}, u32[]{:S(2)}) copy-start(bf16[16,8,128]{2,1,0:T(8,128)(2,1)} %param.13) | copy-start | bytes 98308
  112.1 28.4 %copy-start.4 = (f32[2,512,128]{2,1,0:T(8,128)S(1)}, f32[2,512,128]{2,1,0:T(8,128)}, u32[]{:S(2)}) copy-start(f32[2,512,128]{2,1,0:T(8,128)} %get-tuple-element.15.proj) | copy-start | bytes 1572868
  125.3 15.2 %copy-start.2 = (bf16[128,512]{1,0:T(8,128)(2,1)S(1)}, bf16[128,512]{1,0:T(8,128)(2,1)}, u32[]{:S(2)}) copy-start(bf16[128,512]{1,0:T(8,128)(2,1)} %w_out.3) | copy-start | bytes 393220
  125.3 15.2 %copy-start.3 = (bf16[128,512]{1,0:T(8,128)(2,1)S(1)}, bf16[128,512]{1,0:T(8,128)(2,1)}, u32[]{:S(2)}) copy-start(bf16[128,512]{1,0:T(8,128)(2,1)} %w_in.3) | copy-start | bytes 393220

commit v9 on v8

--- a/solution.py
+++ b/solution.py
@@ -262,7 +262,7 @@
     made[128:256] = mask_in
 
 
-def middle_kernel(pair, cotangent, got, rest, w_gate, w_final, updated, send, grad_gate):
+def middle_kernel(pair, cotangent, got, rest, w_gate, w_final, final, send, grad_gate):
     order = pair_order()
     upstream = dot(cotangent[...], order, TN)
     total = dot(pair[...], order, TN)
@@ -273,18 +273,21 @@
         gain_t = column(rest[130 + t : 131 + t])
         normed = (scaled * gain_t).astype(BF)
         gate = gates[128 * t : 128 * t + 128]
-        final = dot(w_final[t], normed, TN)
-        total = total + gate * final
+        product = dot(w_final[t], normed, TN)
+        total = total + gate * product
         grad_final = (upstream * gate).astype(BF)
-        grad_gate[128 * t : 128 * t + 128] = (upstream * final * gate * (1.0 - gate)).astype(BF)
+        grad_gate[128 * t : 128 * t + 128] = (upstream * product * gate * (1.0 - gate)).astype(BF)
         weighted = dot(w_final[t], grad_final) * gain_t
         send[:, 8 * t : 8 * t + 8] = groups(norm_back(weighted, scaled, inverse))
-    updated[...] = dot(order, total.astype(BF), NT).astype(BF)
-
-
-def last_kernel(cotangent, got, grad_gate, rest, proj, w_out, w_in, w_gate, grad_pair):
+    final[...] = total.astype(BF)
+
+
+def last_kernel(
+    cotangent, got, grad_gate, rest, proj, final, w_out, w_in, w_gate, updated, grad_pair
+):
     order = pair_order()
     upstream = dot(cotangent[...], order, TN)
+    updated[...] = dot(order, final[...], NT).astype(BF)
     grad_normed = dot(w_gate[...], grad_gate[...])
     scaled, inverse, gain = rest[0:128], rest[128:129], column(rest[129:130])
     for half, weights in enumerate((w_out, w_in)):
@@ -384,7 +387,7 @@
     )
     sides = to_channels(send, 1, (0, 2, 3))
     triangles = call(forward_kernel, ((4, 8, 24, 128), BF), sides, made, big)
-    updated, send, grad_gate = call(
+    final, send, grad_gate = call(
         middle_kernel,
         [((128, 128), BF), ((16, 16, 128), BF), ((256, 128), BF)],
         pair,
@@ -402,14 +405,15 @@
         made,
         big,
     )
-    grad_pair = call(
+    updated, grad_pair = call(
         last_kernel,
-        ((128, 128), BF),
+        [((128, 128), BF), ((128, 128), BF)],
         upstream,
         to_pairs(grads, 1, (0, 2, 3)),
         grad_gate,
         rest,
         proj,
+        final,
         w_out_proj,
         w_in_proj,
         w_gate,

time: 143 us -> 143 us (level)
  no operation moved by 1% of the time
where the time goes in v9:
time: 143 us; the launch traced here: 141 us
  blocking collectives  131 us (92%)
  Pallas kernels  8.62 us (6%)
    all_to_all x8, blocking collectives, exchange(): return lax.all_to_all(values, axis, 0, 0, tiled=True)  131 us
    pallas_call x9, Pallas kernels, call(): pl.pallas_call(kernel, out_shape=shapes, in_specs=specs, out_specs=outs,...  8.62 us

profile of v9, /device:TPU:1, one launch (start us, length us, event | category | flops | bytes accessed | tf_op | source)
XLA Modules:
  0.0 140.9 jit_solution(13936613212549383460)
XLA Ops:
  0.6 2.7 %shard_map.140 = (bf16[16,32,128]{2,1,0:T(8,128)(2,1)}, f32[136,128]{1,0:T(8,128)}, f32[256,256]{1,0:T(8,128)}, f32[2,512,128]{2,1,0:T(8,128)}) custom-call(s32[1]{0:T(128)} %bitcast.1.spot, bf16[128,128]{1,0:T(8,128)(2,1)} %bitcast.24, f32[1,128]{1,0:T(1,128)} %bitcast.29, bf16[128,512]{1,0:T(8,128)(2,1)} %w_out.3, bf16[128,512]{1,0:T(8,128)(2,1)} %w_in.3, ...), custom_call_target="tpu_custom_call" | custom-call | tf_op jit(solution)/shard_map/pallas_call | solution.py:316
  3.3 28.1 %all_to_all.40.got = bf16[16,32,128]{2,1,0:T(8,128)(2,1)S(1)} all-to-all(bf16[16,32,128]{2,1,0:T(8,128)(2,1)} %get-tuple-element.11), channel_id=1, replica_groups=mesh['zl'=4,'x'=4,'y'=4,'zh'=4,'core'=2] {'zl','zh'}, dimensions={0} | all-to-all | bytes 262144 | tf_op jit(solution)/shard_map/all_to_all | solution.py:328
  31.4 0.6 shard_map.141
  32.0 0.0 copy-start
  32.0 0.0 copy-start.1
  32.0 19.2 %all_to_all.41 = bf16[32,32,128]{2,1,0:T(8,128)(2,1)S(1)} all-to-all(bf16[32,32,128]{2,1,0:T(8,128)(2,1)S(1)} %bitcast.18), channel_id=1, replica_groups=mesh['zl'=4,'x'=4,'y'=4,'zh'=4,'core'=2] {'x','y','core'}, dimensions={0} | all-to-all | bytes 524288 | tf_op jit(solution)/shard_map/all_to_all | solution.py:328
  51.2 0.0 copy-done
  51.2 0.0 copy-done.1
  51.2 0.8 shard_map.142
  52.1 11.8 %all_to_all.42 = bf16[32,24,128]{2,1,0:T(8,128)(2,1)S(1)} all-to-all(bf16[32,24,128]{2,1,0:T(8,128)(2,1)S(1)} %bitcast.23), channel_id=1, replica_groups=mesh['zl'=4,'x'=4,'y'=4,'zh'=4,'core'=2] {'x','y','core'}, dimensions={0} | all-to-all | bytes 393216 | tf_op jit(solution)/shard_map/all_to_all | solution.py:328
  63.9 0.0 copy-start.6
  63.9 0.0 copy-start.8
  63.9 0.0 copy-start.9
  63.9 0.4 shard_map.143
  64.3 0.0 copy-start.5
  64.3 0.0 copy-start.7
  64.3 15.3 %all_to_all.43.got = bf16[16,16,128]{2,1,0:T(8,128)(2,1)S(1)} all-to-all(bf16[16,16,128]{2,1,0:T(8,128)(2,1)S(1)} %shard_map.143), channel_id=1, replica_groups=mesh['zl'=4,'x'=4,'y'=4,'zh'=4,'core'=2] {'zl','zh'}, dimensions={0} | all-to-all | bytes 131072 | tf_op jit(solution)/shard_map/all_to_all | solution.py:328
  79.6 0.0 copy-done.6
  79.6 0.0 copy-done.8
  79.6 0.0 copy-done.9
  79.6 0.0 copy-done.5
  79.6 0.0 copy-done.7
  79.6 0.4 shard_map.144
  80.1 15.2 %all_to_all.44.got = bf16[16,16,128]{2,1,0:T(8,128)(2,1)S(1)} all-to-all(bf16[16,16,128]{2,1,0:T(8,128)(2,1)S(1)} %get-tuple-element.14), channel_id=1, replica_groups=mesh['zl'=4,'x'=4,'y'=4,'zh'=4,'core'=2] {'zl','zh'}, dimensions={0} | all-to-all | bytes 131072 | tf_op jit(solution)/shard_map/all_to_all | solution.py:328
  95.2 0.5 shard_map.145
  95.8 14.1 %all_to_all.45 = bf16[32,24,128]{2,1,0:T(8,128)(2,1)S(1)} all-to-all(bf16[32,24,128]{2,1,0:T(8,128)(2,1)S(1)} %bitcast.22), channel_id=1, replica_groups=mesh['zl'=4,'x'=4,'y'=4,'zh'=4,'core'=2] {'x','y','core'}, dimensions={0} | all-to-all | bytes 393216 | tf_op jit(solution)/shard_map/all_to_all | solution.py:328
  109.9 1.5 %shard_map.146 = bf16[4,8,32,128]{3,2,1,0:T(8,128)(2,1)S(1)} custom-call(bf16[4,8,32,128]{3,2,1,0:T(8,128)(2,1)S(1)} %bitcast.16, bf16[4,8,24,128]{3,2,1,0:T(8,128)(2,1)S(1)} %bitcast.20, f32[256,256]{1,0:T(8,128)S(1)} %copy-done.1, bf16[512,256]{1,0:T(8,128)(2,1)S(1)} %copy-done), custom_call_target="tpu_custom_call" | custom-call | tf_op jit(solution)/shard_map/pallas_call | solution.py:316
  111.4 0.0 copy-start.4
  111.4 12.7 %all_to_all.46 = bf16[32,32,128]{2,1,0:T(8,128)(2,1)S(1)} all-to-all(bf16[32,32,128]{2,1,0:T(8,128)(2,1)S(1)} %bitcast.17), channel_id=1, replica_groups=mesh['zl'=4,'x'=4,'y'=4,'zh'=4,'core'=2] {'x','y','core'}, dimensions={0} | all-to-all | bytes 524288 | tf_op jit(solution)/shard_map/all_to_all | solution.py:328
  124.1 0.5 shard_map.147
  124.6 0.0 copy-start.2
  124.7 0.0 copy-start.3
  124.7 15.2 %all_to_all.47.got = bf16[16,32,128]{2,1,0:T(8,128)(2,1)S(1)} all-to-all(bf16[16,32,128]{2,1,0:T(8,128)(2,1)S(1)} %shard_map.147), channel_id=1, replica_groups=mesh['zl'=4,'x'=4,'y'=4,'zh'=4,'core'=2] {'zl','zh'}, dimensions={0} | all-to-all | bytes 262144 | tf_op jit(solution)/shard_map/all_to_all | solution.py:328
  139.8 0.0 copy-done.4
  139.8 0.0 copy-done.2
  139.8 0.0 copy-done.3
  139.9 1.1 shard_map.148
Async XLA Ops:
  32.0 19.2 %copy-start = (bf16[512,256]{1,0:T(8,128)(2,1)S(1)}, bf16[512,256]{1,0:T(8,128)(2,1)}, u32[]{:S(2)}) copy-start(bf16[512,256]{1,0:T(8,128)(2,1)} %constant.27.clone.big) | copy-start | bytes 786436
  32.0 19.2 %copy-start.1 = (f32[256,256]{1,0:T(8,128)S(1)}, f32[256,256]{1,0:T(8,128)}, u32[]{:S(2)}) copy-start(f32[256,256]{1,0:T(8,128)} %get-tuple-element.12.made) | copy-start | bytes 786436
  63.9 15.7 %copy-start.6 = (bf16[128,256]{1,0:T(8,128)(2,1)S(1)}, bf16[128,256]{1,0:T(8,128)(2,1)}, u32[]{:S(2)}) copy-start(bf16[128,256]{1,0:T(8,128)(2,1)} %w_gate.3) | copy-start | bytes 196612
  63.9 15.7 %copy-start.8 = (bf16[16,8,128]{2,1,0:T(8,128)(2,1)S(1)}, bf16[16,8,128]{2,1,0:T(8,128)(2,1)}, u32[]{:S(2)}) copy-start(bf16[16,8,128]{2,1,0:T(8,128)(2,1)} %param.14) | copy-start | bytes 98308
  63.9 15.7 %copy-start.9 = (bf16[2,128,128]{2,1,0:T(8,128)(2,1)S(1)}, bf16[2,128,128]{2,1,0:T(8,128)(2,1)}, u32[]{:S(2)}) copy-start(bf16[2,128,128]{2,1,0:T(8,128)(2,1)} %w_final.1) | copy-start | bytes 196612
  64.3 15.3 %copy-start.5 = (f32[136,128]{1,0:T(8,128)S(1)}, f32[136,128]{1,0:T(8,128)}, u32[]{:S(2)}) copy-start(f32[136,128]{1,0:T(8,128)} %get-tuple-element.13.rest) | copy-start | bytes 208900
  64.3 15.3 %copy-start.7 = (bf16[16,8,128]{2,1,0:T(8,128)(2,1)S(1)}, bf16[16,8,128]{2,1,0:T(8,128)(2,1)}, u32[]{:S(2)}) copy-start(bf16[16,8,128]{2,1,0:T(8,128)(2,1)} %param.13) | copy-start | bytes 98308
  111.4 28.4 %copy-start.4 = (f32[2,512,128]{2,1,0:T(8,128)S(1)}, f32[2,512,128]{2,1,0:T(8,128)}, u32[]{:S(2)}) copy-start(f32[2,512,128]{2,1,0:T(8,128)} %get-tuple-element.16.proj) | copy-start | bytes 1572868
  124.6 15.2 %copy-start.2 = (bf16[128,512]{1,0:T(8,128)(2,1)S(1)}, bf16[128,512]{1,0:T(8,128)(2,1)}, u32[]{:S(2)}) copy-start(bf16[128,512]{1,0:T(8,128)(2,1)} %w_out.3) | copy-start | bytes 393220
  124.7 15.2 %copy-start.3 = (bf16[128,512]{1,0:T(8,128)(2,1)S(1)}, bf16[128,512]{1,0:T(8,128)(2,1)}, u32[]{:S(2)}) copy-start(bf16[128,512]{1,0:T(8,128)(2,1)} %w_in.3) | copy-start | bytes 393220

commit v10 on v9

--- a/solution.py
+++ b/solution.py
@@ -206,10 +206,13 @@
     return (values.reshape(32, 8, 256) * mask).reshape(256, 256)
 
 
-def forward_kernel(got, made, big, send):
+def forward_kernel(got, made, big, send, kept):
     left_out, left_in, right_in = quarters(got)
     right_out = whole(got, big)
-    mask_out, mask_in = made[0:128], made[128:256]
+    for n, values in enumerate((left_out, left_in, right_in)):
+        kept[64 * n : 64 * n + 64] = values
+    kept[192:448] = right_out.astype(BF)
+    mask_out, mask_in = made[0:128].astype(F32), made[128:256].astype(F32)
     outs, ins = [], None
     for t in range(4):
         part = slice(16 * t, 16 * t + 16)
@@ -220,12 +223,12 @@
     send_quarters(send, [join(outs)])
 
 
-def backward_kernel(got, grads, made, big, send):
-    left_out, left_in, right_in = quarters(got)
+def backward_kernel(kept, grads, made, big, send):
+    left_out, left_in, right_in = (kept[64 * n : 64 * n + 64] for n in range(3))
     grad_out = quarters(grads)[0]
-    right_out = whole(got, big)
+    right_out = kept[192:448].astype(F32)
     grad_in = whole(grads, big)
-    mask_out, mask_in = made[0:128], made[128:256]
+    mask_out, mask_in = made[0:128].astype(F32), made[128:256].astype(F32)
     grad_left_out, grad_left_in, grad_right_in, grad_right_out = [], [], [], None
     for t in range(4):
         part = slice(16 * t, 16 * t + 16)
@@ -258,8 +261,8 @@
             send[:, row : row + 8] = groups(gated)
     rest[130:132] = update[...]
     mask_out, mask_in = masks(contact, flat, spot[0], blocks, small, wide)
-    made[0:128] = mask_out
-    made[128:256] = mask_in
+    made[0:128] = mask_out.astype(BF)
+    made[128:256] = mask_in.astype(BF)
 
 
 def middle_kernel(pair, cotangent, got, rest, w_gate, w_final, final, send, grad_gate):
@@ -368,7 +371,7 @@
         [
             ((16, 32, 128), BF),
             ((136, 128), F32),
-            ((256, 256), F32),
+            ((256, 256), BF),
             ((2, 512, 128), F32),
         ],
         my_mate().reshape(1),
@@ -386,7 +389,9 @@
         limit=None,
     )
     sides = to_channels(send, 1, (0, 2, 3))
-    triangles = call(forward_kernel, ((4, 8, 24, 128), BF), sides, made, big)
+    triangles, kept = call(
+        forward_kernel, [((4, 8, 24, 128), BF), ((448, 256), BF)], sides, made, big
+    )
     final, send, grad_gate = call(
         middle_kernel,
         [((128, 128), BF), ((16, 16, 128), BF), ((256, 128), BF)],
@@ -400,7 +405,7 @@
     grads = call(
         backward_kernel,
         ((4, 8, 32, 128), BF),
-        sides,
+        kept,
         to_channels(send, 1, (0,)),
         made,
         big,

time: 143 us -> 142 us (level)
  no operation moved by 1% of the time
where the time goes in v10:
time: 142 us; the launch traced here: 140 us
  blocking collectives  131 us (92%)
  Pallas kernels  8.14 us (6%)
    all_to_all x8, blocking collectives, exchange(): return lax.all_to_all(values, axis, 0, 0, tiled=True)  131 us
    pallas_call x9, Pallas kernels, call(): pl.pallas_call(kernel, out_shape=shapes, in_specs=specs, out_specs=outs,...  8.14 us

profile of v10, /device:TPU:1, one launch (start us, length us, event | category | flops | bytes accessed | tf_op | source)
XLA Modules:
  0.0 140.5 jit_solution(8352877426861271132)
XLA Ops:
  0.6 2.6 %shard_map.140 = (bf16[16,32,128]{2,1,0:T(8,128)(2,1)}, f32[136,128]{1,0:T(8,128)}, bf16[256,256]{1,0:T(8,128)(2,1)}, f32[2,512,128]{2,1,0:T(8,128)}) custom-call(s32[1]{0:T(128)} %bitcast.1.spot, bf16[128,128]{1,0:T(8,128)(2,1)} %bitcast.23, f32[1,128]{1,0:T(1,128)} %bitcast.28, bf16[128,512]{1,0:T(8,128)(2,1)} %w_out.3, bf16[128,512]{1,0:T(8,128)(2,1)} %w_in.3, ...), custom_call_target="tpu_custom_call" | custom-call | tf_op jit(solution)/shard_map/pallas_call | solution.py:319
  3.3 28.1 %all_to_all.40.got = bf16[16,32,128]{2,1,0:T(8,128)(2,1)S(1)} all-to-all(bf16[16,32,128]{2,1,0:T(8,128)(2,1)} %get-tuple-element.13), channel_id=1, replica_groups=mesh['zl'=4,'x'=4,'y'=4,'zh'=4,'core'=2] {'zl','zh'}, dimensions={0} | all-to-all | bytes 262144 | tf_op jit(solution)/shard_map/all_to_all | solution.py:331
  31.4 0.6 shard_map.141
  32.0 0.0 copy-start
  32.0 0.0 copy-start.3
  32.0 19.2 %all_to_all.41 = bf16[32,32,128]{2,1,0:T(8,128)(2,1)S(1)} all-to-all(bf16[32,32,128]{2,1,0:T(8,128)(2,1)S(1)} %bitcast.16), channel_id=1, replica_groups=mesh['zl'=4,'x'=4,'y'=4,'zh'=4,'core'=2] {'x','y','core'}, dimensions={0} | all-to-all | bytes 524288 | tf_op jit(solution)/shard_map/all_to_all | solution.py:331
  51.2 0.0 copy-done
  51.2 0.0 copy-done.3
  51.2 0.8 shard_map.142
  52.0 11.8 %all_to_all.42 = bf16[32,24,128]{2,1,0:T(8,128)(2,1)S(1)} all-to-all(bf16[32,24,128]{2,1,0:T(8,128)(2,1)S(1)} %bitcast.22), channel_id=1, replica_groups=mesh['zl'=4,'x'=4,'y'=4,'zh'=4,'core'=2] {'x','y','core'}, dimensions={0} | all-to-all | bytes 393216 | tf_op jit(solution)/shard_map/all_to_all | solution.py:331
  63.8 0.0 copy-start.6
  63.8 0.0 copy-start.8
  63.8 0.0 copy-start.9
  63.8 0.4 shard_map.143
  64.3 0.0 copy-start.5
  64.3 0.0 copy-start.7
  64.3 15.3 %all_to_all.43.got = bf16[16,16,128]{2,1,0:T(8,128)(2,1)S(1)} all-to-all(bf16[16,16,128]{2,1,0:T(8,128)(2,1)S(1)} %shard_map.143), channel_id=1, replica_groups=mesh['zl'=4,'x'=4,'y'=4,'zh'=4,'core'=2] {'zl','zh'}, dimensions={0} | all-to-all | bytes 131072 | tf_op jit(solution)/shard_map/all_to_all | solution.py:331
  79.6 0.0 copy-done.6
  79.6 0.0 copy-done.8
  79.6 0.0 copy-done.9
  79.6 0.0 copy-done.5
  79.6 0.0 copy-done.7
  79.6 0.4 shard_map.144
  80.0 15.2 %all_to_all.44.got = bf16[16,16,128]{2,1,0:T(8,128)(2,1)S(1)} all-to-all(bf16[16,16,128]{2,1,0:T(8,128)(2,1)S(1)} %get-tuple-element.18), channel_id=1, replica_groups=mesh['zl'=4,'x'=4,'y'=4,'zh'=4,'core'=2] {'zl','zh'}, dimensions={0} | all-to-all | bytes 131072 | tf_op jit(solution)/shard_map/all_to_all | solution.py:331
  95.2 0.5 shard_map.145
  95.8 14.1 %all_to_all.45 = bf16[32,24,128]{2,1,0:T(8,128)(2,1)S(1)} all-to-all(bf16[32,24,128]{2,1,0:T(8,128)(2,1)S(1)} %bitcast.20), channel_id=1, replica_groups=mesh['zl'=4,'x'=4,'y'=4,'zh'=4,'core'=2] {'x','y','core'}, dimensions={0} | all-to-all | bytes 393216 | tf_op jit(solution)/shard_map/all_to_all | solution.py:331
  109.9 1.1 shard_map.146
  111.0 0.0 copy-start.4
  111.0 12.7 %all_to_all.46 = bf16[32,32,128]{2,1,0:T(8,128)(2,1)S(1)} all-to-all(bf16[32,32,128]{2,1,0:T(8,128)(2,1)S(1)} %bitcast.18), channel_id=1, replica_groups=mesh['zl'=4,'x'=4,'y'=4,'zh'=4,'core'=2] {'x','y','core'}, dimensions={0} | all-to-all | bytes 524288 | tf_op jit(solution)/shard_map/all_to_all | solution.py:331
  123.6 0.5 shard_map.147
  124.2 0.0 copy-start.1
  124.2 0.0 copy-start.2
  124.2 15.2 %all_to_all.47.got = bf16[16,32,128]{2,1,0:T(8,128)(2,1)S(1)} all-to-all(bf16[16,32,128]{2,1,0:T(8,128)(2,1)S(1)} %shard_map.147), channel_id=1, replica_groups=mesh['zl'=4,'x'=4,'y'=4,'zh'=4,'core'=2] {'zl','zh'}, dimensions={0} | all-to-all | bytes 262144 | tf_op jit(solution)/shard_map/all_to_all | solution.py:331
  139.4 0.0 copy-done.4
  139.4 0.0 copy-done.1
  139.4 0.0 copy-done.2
  139.4 1.1 shard_map.148
Async XLA Ops:
  32.0 19.2 %copy-start = (bf16[512,256]{1,0:T(8,128)(2,1)S(1)}, bf16[512,256]{1,0:T(8,128)(2,1)}, u32[]{:S(2)}) copy-start(bf16[512,256]{1,0:T(8,128)(2,1)} %constant.27.clone.big) | copy-start | bytes 786436
  32.0 19.2 %copy-start.3 = (bf16[256,256]{1,0:T(8,128)(2,1)S(1)}, bf16[256,256]{1,0:T(8,128)(2,1)}, u32[]{:S(2)}) copy-start(bf16[256,256]{1,0:T(8,128)(2,1)} %get-tuple-element.14.made) | copy-start | bytes 393220
  63.8 15.7 %copy-start.6 = (bf16[128,256]{1,0:T(8,128)(2,1)S(1)}, bf16[128,256]{1,0:T(8,128)(2,1)}, u32[]{:S(2)}) copy-start(bf16[128,256]{1,0:T(8,128)(2,1)} %w_gate.3) | copy-start | bytes 196612
  63.8 15.7 %copy-start.8 = (bf16[16,8,128]{2,1,0:T(8,128)(2,1)S(1)}, bf16[16,8,128]{2,1,0:T(8,128)(2,1)}, u32[]{:S(2)}) copy-start(bf16[16,8,128]{2,1,0:T(8,128)(2,1)} %param.14) | copy-start | bytes 98308
  63.8 15.7 %copy-start.9 = (bf16[2,128,128]{2,1,0:T(8,128)(2,1)S(1)}, bf16[2,128,128]{2,1,0:T(8,128)(2,1)}, u32[]{:S(2)}) copy-start(bf16[2,128,128]{2,1,0:T(8,128)(2,1)} %w_final.1) | copy-start | bytes 196612
  64.3 15.3 %copy-start.5 = (f32[136,128]{1,0:T(8,128)S(1)}, f32[136,128]{1,0:T(8,128)}, u32[]{:S(2)}) copy-start(f32[136,128]{1,0:T(8,128)} %get-tuple-element.17.rest) | copy-start | bytes 208900
  64.3 15.3 %copy-start.7 = (bf16[16,8,128]{2,1,0:T(8,128)(2,1)S(1)}, bf16[16,8,128]{2,1,0:T(8,128)(2,1)}, u32[]{:S(2)}) copy-start(bf16[16,8,128]{2,1,0:T(8,128)(2,1)} %param.13) | copy-start | bytes 98308
  111.0 28.4 %copy-start.4 = (f32[2,512,128]{2,1,0:T(8,128)S(1)}, f32[2,512,128]{2,1,0:T(8,128)}, u32[]{:S(2)}) copy-start(f32[2,512,128]{2,1,0:T(8,128)} %get-tuple-element.20.proj) | copy-start | bytes 1572868
  124.2 15.2 %copy-start.1 = (bf16[128,512]{1,0:T(8,128)(2,1)S(1)}, bf16[128,512]{1,0:T(8,128)(2,1)}, u32[]{:S(2)}) copy-start(bf16[128,512]{1,0:T(8,128)(2,1)} %w_out.3) | copy-start | bytes 393220
  124.2 15.2 %copy-start.2 = (bf16[128,512]{1,0:T(8,128)(2,1)S(1)}, bf16[128,512]{1,0:T(8,128)(2,1)}, u32[]{:S(2)}) copy-start(bf16[128,512]{1,0:T(8,128)(2,1)} %w_in.3) | copy-start | bytes 393220
